TPU v7x, 512 devices: a whole 4x4x16 slice. The times are simulated.
512 devices in a mesh: dp: 16 (over y_hi, x, core), tensor: 32 (over z, y_lo).
Axes of the slice: x: 4, y: 4 (y_hi: 2, y_lo: 2; y = y_hi * 2 + y_lo), z: 16, core: 2. Of those that a mesh axis runs over, the one named last changes fastest.
Arguments:
- x_rotated: bfloat16 [1024, 10240], P('tensor', 'dp'), may hold values from -6 to 6
- block_scales: float32 [1024, 80], P('tensor', 'dp'), may hold values from 0.3 to 3
- grad_act: bfloat16 [1024, 36864], P('dp', 'tensor'), may hold values from -6 to 6
- w_in: bfloat16 [10240, 36864], P('dp', 'tensor'), may hold values from -0.0625 to 0.0625
Outputs:
- grad_input: bfloat16 [1024, 10240], P('tensor', 'dp')
- grad_weight: bfloat16 [10240, 36864], P('dp', 'tensor')
All inputs are finite; a program needn't handle non-finite values.
Results may differ from a plain program's by a relative error of at most 0.034.
Values may be sent and summed in bfloat16 or wider, within the bound.
No kernel may reach another device: no remote copies, remote signals or barrier semaphores. Data moves between devices by JAX's collectives and lax.ppermute only.
A program may use at most 64 MiB of HBM per device.

v0:
```python
import math

import jax
import jax.numpy as jnp
from jax import lax
from jax.sharding import PartitionSpec as P


def hadamard_table():
    index = lax.iota(jnp.int32, 128)
    common = jnp.bitwise_and(index[:, None], index[None, :])
    parity = jnp.zeros((128, 128), jnp.int32)
    for shift in range(7):
        parity = parity + jnp.bitwise_and(jnp.right_shift(common, shift), 1)
    signs = 1.0 - 2.0 * (parity % 2).astype(jnp.float32)
    return signs / math.sqrt(128.0)


def decode(coded, scales):
    count = coded.shape[0]
    blocks = coded.astype(jnp.float32).reshape(count, scales.shape[1], 128) * scales[:, :, None]
    turned = jnp.einsum("rbk,kj->rbj", blocks, hadamard_table(), precision=lax.Precision.HIGHEST)
    return turned.reshape(count, coded.shape[1]).astype(jnp.bfloat16)


def gelu_slope(value):
    cdf = 0.5 * (1.0 + jax.scipy.special.erf(value / math.sqrt(2.0)))
    pdf = jnp.exp(-0.5 * value * value) / math.sqrt(2.0 * math.pi)
    return cdf + value * pdf


def slope_grad(pre, grads):
    return (grads.astype(jnp.float32) * gelu_slope(pre)).astype(jnp.bfloat16)


def rounded_term(value):
    return lax.optimization_barrier(value.astype(jnp.bfloat16)).astype(jnp.float32)


def shards(x_rotated, block_scales, grad_act, w_in):
    inputs = lax.all_gather(decode(x_rotated, block_scales), "tensor", axis=0, tiled=True)
    rows_in = inputs
    pre = lax.psum_scatter(
        rounded_term(jnp.dot(rows_in, w_in, preferred_element_type=jnp.float32)).astype(
            jnp.bfloat16
        ),
        "dp",
        scatter_dimension=0,
        tiled=True,
    ).astype(jnp.float32)
    grad_local = slope_grad(pre, grad_act)
    piece = lax.all_gather(grad_local, "dp", axis=0, tiled=True)
    rows_in = inputs
    total = lax.dot_general(
        rows_in, piece, (((0,), (0,)), ((), ())), preferred_element_type=jnp.float32
    )
    total, grad_pre = (total, piece)
    part = lax.dot_general(
        grad_pre, w_in, (((1,), (1,)), ((), ())), preferred_element_type=jnp.float32
    )
    grad_input = lax.psum_scatter(
        rounded_term(part).astype(jnp.bfloat16), "tensor", scatter_dimension=0, tiled=True
    )
    return (grad_input, total.astype(jnp.bfloat16))


def solution(mesh):
    in_specs = (P("tensor", "dp"), P("tensor", "dp"), P("dp", "tensor"), P("dp", "tensor"))
    out_specs = (P("tensor", "dp"), P("dp", "tensor"))
    return jax.shard_map(shards, mesh=mesh, in_specs=in_specs, out_specs=out_specs, check_vma=False)
```

profile of v0, /device:TPU:6, one launch (start us, length us, event | category | flops | bytes accessed | tf_op | source)
XLA Modules:
  0.0 461.8 jit_solution(15673798237053105231)
XLA Ops:
  7.2 0.0 copy-start
  7.2 0.0 all-gather.3.cloned.1.call-start
  7.2 0.9 copy.7
  8.1 0.8 reshape.16
  8.9 0.1 broadcast_multiply_fusion
  9.0 0.3 fusion
  9.3 0.6 copy.14
  10.0 0.0 all-gather.3.cloned.1.call-update
  10.0 0.0 reduce-scatter.3.cloned.1.call-start
  10.0 137.3 %all-gather.3.cloned.1.call-done = bf16[1024,640]{1,0:T(8,128)(2,1)} async-done(((bf16[32,640]{1,0:T(8,128)(2,1)}), bf16[1024,640]{1,0:T(8,128)(2,1)}) %all-gather.3.cloned.1.call-update) | async-done | bytes 1310736 | tf_op jit(solution)/shard_map/all_gather | solution.py:41
  147.3 0.0 copy-done
  147.3 4.9 %convolution_convert_fusion = bf16[1024,1152]{1,0:T(8,128)(2,1)} fusion(bf16[1024,640]{1,0:T(8,128)(2,1)} %all-gather.3.cloned.1.call-done, bf16[640,1152]{1,0:T(8,128)(2,1)S(1)} %copy-done), kind=kOutput, calls=%fused_computation | convolution fusion | flops 1511129088 | bytes 5144576 | tf_op jit(solution)/shard_map/dot_general | solution.py:44
  152.2 0.0 reduce-scatter.3.cloned.1.call-update
  152.2 0.0 all-gather.5.cloned.1.call-start
  152.3 93.8 %reduce-scatter.3.cloned.1.call-done = bf16[64,1152]{1,0:T(8,128)(2,1)} async-done(((bf16[1024,1152]{1,0:T(8,128)(2,1)}), bf16[64,1152]{1,0:T(8,128)(2,1)}) %reduce-scatter.3.cloned.1.call-update) | async-done | bytes 147472 | tf_op jit(solution)/shard_map/reduce_scatter | solution.py:43
  246.1 1.7 fusion.8
  247.8 0.0 all-gather.5.cloned.1.call-update
  247.8 0.0 reduce-scatter.5.cloned.1.call-start
  247.9 66.2 %all-gather.5.cloned.1.call-done = bf16[1024,1152]{1,0:T(8,128)(2,1)} async-done(((bf16[64,1152]{1,0:T(8,128)(2,1)}), bf16[1024,1152]{1,0:T(8,128)(2,1)}) %all-gather.5.cloned.1.call-update) | async-done | bytes 2359312 | tf_op jit(solution)/shard_map/all_gather | solution.py:52
  314.0 4.9 %convolution_convert_fusion.2 = bf16[1024,640]{1,0:T(8,128)(2,1)} fusion(bf16[1024,1152]{1,0:T(8,128)(2,1)} %all-gather.5.cloned.1.call-done, bf16[640,1152]{1,0:T(8,128)(2,1)S(1)} %copy-done), kind=kOutput, calls=%fused_computation.2 | convolution fusion | flops 1510604800 | bytes 5144576 | tf_op jit(solution)/shard_map/dot_general | solution.py:58
  318.9 0.0 reduce-scatter.5.cloned.1.call-update
  319.0 0.0 copy-done.2
  319.0 4.7 %convolution_convert_fusion.1 = bf16[640,1152]{1,0:T(8,128)(2,1)} fusion(bf16[1024,640]{1,0:T(8,128)(2,1)S(1)} %copy-done.2, bf16[1024,1152]{1,0:T(8,128)(2,1)} %all-gather.5.cloned.1.call-done), kind=kOutput, calls=%fused_computation.1 | convolution fusion | flops 1510686720 | bytes 5144576 | tf_op jit(solution)/shard_map/dot_general | solution.py:54
  323.7 131.6 %reduce-scatter.5.cloned.1.call-done = bf16[32,640]{1,0:T(8,128)(2,1)} async-done(((bf16[1024,640]{1,0:T(8,128)(2,1)}), bf16[32,640]{1,0:T(8,128)(2,1)}) %reduce-scatter.5.cloned.1.call-update) | async-done | bytes 40976 | tf_op jit(solution)/shard_map/reduce_scatter | solution.py:61
  (3 shorter events, 0.0 us)
Async XLA Ops:
  7.2 140.2 %copy-start = (bf16[640,1152]{1,0:T(8,128)(2,1)S(1)}, bf16[640,1152]{1,0:T(8,128)(2,1)}, u32[]{:S(2)}) copy-start(bf16[640,1152]{1,0:T(8,128)(2,1)} %param.7) | copy-start | bytes 4423684
  7.2 140.2 %all-gather.3.cloned.1.call-start = ((), (), s32[]{:S(2)}) async-start(), calls=%async_computation.2 | async-start | bytes 1351680 | tf_op jit(solution)/shard_map/all_gather | solution.py:41
  10.0 236.1 %reduce-scatter.3.cloned.1.call-start = ((), (), s32[]{:S(2)}) async-start(), calls=%async_computation.3 | async-start | bytes 2506752 | tf_op jit(solution)/shard_map/reduce_scatter | solution.py:43
  152.2 93.9 %copy-start.1 = (bf16[64,1152]{1,0:T(8,128)(2,1)S(1)}, bf16[64,1152]{1,0:T(8,128)(2,1)}, u32[]{:S(2)}) copy-start(bf16[64,1152]{1,0:T(8,128)(2,1)} %param.6) | copy-start | bytes 442372
  152.2 161.8 %all-gather.5.cloned.1.call-start = ((), (), s32[]{:S(2)}) async-start(), calls=%async_computation.4 | async-start | bytes 2506752 | tf_op jit(solution)/shard_map/all_gather | solution.py:52
  247.8 71.2 %copy-start.2 = (bf16[1024,640]{1,0:T(8,128)(2,1)S(1)}, bf16[1024,640]{1,0:T(8,128)(2,1)}, u32[]{:S(2)}) copy-start(bf16[1024,640]{1,0:T(8,128)(2,1)} %all-gather.3.cloned.1.call-done) | copy-start | bytes 3932164
  247.8 207.4 %reduce-scatter.5.cloned.1.call-start = ((), (), s32[]{:S(2)}) async-start(), calls=%async_computation.5 | async-start | bytes 1351680 | tf_op jit(solution)/shard_map/reduce_scatter | solution.py:61
Sparse Core Ops, SparseCore 0:
  10.7 136.6 all-gather.2
  152.3 93.6 reduce-scatter.2
  249.9 64.0 all-gather.4
  319.1 136.1 reduce-scatter.4
where the time goes:
time: 462 us
  waiting for transfers between devices  429 us (93%)
  matrix products  14.7 us (3%)
  between operations  13.8 us (3%)
    all_gather x1, waiting for transfers between devices, shards(): lax.all_gather(decode(x_rotated, block_scales), 'tensor', axis=0, tiled=T...  137 us
    reduce_scatter x1, waiting for transfers between devices, shards(): lax.psum_scatter(rounded_term(part).astype(jnp.bfloat16), 'tensor', scatt...  132 us
    reduce_scatter x1, waiting for transfers between devices, shards(): lax.psum_scatter(rounded_term(jnp.dot(rows_in, w_in, preferred_element_ty...  93.8 us
    all_gather x1, waiting for transfers between devices, shards(): piece = lax.all_gather(grad_local, 'dp', axis=0, tiled=True)  66.2 us
  transfers between devices with their start and end apart: 4, of which 4 were waited for; matrix products, arithmetic and copies ran while one was open for 1% of the time, Pallas kernels for 0%

commit v1 on v0

v1 whole, which is shorter than its diff:
```python
import math

import jax
import jax.numpy as jnp
from jax import lax
from jax.sharding import Mesh
from jax.sharding import PartitionSpec as P

AXES = ("yh", "x", "c", "zq", "zc", "yl")
SIZES = (2, 4, 2, 8, 2, 2)
DP = ("yh", "x", "c")
TENSOR = ("zq", "zc", "yl")
SWAP = [(0, 1), (1, 0)]


def hadamard_table():
    index = lax.iota(jnp.int32, 128)
    common = jnp.bitwise_and(index[:, None], index[None, :])
    parity = jnp.zeros((128, 128), jnp.int32)
    for shift in range(7):
        parity = parity + jnp.bitwise_and(jnp.right_shift(common, shift), 1)
    signs = 1.0 - 2.0 * (parity % 2).astype(jnp.float32)
    return signs / math.sqrt(128.0)


def decode(coded, scales):
    count = coded.shape[0]
    blocks = coded.astype(jnp.float32).reshape(count, scales.shape[1], 128) * scales[:, :, None]
    turned = jnp.einsum("rbk,kj->rbj", blocks, hadamard_table(), precision=lax.Precision.HIGHEST)
    return turned.reshape(count, coded.shape[1]).astype(jnp.bfloat16)


def gelu_slope(value):
    cdf = 0.5 * (1.0 + jax.scipy.special.erf(value / math.sqrt(2.0)))
    pdf = jnp.exp(-0.5 * value * value) / math.sqrt(2.0 * math.pi)
    return cdf + value * pdf


def slope_grad(pre, grads):
    return (grads.astype(jnp.float32) * gelu_slope(pre)).astype(jnp.bfloat16)


def dot(a, b, dims):
    return lax.dot_general(a, b, (dims, ((), ())), preferred_element_type=jnp.float32)


def half(array, which):
    return lax.dynamic_index_in_dim(array, which, 0, keepdims=False)


def chunk_gradient(rows, grads, w_in, core):
    far = dot(half(rows, 1 - core), w_in, ((1,), (0,))).astype(jnp.bfloat16)
    far = lax.ppermute(far, "c", SWAP)
    near = dot(half(rows, core), w_in, ((1,), (0,)))
    near = (near + far.astype(jnp.float32)).astype(jnp.bfloat16)
    parts = lax.all_to_all(near, ("yh", "x"), 0, 0, tiled=True)
    pre = jnp.sum(parts.reshape(8, 32, -1).astype(jnp.float32), axis=0)
    grad = slope_grad(pre, grads)
    copies = jnp.broadcast_to(grad[None], (8,) + grad.shape).reshape(256, -1)
    mine = lax.all_to_all(copies, ("yh", "x"), 0, 0, tiled=True)
    other = lax.ppermute(mine, "c", SWAP)
    return mine, other


def in_core_order(mine, other, core):
    return jnp.where(core == 0, jnp.stack([mine, other]), jnp.stack([other, mine]))


def shards(x_rotated, block_scales, grad_act, w_in):
    core = lax.axis_index("c")
    side = lax.axis_index("yl")
    own = decode(x_rotated, block_scales)
    partner = lax.ppermute(own, "yl", SWAP)
    first = lax.all_gather(partner, ("zc", "zq"), axis=0, tiled=True)
    second = lax.ppermute(first, "yl", SWAP)
    grads = grad_act.reshape(2, 32, -1)
    sums, weights = [], []
    for rows, which in ((first, 1 - side), (second, side)):
        rows = rows.reshape(2, 256, -1)
        mine, other = chunk_gradient(rows, half(grads, which), w_in, core)
        grad_pre = in_core_order(mine, other, core).reshape(512, -1)
        weights.append(dot(rows.reshape(512, -1), grad_pre, ((0,), (0,))))
        part = dot(grad_pre, w_in, ((1,), (1,)))
        if not sums:
            sums.append(lax.ppermute(part.astype(jnp.bfloat16), "yl", SWAP))
        else:
            sums.append(part)
    part = (sums[1] + sums[0].astype(jnp.float32)).astype(jnp.bfloat16)
    blocks = lax.all_to_all(part, ("zc", "zq"), 0, 0, tiled=True)
    grad_input = jnp.sum(blocks.reshape(16, 32, -1).astype(jnp.float32), axis=0)
    grad_weight = (weights[0] + weights[1]).astype(jnp.bfloat16)
    return grad_input.astype(jnp.bfloat16), grad_weight


def solution(mesh):
    fine = Mesh(mesh.devices.reshape(SIZES), AXES)
    in_specs = (P(TENSOR, DP), P(TENSOR, DP), P(DP, TENSOR), P(DP, TENSOR))
    out_specs = (P(TENSOR, DP), P(DP, TENSOR))
    return jax.shard_map(shards, mesh=fine, in_specs=in_specs, out_specs=out_specs, check_vma=False)
```

time: 462 us -> 217 us (0.47)
  the two profiles are of different devices: /device:TPU:6 before, /device:TPU:64 now
where the time goes in v1:
time: 217 us; the launch traced here: 216 us
  waiting for transfers between devices  89.8 us (41%)
  blocking collectives  56.5 us (26%)
  starting transfers between devices  43.5 us (20%)
  matrix products  15.2 us (7%)
  other arithmetic  6.57 us (3%)
  local copies, waits for them, and re-layouts  3.45 us (2%)
    all_gather x1, blocking collectives, shards(): first = lax.all_gather(partner, ('zc', 'zq'), axis=0, tiled=True)  41.6 us
    all_to_all x1, waiting for transfers between devices, shards(): blocks = lax.all_to_all(part, ('zc', 'zq'), 0, 0, tiled=True)  31.3 us
    all_to_all x2, waiting for transfers between devices, chunk_gradient(): parts = lax.all_to_all(near, ('yh', 'x'), 0, 0, tiled=True)  22.7 us
    dot_general x8, matrix products, dot(): lax.dot_general(a, b, (dims, ((), ())), preferred_element_type=jnp.float32)  14.9 us
    all_to_all x1, blocking collectives, chunk_gradient(): mine = lax.all_to_all(copies, ('yh', 'x'), 0, 0, tiled=True)  14.9 us
    ppermute x1, waiting for transfers between devices, shards(): sums.append(lax.ppermute(part.astype(jnp.bfloat16), 'yl', SWAP))  14.9 us
    all_to_all x1, waiting for transfers between devices, chunk_gradient(): mine = lax.all_to_all(copies, ('yh', 'x'), 0, 0, tiled=True)  13.2 us
    all_to_all x2, starting transfers between devices, chunk_gradient(): parts = lax.all_to_all(near, ('yh', 'x'), 0, 0, tiled=True)  10.6 us
  transfers between devices with their start and end apart: 11, of which 7 were waited for; matrix products, arithmetic and copies ran while one was open for 8% of the time, Pallas kernels for 0%

profile of v1, /device:TPU:64, one launch (start us, length us, event | category | flops | bytes accessed | tf_op | source)
XLA Modules:
  0.0 215.9 jit_solution(5318507234500343113)
XLA Ops:
  2.8 3.5 %collective-permute-start = (bf16[32,640]{1,0:T(8,128)(2,1)S(1)}, bf16[32,640]{1,0:T(8,128)(2,1)S(1)}, u32[]{:S(2)}, u32[]{:S(2)}) collective-permute-start(bf16[32,640]{1,0:T(8,128)(2,1)S(1)} %bitcast.90), channel_id=1, source_target_pairs={{0,1},{1,0},{2,3},{3,2},{4,5},{5,4},{6,7},{7,6},{8,9},{9,8},{10,11... | collective-permute-start | bytes 122888 | tf_op jit(solution)/shard_map/ppermute | solution.py:73
  6.3 2.4 %collective-permute-done = bf16[32,640]{1,0:T(8,128)(2,1)S(1)} collective-permute-done((bf16[32,640]{1,0:T(8,128)(2,1)S(1)}, bf16[32,640]{1,0:T(8,128)(2,1)S(1)}, u32[]{:S(2)}, u32[]{:S(2)}) %collective-permute-start) | collective-permute-done | bytes 40992 | tf_op jit(solution)/shard_map/ppermute | solution.py:73
  8.7 41.6 %all_gather.3 = bf16[512,640]{1,0:T(8,128)(2,1)S(1)} all-gather(bf16[32,640]{1,0:T(8,128)(2,1)S(1)} %collective-permute-done), channel_id=1, replica_groups=mesh['yh'=2,'x'=4,'c'=2,'zq'=8,'zc'=2,'yl'=2] {'zc','zq'}, dimensions={0}, use_global_device_ids=true | all-gather | bytes 696320 | tf_op jit(solution)/shard_map/all_gather | solution.py:74
  50.3 4.7 %collective-permute-start.1 = (bf16[512,640]{1,0:T(8,128)(2,1)S(1)}, bf16[512,640]{1,0:T(8,128)(2,1)S(1)}, u32[]{:S(2)}, u32[]{:S(2)}) collective-permute-start(bf16[512,640]{1,0:T(8,128)(2,1)S(1)} %all_gather.3), channel_id=1, source_target_pairs={{0,1},{1,0},{2,3},{3,2},{4,5},{5,4},{6,7},{7,6},{8,9},{9,8},{10,11... | collective-permute-start | bytes 1966088 | tf_op jit(solution)/shard_map/ppermute | solution.py:75
  58.4 5.1 %collective-permute-done.1 = bf16[512,640]{1,0:T(8,128)(2,1)S(1)} collective-permute-done((bf16[512,640]{1,0:T(8,128)(2,1)S(1)}, bf16[512,640]{1,0:T(8,128)(2,1)S(1)}, u32[]{:S(2)}, u32[]{:S(2)}) %collective-permute-start.1) | collective-permute-done | bytes 655392 | tf_op jit(solution)/shard_map/ppermute | solution.py:75
  65.1 1.9 collective-permute-start.2
  68.5 7.1 %all-to-all-start.2 = ((bf16[8,32,1152]{2,1,0:T(8,128)(2,1)}), bf16[8,32,1152]{2,1,0:T(8,128)(2,1)S(1)}, u32[]{:S(2)}, u32[]{:S(2)}) async-start(bf16[8,32,1152]{2,1,0:T(8,128)(2,1)} %bitcast.15), calls=%async_computation.2 | async-start | bytes 1179648 | tf_op jit(solution)/shard_map/all_to_all | solution.py:56
  75.6 2.6 %fusion.1 = bf16[256,1152]{1,0:T(8,128)(2,1)} fusion(bf16[640,1152]{1,0:T(8,128)(2,1)S(1)} %copy-done, bf16[256,1152]{1,0:T(8,128)(2,1)} %collective-permute-done.2, bf16[2,256,640]{2,1,0:T(8,128)(2,1)S(1)} %bitcast.83, s32[]{:T(128)S(6)} %select_n.46), kind=kOutput, calls=%fused_computation.4 | convolution fusion | flops 378372096 | bytes 2981892 | tf_op jit(solution)/shard_map/dot_general | solution.py:44
  78.1 10.4 %all-to-all-done.2 = bf16[8,32,1152]{2,1,0:T(8,128)(2,1)S(1)} async-done(((bf16[8,32,1152]{2,1,0:T(8,128)(2,1)}), bf16[8,32,1152]{2,1,0:T(8,128)(2,1)S(1)}, u32[]{:S(2)}, u32[]{:S(2)}) %all-to-all-start.2) | async-done | bytes 589856 | tf_op jit(solution)/shard_map/all_to_all | solution.py:56
  88.5 3.5 %all-to-all-start = ((bf16[8,32,1152]{2,1,0:T(8,128)(2,1)}), bf16[8,32,1152]{2,1,0:T(8,128)(2,1)S(1)}, u32[]{:S(2)}, u32[]{:S(2)}) async-start(bf16[8,32,1152]{2,1,0:T(8,128)(2,1)} %bitcast.5), calls=%async_computation | async-start | bytes 1179648 | tf_op jit(solution)/shard_map/all_to_all | solution.py:56
  92.2 12.3 %all-to-all-done = bf16[8,32,1152]{2,1,0:T(8,128)(2,1)S(1)} async-done(((bf16[8,32,1152]{2,1,0:T(8,128)(2,1)}), bf16[8,32,1152]{2,1,0:T(8,128)(2,1)S(1)}, u32[]{:S(2)}, u32[]{:S(2)}) %all-to-all-start) | async-done | bytes 589856 | tf_op jit(solution)/shard_map/all_to_all | solution.py:56
  105.7 14.9 %all_to_all.45 = bf16[8,32,1152]{2,1,0:T(8,128)(2,1)S(1)} all-to-all(bf16[8,32,1152]{2,1,0:T(8,128)(2,1)S(1)} %broadcast_in_dim.22), channel_id=1, replica_groups=mesh['yh'=2,'x'=4,'c'=2,'zq'=8,'zc'=2,'yl'=2] {'yh','x'}, dimensions={0} | all-to-all | bytes 1179648 | tf_op jit(solution)/shard_map/all_to_all | solution.py:60
  120.6 1.9 collective-permute-start.5
  123.4 4.2 %all-to-all-start.1 = ((bf16[8,32,1152]{2,1,0:T(8,128)(2,1)}), bf16[8,32,1152]{2,1,0:T(8,128)(2,1)}, u32[]{:S(2)}, u32[]{:S(2)}) async-start(bf16[8,32,1152]{2,1,0:T(8,128)(2,1)} %broadcast_in_dim.9), calls=%async_computation.1 | async-start | bytes 1179648 | tf_op jit(solution)/shard_map/all_to_all | solution.py:60
  127.6 13.2 %all-to-all-done.1 = bf16[8,32,1152]{2,1,0:T(8,128)(2,1)} async-done(((bf16[8,32,1152]{2,1,0:T(8,128)(2,1)}), bf16[8,32,1152]{2,1,0:T(8,128)(2,1)}, u32[]{:S(2)}, u32[]{:S(2)}) %all-to-all-start.1) | async-done | bytes 589856 | tf_op jit(solution)/shard_map/all_to_all | solution.py:60
  140.9 1.9 collective-permute-start.3
  143.6 2.0 maximum_select_fusion.1
  146.8 2.6 %collective-permute-start.6 = (bf16[512,640]{1,0:T(8,128)(2,1)S(1)}, bf16[512,640]{1,0:T(8,128)(2,1)S(1)}, u32[]{:S(2)}, u32[]{:S(2)}) collective-permute-start(bf16[512,640]{1,0:T(8,128)(2,1)S(1)} %convolution_convert_fusion.2), channel_id=1, source_target_pairs={{0,1},{1,0},{2,3},{3,2},{4,5},{5,4},{6,7},{7,6},{8,9},{9,8},{10,11... | collective-permute-start | bytes 1966088 | tf_op jit(solution)/shard_map/ppermute | solution.py:85
  150.9 14.9 %collective-permute-done.6 = bf16[512,640]{1,0:T(8,128)(2,1)S(1)} collective-permute-done((bf16[512,640]{1,0:T(8,128)(2,1)S(1)}, bf16[512,640]{1,0:T(8,128)(2,1)S(1)}, u32[]{:S(2)}, u32[]{:S(2)}) %collective-permute-start.6) | collective-permute-done | bytes 655392 | tf_op jit(solution)/shard_map/ppermute | solution.py:85
  165.8 2.0 add_convert_fusion
  167.8 10.2 %all-to-all-start.4 = ((bf16[16,32,640]{2,1,0:T(8,128)(2,1)}), bf16[16,32,640]{2,1,0:T(8,128)(2,1)}, u32[]{:S(2)}, u32[]{:S(2)}) async-start(bf16[16,32,640]{2,1,0:T(8,128)(2,1)} %bitcast.86), calls=%async_computation.4 | async-start | bytes 1310720 | tf_op jit(solution)/shard_map/all_to_all | solution.py:89
  178.0 2.5 %fusion.67 = f32[640,1152]{1,0:T(8,128)S(1)} fusion(bf16[512,640]{1,0:T(8,128)(2,1)} %copy-done.2, bf16[512,1152]{1,0:T(8,128)(2,1)} %bitcast.81), kind=kOutput, calls=%fused_computation.87 | convolution fusion | flops 754974720 | bytes 4784128 | tf_op jit(solution)/shard_map/dot_general | solution.py:44
  180.5 2.2 %fusion = bf16[640,1152]{1,0:T(8,128)(2,1)} fusion(f32[640,1152]{1,0:T(8,128)S(1)} %fusion.67, bf16[512,640]{1,0:T(8,128)(2,1)S(1)} %all_gather.3, bf16[512,1152]{1,0:T(8,128)(2,1)S(1)} %bitcast.79), kind=kOutput, calls=%fused_computation.1 | convolution fusion | flops 756449280 | bytes 6258688 | tf_op jit(solution)/shard_map/dot_general | solution.py:44
  182.7 31.3 %all-to-all-done.4 = bf16[16,32,640]{2,1,0:T(8,128)(2,1)} async-done(((bf16[16,32,640]{2,1,0:T(8,128)(2,1)}), bf16[16,32,640]{2,1,0:T(8,128)(2,1)}, u32[]{:S(2)}, u32[]{:S(2)}) %all-to-all-start.4) | async-done | bytes 655392 | tf_op jit(solution)/shard_map/all_to_all | solution.py:89
  (31 shorter events, 15.9 us)
Async XLA Ops:
  0.6 54.4 %copy-start = (bf16[640,1152]{1,0:T(8,128)(2,1)S(1)}, bf16[640,1152]{1,0:T(8,128)(2,1)}, u32[]{:S(2)}) copy-start(bf16[640,1152]{1,0:T(8,128)(2,1)} %param.7) | copy-start | bytes 4423684
  2.8 5.9 %collective-permute-start = (bf16[32,640]{1,0:T(8,128)(2,1)S(1)}, bf16[32,640]{1,0:T(8,128)(2,1)S(1)}, u32[]{:S(2)}, u32[]{:S(2)}) collective-permute-start(bf16[32,640]{1,0:T(8,128)(2,1)S(1)} %bitcast.90), channel_id=1, source_target_pairs={{0,1},{1,0},{2,3},{3,2},{4,5},{5,4},{6,7},{7,6},{8,9},{9,8},{10,11... | collective-permute-start | bytes 122888 | tf_op jit(solution)/shard_map/ppermute | solution.py:73
  50.3 13.3 %collective-permute-start.1 = (bf16[512,640]{1,0:T(8,128)(2,1)S(1)}, bf16[512,640]{1,0:T(8,128)(2,1)S(1)}, u32[]{:S(2)}, u32[]{:S(2)}) collective-permute-start(bf16[512,640]{1,0:T(8,128)(2,1)S(1)} %all_gather.3), channel_id=1, source_target_pairs={{0,1},{1,0},{2,3},{3,2},{4,5},{5,4},{6,7},{7,6},{8,9},{9,8},{10,11... | collective-permute-start | bytes 1966088 | tf_op jit(solution)/shard_map/ppermute | solution.py:75
  56.5 10.5 %collective-permute-start.4 = (bf16[256,1152]{1,0:T(8,128)(2,1)}, bf16[256,1152]{1,0:T(8,128)(2,1)S(1)}, u32[]{:S(2)}, u32[]{:S(2)}) collective-permute-start(bf16[256,1152]{1,0:T(8,128)(2,1)} %convolution_convert_fusion), channel_id=1, source_target_pairs={{0,32},{32,0},{1,33},{33,1},{2,34},{34,2},{3,35},{35,3},{4,36},{36... | collective-permute-start | bytes 1769480 | tf_op jit(solution)/shard_map/ppermute | solution.py:53
  63.6 12.0 %copy-start.2 = (bf16[512,640]{1,0:T(8,128)(2,1)}, bf16[512,640]{1,0:T(8,128)(2,1)S(1)}, u32[]{:S(2)}) copy-start(bf16[512,640]{1,0:T(8,128)(2,1)S(1)} %collective-permute-done.1) | copy-start | bytes 1966084
  65.1 10.5 %collective-permute-start.2 = (bf16[256,1152]{1,0:T(8,128)(2,1)}, bf16[256,1152]{1,0:T(8,128)(2,1)}, u32[]{:S(2)}, u32[]{:S(2)}) collective-permute-start(bf16[256,1152]{1,0:T(8,128)(2,1)} %convolution_convert_fusion.1), channel_id=1, source_target_pairs={{0,32},{32,0},{1,33},{33,1},{2,34},{34,2},{3,35},{35,3},{4,36},{36... | collective-permute-start | bytes 1769480 | tf_op jit(solution)/shard_map/ppermute | solution.py:53
  68.5 20.1 %all-to-all-start.2 = ((bf16[8,32,1152]{2,1,0:T(8,128)(2,1)}), bf16[8,32,1152]{2,1,0:T(8,128)(2,1)S(1)}, u32[]{:S(2)}, u32[]{:S(2)}) async-start(bf16[8,32,1152]{2,1,0:T(8,128)(2,1)} %bitcast.15), calls=%async_computation.2 | async-start | bytes 1179648 | tf_op jit(solution)/shard_map/all_to_all | solution.py:56
  88.5 16.0 %all-to-all-start = ((bf16[8,32,1152]{2,1,0:T(8,128)(2,1)}), bf16[8,32,1152]{2,1,0:T(8,128)(2,1)S(1)}, u32[]{:S(2)}, u32[]{:S(2)}) async-start(bf16[8,32,1152]{2,1,0:T(8,128)(2,1)} %bitcast.5), calls=%async_computation | async-start | bytes 1179648 | tf_op jit(solution)/shard_map/all_to_all | solution.py:56
  120.6 22.2 %copy-start.3 = (bf16[8,32,1152]{2,1,0:T(8,128)(2,1)}, bf16[8,32,1152]{2,1,0:T(8,128)(2,1)S(1)}, u32[]{:S(2)}) copy-start(bf16[8,32,1152]{2,1,0:T(8,128)(2,1)S(1)} %all_to_all.45) | copy-start | bytes 1769476
  120.6 22.1 %collective-permute-start.5 = (bf16[256,1152]{1,0:T(8,128)(2,1)S(1)}, bf16[256,1152]{1,0:T(8,128)(2,1)S(1)}, u32[]{:S(2)}, u32[]{:S(2)}) collective-permute-start(bf16[256,1152]{1,0:T(8,128)(2,1)S(1)} %bitcast.84), channel_id=1, source_target_pairs={{0,32},{32,0},{1,33},{33,1},{2,34},{34,2},{3,35},{35,3},{4,36},{36... | collective-permute-start | bytes 1769480 | tf_op jit(solution)/shard_map/ppermute | solution.py:61
  123.4 17.5 %all-to-all-start.1 = ((bf16[8,32,1152]{2,1,0:T(8,128)(2,1)}), bf16[8,32,1152]{2,1,0:T(8,128)(2,1)}, u32[]{:S(2)}, u32[]{:S(2)}) async-start(bf16[8,32,1152]{2,1,0:T(8,128)(2,1)} %broadcast_in_dim.9), calls=%async_computation.1 | async-start | bytes 1179648 | tf_op jit(solution)/shard_map/all_to_all | solution.py:60
  140.9 8.5 %collective-permute-start.3 = (bf16[256,1152]{1,0:T(8,128)(2,1)}, bf16[256,1152]{1,0:T(8,128)(2,1)S(1)}, u32[]{:S(2)}, u32[]{:S(2)}) collective-permute-start(bf16[256,1152]{1,0:T(8,128)(2,1)} %bitcast.9), channel_id=1, source_target_pairs={{0,32},{32,0},{1,33},{33,1},{2,34},{34,2},{3,35},{35,3},{4,36},{36... | collective-permute-start | bytes 1769480 | tf_op jit(solution)/shard_map/ppermute | solution.py:61
  142.8 0.8 copy-start.4
  146.8 19.0 %collective-permute-start.6 = (bf16[512,640]{1,0:T(8,128)(2,1)S(1)}, bf16[512,640]{1,0:T(8,128)(2,1)S(1)}, u32[]{:S(2)}, u32[]{:S(2)}) collective-permute-start(bf16[512,640]{1,0:T(8,128)(2,1)S(1)} %convolution_convert_fusion.2), channel_id=1, source_target_pairs={{0,1},{1,0},{2,3},{3,2},{4,5},{5,4},{6,7},{7,6},{8,9},{9,8},{10,11... | collective-permute-start | bytes 1966088 | tf_op jit(solution)/shard_map/ppermute | solution.py:85
  150.9 17.0 %copy-start.1 = (bf16[2,256,1152]{2,1,0:T(8,128)(2,1)}, bf16[2,256,1152]{2,1,0:T(8,128)(2,1)S(1)}, u32[]{:S(2)}) copy-start(bf16[2,256,1152]{2,1,0:T(8,128)(2,1)S(1)} %maximum_select_fusion) | copy-start | bytes 3538948
  167.8 46.2 %all-to-all-start.4 = ((bf16[16,32,640]{2,1,0:T(8,128)(2,1)}), bf16[16,32,640]{2,1,0:T(8,128)(2,1)}, u32[]{:S(2)}, u32[]{:S(2)}) async-start(bf16[16,32,640]{2,1,0:T(8,128)(2,1)} %bitcast.86), calls=%async_computation.4 | async-start | bytes 1310720 | tf_op jit(solution)/shard_map/all_to_all | solution.py:89

commit v2 on v1

v2 whole, which is shorter than its diff:
```python
import math

import jax
import jax.numpy as jnp
from jax import lax
from jax.experimental import pallas as pl
from jax.experimental.pallas import tpu as pltpu
from jax.sharding import Mesh
from jax.sharding import PartitionSpec as P

AXES = ("yh", "x", "c", "z", "yl")
SIZES = (2, 4, 2, 16, 2)
DP = ("yh", "x", "c")
TENSOR = ("z", "yl")
SWAP = [(0, 1), (1, 0)]
PIECES = ((-4, 0, 4, 8), (-5, -1, 3, 7), (-3, 1, 5, 9), (-6, -2), (2, 6))
VMEM = pl.BlockSpec(memory_space=pltpu.VMEM)
SMEM = pl.BlockSpec(memory_space=pltpu.SMEM)
PARAMS = pltpu.CompilerParams(vmem_limit_bytes=24 * 1024 * 1024)


def hadamard_table():
    index = lax.iota(jnp.int32, 128)
    common = jnp.bitwise_and(index[:, None], index[None, :])
    parity = jnp.zeros((128, 128), jnp.int32)
    for shift in range(7):
        parity = parity + jnp.bitwise_and(jnp.right_shift(common, shift), 1)
    signs = 1.0 - 2.0 * (parity % 2).astype(jnp.float32)
    return signs / math.sqrt(128.0)


def decode(coded, scales):
    count = coded.shape[0]
    blocks = coded.astype(jnp.float32).reshape(count, scales.shape[1], 128) * scales[:, :, None]
    turned = jnp.einsum("rbk,kj->rbj", blocks, hadamard_table(), precision=lax.Precision.HIGHEST)
    return turned.reshape(count, coded.shape[1]).astype(jnp.bfloat16)


def gelu_slope(value):
    cdf = 0.5 * (1.0 + jax.scipy.special.erf(value / math.sqrt(2.0)))
    pdf = jnp.exp(-0.5 * value * value) / math.sqrt(2.0 * math.pi)
    return cdf + value * pdf


def slope_grad(pre, grads):
    return (grads.astype(jnp.float32) * gelu_slope(pre)).astype(jnp.bfloat16)


def dot(a, b, dims):
    return lax.dot_general(a, b, (dims, ((), ())), preferred_element_type=jnp.float32)


def along_z(array, step, flip=False):
    pairs = [(2 * z + y, 2 * ((z + step) % 16) + (1 - y if flip else y)) for z in range(16) for y in range(2)]
    return lax.ppermute(array, TENSOR, pairs)


def swap_cores(array):
    return lax.ppermute(array, "c", SWAP)


def exchange(blocks):
    return lax.all_to_all(blocks, ("yh", "x"), 0, 0, tiled=True)


def copies(grad):
    return jnp.broadcast_to(grad[None], (8,) + grad.shape)


def places(pieces):
    z, core = lax.axis_index("z"), lax.axis_index("c")
    offsets = jnp.array([d for piece in pieces for d in piece], jnp.int32)
    block = lax.rem(z + offsets + 16, 16)
    return jnp.bitwise_xor(jnp.bitwise_and(block, 1), core) * 8 + block // 2


def gather_kernel(place_ref, a_ref, b_ref, c_ref, d_ref, e_ref, w_ref, rows_ref, far_ref):
    at = 0
    for piece in (a_ref, b_ref, c_ref, d_ref, e_ref):
        for i in range(piece.shape[0]):
            rows_ref[place_ref[at]] = piece[i]
            at += 1
    rows = rows_ref[8:16].reshape(256, 640)
    for j in range(0, 1152, 384):
        far_ref[:, j : j + 384] = jnp.dot(
            rows, w_ref[:, j : j + 384], preferred_element_type=jnp.float32
        ).astype(jnp.bfloat16)


def spread_kernel(place_ref, part_ref, *out_refs):
    at = 0
    for piece in out_refs:
        for i in range(piece.shape[0]):
            piece[i] = part_ref[place_ref[at]]
            at += 1


def gathered(own, w_in):
    a1, a0, a2, a3 = (along_z(own, step, flip=True) for step in (4, 0, -4, 8))
    stack = jnp.stack([a1, a0, a2, a3])
    pieces = (stack, along_z(stack, 1), along_z(stack, -1), along_z(stack[0:2], 2), along_z(stack[1:3], -2))
    return pl.pallas_call(
        gather_kernel,
        out_shape=(
            jax.ShapeDtypeStruct((16, 32, 640), jnp.bfloat16),
            jax.ShapeDtypeStruct((256, 1152), jnp.bfloat16),
        ),
        in_specs=[SMEM] + [VMEM] * 6,
        out_specs=(VMEM, VMEM),
        compiler_params=PARAMS,
        cost_estimate=pl.CostEstimate(flops=2 * 256 * 640 * 1152, bytes_accessed=4 * 1024 * 1024, transcendentals=0),
    )(places(PIECES), *pieces, w_in)


SENT = ((-4, 0, 4, 8), (-3, 1, 5, 9), (-5, -1, 3, 7), (2, 6), (-6, -2))


def scattered(part):
    shapes = [jax.ShapeDtypeStruct((len(s), 32, 640), jnp.bfloat16) for s in SENT]
    own, right, left, right2, left2 = pl.pallas_call(
        spread_kernel,
        out_shape=shapes,
        in_specs=[SMEM, VMEM],
        out_specs=[VMEM] * 5,
        compiler_params=PARAMS,
        cost_estimate=pl.CostEstimate(flops=0, bytes_accessed=1310720, transcendentals=0),
    )(places(SENT), part.reshape(16, 32, 640))
    right, left, right2, left2 = along_z(right, 1), along_z(left, -1), along_z(right2, 2), along_z(left2, -2)
    f = lambda v: v.astype(jnp.float32)
    near = f(own) + f(right) + f(left)
    low = (near[0] + f(left2[0])).astype(jnp.bfloat16)
    high = (near[2] + f(right2[1])).astype(jnp.bfloat16)
    apart = near[3].astype(jnp.bfloat16)
    low, high, apart = along_z(low, -4), along_z(high, 4), along_z(apart, 8)
    mine = near[1] + f(right2[0]) + f(left2[1])
    return mine + f(low) + f(high) + f(apart)


def shards(x_rotated, block_scales, grad_act, w_in):
    side = lax.axis_index("yl")
    grads = grad_act.reshape(2, 32, -1)
    grads_p = lax.dynamic_index_in_dim(grads, 1 - side, 0, keepdims=False)
    grads_o = lax.dynamic_index_in_dim(grads, side, 0, keepdims=False)
    own = decode(x_rotated, block_scales)
    rows_p, far_p = gathered(own, w_in)
    rows_p = rows_p.reshape(512, -1)
    rows_o = lax.ppermute(rows_p, "yl", SWAP)
    far_p = swap_cores(far_p)

    def near_sum(rows, far):
        near = dot(rows[:256], w_in, ((1,), (0,))) + far.astype(jnp.float32)
        return near.astype(jnp.bfloat16).reshape(8, 32, -1)

    def slopes(parts, grads):
        return slope_grad(jnp.sum(parts.astype(jnp.float32), axis=0), grads)

    parts_p = exchange(near_sum(rows_p, far_p))
    far_o = swap_cores(dot(rows_o[256:], w_in, ((1,), (0,))).astype(jnp.bfloat16))
    near_o = near_sum(rows_o, far_o)
    grad_p = slopes(parts_p, grads_p)
    mixed = exchange(jnp.concatenate([near_o, copies(grad_p)], axis=1))
    grad_o = slopes(mixed[:, :32], grads_o)
    mine_p = mixed[:, 32:].reshape(256, -1)
    mine_o = exchange(copies(grad_o)).reshape(256, -1)
    other_p = swap_cores(mine_p)
    pre_p = jnp.concatenate([mine_p, other_p])
    part_p = dot(pre_p, w_in, ((1,), (1,))).astype(jnp.bfloat16)
    part_p = lax.ppermute(part_p, "yl", SWAP)
    pre_o = jnp.concatenate([mine_o, swap_cores(mine_o)])
    part = (dot(pre_o, w_in, ((1,), (1,))) + part_p.astype(jnp.float32)).astype(jnp.bfloat16)
    grad_input = scattered(part)
    grad_weight = dot(rows_p, pre_p, ((0,), (0,))) + dot(rows_o, pre_o, ((0,), (0,)))
    return grad_input.astype(jnp.bfloat16), grad_weight.astype(jnp.bfloat16)


def solution(mesh):
    fine = Mesh(mesh.devices.reshape(SIZES), AXES)
    in_specs = (P(TENSOR, DP), P(TENSOR, DP), P(DP, TENSOR), P(DP, TENSOR))
    out_specs = (P(TENSOR, DP), P(DP, TENSOR))
    return jax.shard_map(shards, mesh=fine, in_specs=in_specs, out_specs=out_specs, check_vma=False)
```

time: 217 us -> 192 us (0.88)
  the two profiles are of different devices: /device:TPU:64 before, /device:TPU:6 now
where the time goes in v2:
time: 192 us; the launch traced here: 189 us
  starting transfers between devices  108 us (56%)
  waiting for transfers between devices  58 us (30%)
  matrix products  14 us (7%)
  local copies, waits for them, and re-layouts  3.6 us (2%)
  other arithmetic  2.41 us (1%)
    ppermute x15, starting transfers between devices, along_z(): return lax.ppermute(array, TENSOR, pairs)  77.5 us
    all_to_all x3, waiting for transfers between devices, exchange(): return lax.all_to_all(blocks, ('yh', 'x'), 0, 0, tiled=True)  21.9 us
    all_to_all x3, starting transfers between devices, exchange(): return lax.all_to_all(blocks, ('yh', 'x'), 0, 0, tiled=True)  19.2 us
    ppermute x1, waiting for transfers between devices, shards(): rows_o = lax.ppermute(rows_p, 'yl', SWAP)  13.8 us
    dot_general x7, matrix products, dot(): lax.dot_general(a, b, (dims, ((), ())), preferred_element_type=jnp.float32)  13.7 us
    ppermute x15, waiting for transfers between devices, along_z(): return lax.ppermute(array, TENSOR, pairs)  10.8 us
    ppermute x4, starting transfers between devices, swap_cores(): return lax.ppermute(array, 'c', SWAP)  7.65 us
    ppermute x1, waiting for transfers between devices, shards(): part_p = lax.ppermute(part_p, 'yl', SWAP)  7.43 us
  transfers between devices with their start and end apart: 24, of which 9 were waited for; matrix products, arithmetic and copies ran while one was open for 6% of the time, Pallas kernels for 0%

profile of v2, /device:TPU:6, one launch (start us, length us, event | category | flops | bytes accessed | tf_op | source)
XLA Modules:
  0.0 189.2 jit_solution(4064912857480136428)
XLA Ops:
  2.8 13.7 %collective-permute-start.2 = (bf16[32,640]{1,0:T(8,128)(2,1)S(1)}, bf16[32,640]{1,0:T(8,128)(2,1)S(1)}, u32[]{:S(2)}, u32[]{:S(2)}) collective-permute-start(bf16[32,640]{1,0:T(8,128)(2,1)S(1)} %bitcast.92), channel_id=1, source_target_pairs={{0,25},{1,24},{2,27},{3,26},{4,29},{5,28},{6,31},{7,30},{8,1},{9,0... | collective-permute-start | bytes 122888 | tf_op jit(solution)/shard_map/ppermute | solution.py:55
  16.6 2.4 %collective-permute-start.1 = (bf16[32,640]{1,0:T(8,128)(2,1)S(1)}, bf16[32,640]{1,0:T(8,128)(2,1)S(1)}, u32[]{:S(2)}, u32[]{:S(2)}) collective-permute-start(bf16[32,640]{1,0:T(8,128)(2,1)S(1)} %bitcast.93), channel_id=1, source_target_pairs={{0,1},{1,0},{2,3},{3,2},{4,5},{5,4},{6,7},{7,6},{8,9},{9,8},{10,11... | collective-permute-start | bytes 122888 | tf_op jit(solution)/shard_map/ppermute | solution.py:55
  20.8 11.7 %collective-permute-start.3 = (bf16[32,640]{1,0:T(8,128)(2,1)S(1)}, bf16[32,640]{1,0:T(8,128)(2,1)S(1)}, u32[]{:S(2)}, u32[]{:S(2)}) collective-permute-start(bf16[32,640]{1,0:T(8,128)(2,1)S(1)} %bitcast.95), channel_id=1, source_target_pairs={{0,17},{1,16},{2,19},{3,18},{4,21},{5,20},{6,23},{7,22},{8,25},{9,... | collective-permute-start | bytes 122888 | tf_op jit(solution)/shard_map/ppermute | solution.py:55
  32.6 3.7 %collective-permute-done.3 = bf16[32,640]{1,0:T(8,128)(2,1)S(1)} collective-permute-done((bf16[32,640]{1,0:T(8,128)(2,1)S(1)}, bf16[32,640]{1,0:T(8,128)(2,1)S(1)}, u32[]{:S(2)}, u32[]{:S(2)}) %collective-permute-start.3) | collective-permute-done | bytes 40992 | tf_op jit(solution)/shard_map/ppermute | solution.py:55
  36.4 7.5 %collective-permute-start.5 = (bf16[4,32,640]{2,1,0:T(8,128)(2,1)S(1)}, bf16[4,32,640]{2,1,0:T(8,128)(2,1)S(1)}, u32[]{:S(2)}, u32[]{:S(2)}) collective-permute-start(bf16[4,32,640]{2,1,0:T(8,128)(2,1)S(1)} %pad_maximum_fusion.7.a_ref), channel_id=1, source_target_pairs={{0,30},{1,31},{2,0},{3,1},{4,2},{5,3},{6,4},{7,5},{8,6},{9,7},{10,... | collective-permute-start | bytes 491528 | tf_op jit(solution)/shard_map/ppermute | solution.py:55
  45.8 4.4 %collective-permute-start.7 = (bf16[2,32,640]{2,1,0:T(8,128)(2,1)S(1)}, bf16[2,32,640]{2,1,0:T(8,128)(2,1)S(1)}, u32[]{:S(2)}, u32[]{:S(2)}) collective-permute-start(bf16[2,32,640]{2,1,0:T(8,128)(2,1)S(1)} %get-tuple-element.18), channel_id=1, source_target_pairs={{0,28},{1,29},{2,30},{3,31},{4,0},{5,1},{6,2},{7,3},{8,4},{9,5},{1... | collective-permute-start | bytes 245768 | tf_op jit(solution)/shard_map/ppermute | solution.py:55
  50.2 2.4 %collective-permute-start.6 = (bf16[2,32,640]{2,1,0:T(8,128)(2,1)S(1)}, bf16[2,32,640]{2,1,0:T(8,128)(2,1)S(1)}, u32[]{:S(2)}, u32[]{:S(2)}) collective-permute-start(bf16[2,32,640]{2,1,0:T(8,128)(2,1)S(1)} %get-tuple-element.19), channel_id=1, source_target_pairs={{0,4},{1,5},{2,6},{3,7},{4,8},{5,9},{6,10},{7,11},{8,12},{9,13},{1... | collective-permute-start | bytes 245768 | tf_op jit(solution)/shard_map/ppermute | solution.py:55
  53.1 6.6 %collective-permute-done.6.d_ref = bf16[2,32,640]{2,1,0:T(8,128)(2,1)S(1)} collective-permute-done((bf16[2,32,640]{2,1,0:T(8,128)(2,1)S(1)}, bf16[2,32,640]{2,1,0:T(8,128)(2,1)S(1)}, u32[]{:S(2)}, u32[]{:S(2)}) %collective-permute-start.6) | collective-permute-done | bytes 81952 | tf_op jit(solution)/shard_map/ppermute | solution.py:55
  66.3 6.9 %all-to-all-start = ((bf16[8,32,1152]{2,1,0:T(8,128)(2,1)}), bf16[8,32,1152]{2,1,0:T(8,128)(2,1)S(1)}, u32[]{:S(2)}, u32[]{:S(2)}) async-start(bf16[8,32,1152]{2,1,0:T(8,128)(2,1)} %bitcast.80), calls=%async_computation | async-start | bytes 1179648 | tf_op jit(solution)/shard_map/all_to_all | solution.py:63
  73.2 13.8 %collective-permute-done.8 = bf16[512,640]{1,0:T(8,128)(2,1)S(1)} collective-permute-done((bf16[512,640]{1,0:T(8,128)(2,1)S(1)}, bf16[512,640]{1,0:T(8,128)(2,1)S(1)}, u32[]{:S(2)}, u32[]{:S(2)}) %collective-permute-start.8) | collective-permute-done | bytes 655392 | tf_op jit(solution)/shard_map/ppermute | solution.py:147
  95.7 6.2 %all-to-all-start.1 = ((bf16[8,64,1152]{2,1,0:T(8,128)(2,1)}), bf16[8,64,1152]{2,1,0:T(8,128)(2,1)S(1)}, u32[]{:S(2)}, u32[]{:S(2)}) async-start(bf16[8,64,1152]{2,1,0:T(8,128)(2,1)} %pad_maximum_fusion), calls=%async_computation.1 | async-start | bytes 2359296 | tf_op jit(solution)/shard_map/all_to_all | solution.py:63
  102.0 16.2 %all-to-all-done.1 = bf16[8,64,1152]{2,1,0:T(8,128)(2,1)S(1)} async-done(((bf16[8,64,1152]{2,1,0:T(8,128)(2,1)}), bf16[8,64,1152]{2,1,0:T(8,128)(2,1)S(1)}, u32[]{:S(2)}, u32[]{:S(2)}) %all-to-all-start.1) | async-done | bytes 1179680 | tf_op jit(solution)/shard_map/all_to_all | solution.py:63
  122.1 6.1 %all-to-all-start.2 = ((bf16[8,32,1152]{2,1,0:T(8,128)(2,1)}), bf16[8,32,1152]{2,1,0:T(8,128)(2,1)S(1)}, u32[]{:S(2)}, u32[]{:S(2)}) async-start(bf16[8,32,1152]{2,1,0:T(8,128)(2,1)} %broadcast_in_dim.22), calls=%async_computation.2 | async-start | bytes 1179648 | tf_op jit(solution)/shard_map/all_to_all | solution.py:63
  128.2 3.3 %convolution_convert_fusion.1 = bf16[512,640]{1,0:T(8,128)(2,1)} fusion(bf16[640,1152]{1,0:T(8,128)(2,1)S(1)} %copy-done, bf16[256,1152]{1,0:T(8,128)(2,1)} %collective-permute-done.12, bf16[256,1152]{1,0:T(8,128)(2,1)} %bitcast.15), kind=kOutput, calls=%fused_computation.9 | convolution fusion | flops 757661696 | bytes 3309568 | tf_op jit(solution)/shard_map/dot_general | solution.py:50
  133.4 5.7 %all-to-all-done.2 = bf16[8,32,1152]{2,1,0:T(8,128)(2,1)S(1)} async-done(((bf16[8,32,1152]{2,1,0:T(8,128)(2,1)}), bf16[8,32,1152]{2,1,0:T(8,128)(2,1)S(1)}, u32[]{:S(2)}, u32[]{:S(2)}) %all-to-all-start.2) | async-done | bytes 589856 | tf_op jit(solution)/shard_map/all_to_all | solution.py:63
  143.0 7.4 %collective-permute-done.13 = bf16[512,640]{1,0:T(8,128)(2,1)S(1)} collective-permute-done((bf16[512,640]{1,0:T(8,128)(2,1)}, bf16[512,640]{1,0:T(8,128)(2,1)S(1)}, u32[]{:S(2)}, u32[]{:S(2)}) %collective-permute-start.13) | collective-permute-done | bytes 655392 | tf_op jit(solution)/shard_map/ppermute | solution.py:168
  152.3 4.1 %collective-permute-start.14 = (bf16[4,32,640]{2,1,0:T(8,128)(2,1)S(1)}, bf16[4,32,640]{2,1,0:T(8,128)(2,1)S(1)}, u32[]{:S(2)}, u32[]{:S(2)}) collective-permute-start(bf16[4,32,640]{2,1,0:T(8,128)(2,1)S(1)} %get-tuple-element.12), channel_id=1, source_target_pairs={{0,2},{1,3},{2,4},{3,5},{4,6},{5,7},{6,8},{7,9},{8,10},{9,11},{10,... | collective-permute-start | bytes 491528 | tf_op jit(solution)/shard_map/ppermute | solution.py:55
  156.4 2.9 %collective-permute-start.15 = (bf16[4,32,640]{2,1,0:T(8,128)(2,1)S(1)}, bf16[4,32,640]{2,1,0:T(8,128)(2,1)S(1)}, u32[]{:S(2)}, u32[]{:S(2)}) collective-permute-start(bf16[4,32,640]{2,1,0:T(8,128)(2,1)S(1)} %get-tuple-element.13), channel_id=1, source_target_pairs={{0,30},{1,31},{2,0},{3,1},{4,2},{5,3},{6,4},{7,5},{8,6},{9,7},{10,... | collective-permute-start | bytes 491528 | tf_op jit(solution)/shard_map/ppermute | solution.py:55
  160.4 2.4 %collective-permute-start.16 = (bf16[2,32,640]{2,1,0:T(8,128)(2,1)S(1)}, bf16[2,32,640]{2,1,0:T(8,128)(2,1)S(1)}, u32[]{:S(2)}, u32[]{:S(2)}) collective-permute-start(bf16[2,32,640]{2,1,0:T(8,128)(2,1)S(1)} %get-tuple-element.14), channel_id=1, source_target_pairs={{0,4},{1,5},{2,6},{3,7},{4,8},{5,9},{6,10},{7,11},{8,12},{9,13},{1... | collective-permute-start | bytes 245768 | tf_op jit(solution)/shard_map/ppermute | solution.py:55
  162.8 5.6 %collective-permute-start.17 = (bf16[2,32,640]{2,1,0:T(8,128)(2,1)S(1)}, bf16[2,32,640]{2,1,0:T(8,128)(2,1)S(1)}, u32[]{:S(2)}, u32[]{:S(2)}) collective-permute-start(bf16[2,32,640]{2,1,0:T(8,128)(2,1)S(1)} %get-tuple-element.15), channel_id=1, source_target_pairs={{0,28},{1,29},{2,30},{3,31},{4,0},{5,1},{6,2},{7,3},{8,4},{9,5},{1... | collective-permute-start | bytes 245768 | tf_op jit(solution)/shard_map/ppermute | solution.py:55
  168.5 6.8 %collective-permute-start.20 = (bf16[32,640]{1,0:T(8,128)(2,1)S(1)}, bf16[32,640]{1,0:T(8,128)(2,1)S(1)}, u32[]{:S(2)}, u32[]{:S(2)}) collective-permute-start(bf16[32,640]{1,0:T(8,128)(2,1)S(1)} %fusion.49), channel_id=1, source_target_pairs={{0,16},{1,17},{2,18},{3,19},{4,20},{5,21},{6,22},{7,23},{8,24},{9,... | collective-permute-start | bytes 122888 | tf_op jit(solution)/shard_map/ppermute | solution.py:55
  175.3 3.0 %collective-permute-start.18 = (bf16[32,640]{1,0:T(8,128)(2,1)S(1)}, bf16[32,640]{1,0:T(8,128)(2,1)S(1)}, u32[]{:S(2)}, u32[]{:S(2)}) collective-permute-start(bf16[32,640]{1,0:T(8,128)(2,1)S(1)} %get-tuple-element.16), channel_id=1, source_target_pairs={{0,24},{1,25},{2,26},{3,27},{4,28},{5,29},{6,30},{7,31},{8,0},{9,1... | collective-permute-start | bytes 122888 | tf_op jit(solution)/shard_map/ppermute | solution.py:55
  178.3 6.8 %collective-permute-start.19 = (bf16[32,640]{1,0:T(8,128)(2,1)S(1)}, bf16[32,640]{1,0:T(8,128)(2,1)S(1)}, u32[]{:S(2)}, u32[]{:S(2)}) collective-permute-start(bf16[32,640]{1,0:T(8,128)(2,1)S(1)} %get-tuple-element.17), channel_id=1, source_target_pairs={{0,8},{1,9},{2,10},{3,11},{4,12},{5,13},{6,14},{7,15},{8,16},{9,17... | collective-permute-start | bytes 122888 | tf_op jit(solution)/shard_map/ppermute | solution.py:55
  185.1 3.4 %fusion = bf16[640,1152]{1,0:T(8,128)(2,1)} fusion(f32[640,1152]{1,0:T(8,128)S(1)} %fusion.5, bf16[512,640]{1,0:T(8,128)(2,1)S(1)} %bitcast.75, bf16[256,1152]{1,0:T(8,128)(2,1)} %collective-permute-done.12, bf16[256,1152]{1,0:T(8,128)(2,1)} %bitcast.15), kind=kOutput, calls=%fused_computation.1 | convolution fusion | flops 758808576 | bytes 6258688 | tf_op jit(solution)/shard_map/dot_general | solution.py:50
  (67 shorter events, 35.1 us)
Async XLA Ops:
  2.8 29.8 %collective-permute-start.2 = (bf16[32,640]{1,0:T(8,128)(2,1)S(1)}, bf16[32,640]{1,0:T(8,128)(2,1)S(1)}, u32[]{:S(2)}, u32[]{:S(2)}) collective-permute-start(bf16[32,640]{1,0:T(8,128)(2,1)S(1)} %bitcast.92), channel_id=1, source_target_pairs={{0,25},{1,24},{2,27},{3,26},{4,29},{5,28},{6,31},{7,30},{8,1},{9,0... | collective-permute-start | bytes 122888 | tf_op jit(solution)/shard_map/ppermute | solution.py:55
  16.6 16.0 %collective-permute-start.1 = (bf16[32,640]{1,0:T(8,128)(2,1)S(1)}, bf16[32,640]{1,0:T(8,128)(2,1)S(1)}, u32[]{:S(2)}, u32[]{:S(2)}) collective-permute-start(bf16[32,640]{1,0:T(8,128)(2,1)S(1)} %bitcast.93), channel_id=1, source_target_pairs={{0,1},{1,0},{2,3},{3,2},{4,5},{5,4},{6,7},{7,6},{8,9},{9,8},{10,11... | collective-permute-start | bytes 122888 | tf_op jit(solution)/shard_map/ppermute | solution.py:55
  18.9 13.7 %collective-permute-start = (bf16[32,640]{1,0:T(8,128)(2,1)S(1)}, bf16[32,640]{1,0:T(8,128)(2,1)S(1)}, u32[]{:S(2)}, u32[]{:S(2)}) collective-permute-start(bf16[32,640]{1,0:T(8,128)(2,1)S(1)} %bitcast.94), channel_id=1, source_target_pairs={{0,9},{1,8},{2,11},{3,10},{4,13},{5,12},{6,15},{7,14},{8,17},{9,16... | collective-permute-start | bytes 122888 | tf_op jit(solution)/shard_map/ppermute | solution.py:55
  20.8 15.5 %collective-permute-start.3 = (bf16[32,640]{1,0:T(8,128)(2,1)S(1)}, bf16[32,640]{1,0:T(8,128)(2,1)S(1)}, u32[]{:S(2)}, u32[]{:S(2)}) collective-permute-start(bf16[32,640]{1,0:T(8,128)(2,1)S(1)} %bitcast.95), channel_id=1, source_target_pairs={{0,17},{1,16},{2,19},{3,18},{4,21},{5,20},{6,23},{7,22},{8,25},{9,... | collective-permute-start | bytes 122888 | tf_op jit(solution)/shard_map/ppermute | solution.py:55
  36.4 23.2 %collective-permute-start.5 = (bf16[4,32,640]{2,1,0:T(8,128)(2,1)S(1)}, bf16[4,32,640]{2,1,0:T(8,128)(2,1)S(1)}, u32[]{:S(2)}, u32[]{:S(2)}) collective-permute-start(bf16[4,32,640]{2,1,0:T(8,128)(2,1)S(1)} %pad_maximum_fusion.7.a_ref), channel_id=1, source_target_pairs={{0,30},{1,31},{2,0},{3,1},{4,2},{5,3},{6,4},{7,5},{8,6},{9,7},{10,... | collective-permute-start | bytes 491528 | tf_op jit(solution)/shard_map/ppermute | solution.py:55
  43.9 15.7 %collective-permute-start.4 = (bf16[4,32,640]{2,1,0:T(8,128)(2,1)S(1)}, bf16[4,32,640]{2,1,0:T(8,128)(2,1)S(1)}, u32[]{:S(2)}, u32[]{:S(2)}) collective-permute-start(bf16[4,32,640]{2,1,0:T(8,128)(2,1)S(1)} %pad_maximum_fusion.7.a_ref), channel_id=1, source_target_pairs={{0,2},{1,3},{2,4},{3,5},{4,6},{5,7},{6,8},{7,9},{8,10},{9,11},{10,... | collective-permute-start | bytes 491528 | tf_op jit(solution)/shard_map/ppermute | solution.py:55
  45.8 7.2 %collective-permute-start.7 = (bf16[2,32,640]{2,1,0:T(8,128)(2,1)S(1)}, bf16[2,32,640]{2,1,0:T(8,128)(2,1)S(1)}, u32[]{:S(2)}, u32[]{:S(2)}) collective-permute-start(bf16[2,32,640]{2,1,0:T(8,128)(2,1)S(1)} %get-tuple-element.18), channel_id=1, source_target_pairs={{0,28},{1,29},{2,30},{3,31},{4,0},{5,1},{6,2},{7,3},{8,4},{9,5},{1... | collective-permute-start | bytes 245768 | tf_op jit(solution)/shard_map/ppermute | solution.py:55
  50.2 9.4 %collective-permute-start.6 = (bf16[2,32,640]{2,1,0:T(8,128)(2,1)S(1)}, bf16[2,32,640]{2,1,0:T(8,128)(2,1)S(1)}, u32[]{:S(2)}, u32[]{:S(2)}) collective-permute-start(bf16[2,32,640]{2,1,0:T(8,128)(2,1)S(1)} %get-tuple-element.19), channel_id=1, source_target_pairs={{0,4},{1,5},{2,6},{3,7},{4,8},{5,9},{6,10},{7,11},{8,12},{9,13},{1... | collective-permute-start | bytes 245768 | tf_op jit(solution)/shard_map/ppermute | solution.py:55
  61.0 3.9 %collective-permute-start.10 = (bf16[256,1152]{1,0:T(8,128)(2,1)S(1)}, bf16[256,1152]{1,0:T(8,128)(2,1)S(1)}, u32[]{:S(2)}, u32[]{:S(2)}) collective-permute-start(bf16[256,1152]{1,0:T(8,128)(2,1)S(1)} %get-tuple-element.10), channel_id=1, source_target_pairs={{0,32},{32,0},{1,33},{33,1},{2,34},{34,2},{3,35},{35,3},{4,36},{36... | collective-permute-start | bytes 1769480 | tf_op jit(solution)/shard_map/ppermute | solution.py:59
  62.9 24.2 %collective-permute-start.8 = (bf16[512,640]{1,0:T(8,128)(2,1)S(1)}, bf16[512,640]{1,0:T(8,128)(2,1)S(1)}, u32[]{:S(2)}, u32[]{:S(2)}) collective-permute-start(bf16[512,640]{1,0:T(8,128)(2,1)S(1)} %bitcast.74), channel_id=1, source_target_pairs={{0,1},{1,0},{2,3},{3,2},{4,5},{5,4},{6,7},{7,6},{8,9},{9,8},{10,11... | collective-permute-start | bytes 1966088 | tf_op jit(solution)/shard_map/ppermute | solution.py:147
  66.3 24.1 %all-to-all-start = ((bf16[8,32,1152]{2,1,0:T(8,128)(2,1)}), bf16[8,32,1152]{2,1,0:T(8,128)(2,1)S(1)}, u32[]{:S(2)}, u32[]{:S(2)}) async-start(bf16[8,32,1152]{2,1,0:T(8,128)(2,1)} %bitcast.80), calls=%async_computation | async-start | bytes 1179648 | tf_op jit(solution)/shard_map/all_to_all | solution.py:63
  88.6 4.2 %collective-permute-start.9 = (bf16[256,1152]{1,0:T(8,128)(2,1)}, bf16[256,1152]{1,0:T(8,128)(2,1)}, u32[]{:S(2)}, u32[]{:S(2)}) collective-permute-start(bf16[256,1152]{1,0:T(8,128)(2,1)} %convolution_convert_fusion), channel_id=1, source_target_pairs={{0,32},{32,0},{1,33},{33,1},{2,34},{34,2},{3,35},{35,3},{4,36},{36... | collective-permute-start | bytes 1769480 | tf_op jit(solution)/shard_map/ppermute | solution.py:59
  95.7 22.5 %all-to-all-start.1 = ((bf16[8,64,1152]{2,1,0:T(8,128)(2,1)}), bf16[8,64,1152]{2,1,0:T(8,128)(2,1)S(1)}, u32[]{:S(2)}, u32[]{:S(2)}) async-start(bf16[8,64,1152]{2,1,0:T(8,128)(2,1)} %pad_maximum_fusion), calls=%async_computation.1 | async-start | bytes 2359296 | tf_op jit(solution)/shard_map/all_to_all | solution.py:63
  119.1 9.1 %collective-permute-start.12 = (bf16[256,1152]{1,0:T(8,128)(2,1)}, bf16[256,1152]{1,0:T(8,128)(2,1)}, u32[]{:S(2)}, u32[]{:S(2)}) collective-permute-start(bf16[256,1152]{1,0:T(8,128)(2,1)} %bitcast.15), channel_id=1, source_target_pairs={{0,32},{32,0},{1,33},{33,1},{2,34},{34,2},{3,35},{35,3},{4,36},{36... | collective-permute-start | bytes 1769480 | tf_op jit(solution)/shard_map/ppermute | solution.py:59
  122.1 17.0 %all-to-all-start.2 = ((bf16[8,32,1152]{2,1,0:T(8,128)(2,1)}), bf16[8,32,1152]{2,1,0:T(8,128)(2,1)S(1)}, u32[]{:S(2)}, u32[]{:S(2)}) async-start(bf16[8,32,1152]{2,1,0:T(8,128)(2,1)} %broadcast_in_dim.22), calls=%async_computation.2 | async-start | bytes 1179648 | tf_op jit(solution)/shard_map/all_to_all | solution.py:63
  131.5 19.0 %collective-permute-start.13 = (bf16[512,640]{1,0:T(8,128)(2,1)}, bf16[512,640]{1,0:T(8,128)(2,1)S(1)}, u32[]{:S(2)}, u32[]{:S(2)}) collective-permute-start(bf16[512,640]{1,0:T(8,128)(2,1)} %convolution_convert_fusion.1), channel_id=1, source_target_pairs={{0,1},{1,0},{2,3},{3,2},{4,5},{5,4},{6,7},{7,6},{8,9},{9,8},{10,11... | collective-permute-start | bytes 1966088 | tf_op jit(solution)/shard_map/ppermute | solution.py:168
  139.1 3.9 %collective-permute-start.11 = (bf16[256,1152]{1,0:T(8,128)(2,1)S(1)}, bf16[256,1152]{1,0:T(8,128)(2,1)S(1)}, u32[]{:S(2)}, u32[]{:S(2)}) collective-permute-start(bf16[256,1152]{1,0:T(8,128)(2,1)S(1)} %bitcast.77), channel_id=1, source_target_pairs={{0,32},{32,0},{1,33},{33,1},{2,34},{34,2},{3,35},{35,3},{4,36},{36... | collective-permute-start | bytes 1769480 | tf_op jit(solution)/shard_map/ppermute | solution.py:59
  152.3 16.1 %collective-permute-start.14 = (bf16[4,32,640]{2,1,0:T(8,128)(2,1)S(1)}, bf16[4,32,640]{2,1,0:T(8,128)(2,1)S(1)}, u32[]{:S(2)}, u32[]{:S(2)}) collective-permute-start(bf16[4,32,640]{2,1,0:T(8,128)(2,1)S(1)} %get-tuple-element.12), channel_id=1, source_target_pairs={{0,2},{1,3},{2,4},{3,5},{4,6},{5,7},{6,8},{7,9},{8,10},{9,11},{10,... | collective-permute-start | bytes 491528 | tf_op jit(solution)/shard_map/ppermute | solution.py:55
  156.4 12.0 %collective-permute-start.15 = (bf16[4,32,640]{2,1,0:T(8,128)(2,1)S(1)}, bf16[4,32,640]{2,1,0:T(8,128)(2,1)S(1)}, u32[]{:S(2)}, u32[]{:S(2)}) collective-permute-start(bf16[4,32,640]{2,1,0:T(8,128)(2,1)S(1)} %get-tuple-element.13), channel_id=1, source_target_pairs={{0,30},{1,31},{2,0},{3,1},{4,2},{5,3},{6,4},{7,5},{8,6},{9,7},{10,... | collective-permute-start | bytes 491528 | tf_op jit(solution)/shard_map/ppermute | solution.py:55
  160.4 14.9 %collective-permute-start.16 = (bf16[2,32,640]{2,1,0:T(8,128)(2,1)S(1)}, bf16[2,32,640]{2,1,0:T(8,128)(2,1)S(1)}, u32[]{:S(2)}, u32[]{:S(2)}) collective-permute-start(bf16[2,32,640]{2,1,0:T(8,128)(2,1)S(1)} %get-tuple-element.14), channel_id=1, source_target_pairs={{0,4},{1,5},{2,6},{3,7},{4,8},{5,9},{6,10},{7,11},{8,12},{9,13},{1... | collective-permute-start | bytes 245768 | tf_op jit(solution)/shard_map/ppermute | solution.py:55
  162.8 12.5 %collective-permute-start.17 = (bf16[2,32,640]{2,1,0:T(8,128)(2,1)S(1)}, bf16[2,32,640]{2,1,0:T(8,128)(2,1)S(1)}, u32[]{:S(2)}, u32[]{:S(2)}) collective-permute-start(bf16[2,32,640]{2,1,0:T(8,128)(2,1)S(1)} %get-tuple-element.15), channel_id=1, source_target_pairs={{0,28},{1,29},{2,30},{3,31},{4,0},{5,1},{6,2},{7,3},{8,4},{9,5},{1... | collective-permute-start | bytes 245768 | tf_op jit(solution)/shard_map/ppermute | solution.py:55
  168.5 20.1 %collective-permute-start.20 = (bf16[32,640]{1,0:T(8,128)(2,1)S(1)}, bf16[32,640]{1,0:T(8,128)(2,1)S(1)}, u32[]{:S(2)}, u32[]{:S(2)}) collective-permute-start(bf16[32,640]{1,0:T(8,128)(2,1)S(1)} %fusion.49), channel_id=1, source_target_pairs={{0,16},{1,17},{2,18},{3,19},{4,20},{5,21},{6,22},{7,23},{8,24},{9,... | collective-permute-start | bytes 122888 | tf_op jit(solution)/shard_map/ppermute | solution.py:55
  175.3 13.2 %collective-permute-start.18 = (bf16[32,640]{1,0:T(8,128)(2,1)S(1)}, bf16[32,640]{1,0:T(8,128)(2,1)S(1)}, u32[]{:S(2)}, u32[]{:S(2)}) collective-permute-start(bf16[32,640]{1,0:T(8,128)(2,1)S(1)} %get-tuple-element.16), channel_id=1, source_target_pairs={{0,24},{1,25},{2,26},{3,27},{4,28},{5,29},{6,30},{7,31},{8,0},{9,1... | collective-permute-start | bytes 122888 | tf_op jit(solution)/shard_map/ppermute | solution.py:55
  178.3 10.2 %collective-permute-start.19 = (bf16[32,640]{1,0:T(8,128)(2,1)S(1)}, bf16[32,640]{1,0:T(8,128)(2,1)S(1)}, u32[]{:S(2)}, u32[]{:S(2)}) collective-permute-start(bf16[32,640]{1,0:T(8,128)(2,1)S(1)} %get-tuple-element.17), channel_id=1, source_target_pairs={{0,8},{1,9},{2,10},{3,11},{4,12},{5,13},{6,14},{7,15},{8,16},{9,17... | collective-permute-start | bytes 122888 | tf_op jit(solution)/shard_map/ppermute | solution.py:55
  (6 other events, 165.2 us)

commit v3 on v2

v3 whole, which is shorter than its diff:
```python
import math

import jax
import jax.numpy as jnp
from jax import lax
from jax.experimental import pallas as pl
from jax.experimental.pallas import tpu as pltpu
from jax.sharding import Mesh
from jax.sharding import PartitionSpec as P

AXES = ("yh", "x", "c", "z", "yl")
SIZES = (2, 4, 2, 16, 2)
DP = ("yh", "x", "c")
TENSOR = ("z", "yl")
SWAP = [(0, 1), (1, 0)]
PIECES = ((-4, 0, 4, 8), (-3, 1, 5, 9), (-5, -1, 3, 7), (2, 6), (-6, -2))
VMEM = pl.BlockSpec(memory_space=pltpu.VMEM)
SMEM = pl.BlockSpec(memory_space=pltpu.SMEM)
PARAMS = pltpu.CompilerParams(vmem_limit_bytes=24 * 1024 * 1024)


def hadamard_table():
    index = lax.iota(jnp.int32, 128)
    common = jnp.bitwise_and(index[:, None], index[None, :])
    parity = jnp.zeros((128, 128), jnp.int32)
    for shift in range(7):
        parity = parity + jnp.bitwise_and(jnp.right_shift(common, shift), 1)
    signs = 1.0 - 2.0 * (parity % 2).astype(jnp.float32)
    return signs / math.sqrt(128.0)


def decode(coded, scales):
    count = coded.shape[0]
    blocks = coded.astype(jnp.float32).reshape(count, scales.shape[1], 128) * scales[:, :, None]
    turned = jnp.einsum("rbk,kj->rbj", blocks, hadamard_table(), precision=lax.Precision.HIGHEST)
    return turned.reshape(count, coded.shape[1]).astype(jnp.bfloat16)


def gelu_slope(value):
    cdf = 0.5 * (1.0 + jax.scipy.special.erf(value / math.sqrt(2.0)))
    pdf = jnp.exp(-0.5 * value * value) / math.sqrt(2.0 * math.pi)
    return cdf + value * pdf


def slope_grad(pre, grads):
    return (grads.astype(jnp.float32) * gelu_slope(pre)).astype(jnp.bfloat16)


def dot(a, b, dims):
    return lax.dot_general(a, b, (dims, ((), ())), preferred_element_type=jnp.float32)


def along_z(array, step):
    return lax.ppermute(array, "z", [(z, (z + step) % 16) for z in range(16)])


def swap_cores(array):
    return lax.ppermute(array, "c", SWAP)


def exchange(blocks):
    return lax.all_to_all(blocks, ("yh", "x"), 0, 0, tiled=True)


def copies(grad):
    return jnp.broadcast_to(grad[None], (8,) + grad.shape)


def places(pieces):
    z, core = lax.axis_index("z"), lax.axis_index("c")
    offsets = jnp.array([d for piece in pieces for d in piece], jnp.int32)
    block = lax.rem(z + offsets + 16, 16)
    return jnp.bitwise_xor(jnp.bitwise_and(block, 1), core) * 8 + block // 2


def call(kernel, out_shape, count, flops, moved):
    return pl.pallas_call(
        kernel,
        out_shape=out_shape,
        in_specs=[SMEM] + [VMEM] * count,
        out_specs=[VMEM] * len(out_shape),
        compiler_params=PARAMS,
        cost_estimate=pl.CostEstimate(flops=flops, bytes_accessed=moved, transcendentals=0),
    )


def shape(*dims):
    return jax.ShapeDtypeStruct(dims, jnp.bfloat16)


def far_kernel(core_ref, rows_ref, w_ref, v_ref, far_ref):
    rows = rows_ref[:, 1 - core_ref[0]].reshape(256, 640)
    for i, weight in enumerate((w_ref, v_ref)):
        for j in range(0, 1152, 384):
            far_ref[:, 1152 * i + j : 1152 * i + j + 384] = jnp.dot(
                rows, weight[:, j : j + 384], preferred_element_type=jnp.float32
            ).astype(jnp.bfloat16)


def near_kernel(core_ref, rows_ref, w_ref, v_ref, far_ref, near_ref):
    rows = rows_ref[:, core_ref[0]].reshape(256, 640)
    for i, weight in enumerate((w_ref, v_ref)):
        for j in range(0, 1152, 384):
            at = slice(1152 * i + j, 1152 * i + j + 384)
            total = jnp.dot(rows, weight[:, j : j + 384], preferred_element_type=jnp.float32)
            near_ref[:, :, at] = (total + far_ref[:, at].astype(jnp.float32)).astype(jnp.bfloat16).reshape(8, 32, 384)


def input_part(pre_ref, w_ref, v_ref):
    nt = (((1,), (1,)), ((), ()))
    part = lax.dot_general(pre_ref[:, :1152], w_ref[...], nt, preferred_element_type=jnp.float32)
    part += lax.dot_general(pre_ref[:, 1152:], v_ref[...], nt, preferred_element_type=jnp.float32)
    return part.astype(jnp.bfloat16).reshape(8, 32, 640)


def part_kernel(core_ref, pre_ref, w_ref, v_ref, part_ref):
    part_ref[...] = input_part(pre_ref, w_ref, v_ref)


def spread_kernel(place_ref, mine_ref, pre_ref, w_ref, v_ref, *refs):
    part_ref = refs[-1]
    part_ref[:8] = mine_ref[...]
    part_ref[8:] = input_part(pre_ref, w_ref, v_ref)
    at = 0
    for piece in refs[:-1]:
        for i in range(piece.shape[0]):
            piece[i] = part_ref[place_ref[at]]
            at += 1


def spread(mine, pre, w_in, w_pair):
    shapes = [shape(len(piece), 32, 640) for piece in PIECES]
    return pl.pallas_call(
        spread_kernel,
        out_shape=shapes,
        in_specs=[SMEM] + [VMEM] * 4,
        out_specs=[VMEM] * 5,
        scratch_shapes=[pltpu.VMEM((16, 32, 640), jnp.bfloat16)],
        compiler_params=PARAMS,
        cost_estimate=pl.CostEstimate(flops=2 * 256 * 640 * 2304, bytes_accessed=6000000, transcendentals=0),
    )(places(PIECES), mine, pre, w_in, w_pair)


def summed_along_z(own, right, left, right2, left2):
    right, left, right2, left2 = along_z(right, 1), along_z(left, -1), along_z(right2, 2), along_z(left2, -2)
    f = lambda v: v.astype(jnp.float32)
    near = f(own) + f(right) + f(left)
    low = (near[0] + f(left2[0])).astype(jnp.bfloat16)
    high = (near[2] + f(right2[1])).astype(jnp.bfloat16)
    apart = near[3].astype(jnp.bfloat16)
    low, high, apart = along_z(low, -4), along_z(high, 4), along_z(apart, 8)
    mine = near[1] + f(right2[0]) + f(left2[1])
    return (mine + f(low) + f(high) + f(apart)).astype(jnp.bfloat16)


def swap_pair(array):
    return lax.ppermute(array, "yl", SWAP)


def shards(x_rotated, block_scales, grad_act, w_in):
    side, core = lax.axis_index("yl"), lax.axis_index("c")
    w_pair = swap_pair(w_in)
    own = decode(x_rotated, block_scales)
    rows = lax.all_gather(own, "z", axis=0, tiled=True).reshape(8, 2, 32, 640)
    at = jnp.reshape(core, (1,)).astype(jnp.int32)
    flops = 2 * 256 * 640 * 2304
    (far,) = call(far_kernel, [shape(256, 2304)], 3, flops, 6000000)(at, rows, w_in, w_pair)
    far = swap_cores(far)
    (near,) = call(near_kernel, [shape(8, 32, 2304)], 4, flops, 6000000)(at, rows, w_in, w_pair, far)
    parts = exchange(near)
    grads = grad_act.reshape(2, 32, 1152)
    lent = lax.dynamic_index_in_dim(grads, 1 - side, 0, keepdims=False)
    kept = lax.dynamic_index_in_dim(grads, side, 0, keepdims=False)
    grads = jnp.concatenate([kept, swap_pair(lent)], axis=1)
    pre = jnp.sum(parts.astype(jnp.float32), axis=0)
    mine = exchange(copies(slope_grad(pre, grads))).reshape(256, 2304)
    other = swap_cores(mine)
    (part,) = call(part_kernel, [shape(8, 32, 640)], 3, flops, 6000000)(at, mine, w_in, w_pair)
    pieces = spread(part, other, w_in, w_pair)
    rows_mine = lax.dynamic_index_in_dim(rows, core, 1, keepdims=False).reshape(256, 640)
    rows_other = lax.dynamic_index_in_dim(rows, 1 - core, 1, keepdims=False).reshape(256, 640)
    tn = ((0,), (0,))
    lent = dot(rows_mine, mine[:, 1152:], tn) + dot(rows_other, other[:, 1152:], tn)
    lent = swap_pair(lent.astype(jnp.bfloat16))
    kept = dot(rows_mine, mine[:, :1152], tn) + dot(rows_other, other[:, :1152], tn)
    grad_weight = (kept + lent.astype(jnp.float32)).astype(jnp.bfloat16)
    return summed_along_z(*pieces), grad_weight


def solution(mesh):
    fine = Mesh(mesh.devices.reshape(SIZES), AXES)
    in_specs = (P(TENSOR, DP), P(TENSOR, DP), P(DP, TENSOR), P(DP, TENSOR))
    out_specs = (P(TENSOR, DP), P(DP, TENSOR))
    return jax.shard_map(shards, mesh=fine, in_specs=in_specs, out_specs=out_specs, check_vma=False)
```

time: 192 us -> 158 us (0.82)
  blocking collectives: 0 us -> 62 us
  starting transfers between devices: 108 us -> 51.3 us
  waiting for transfers between devices: 58 us -> 18.7 us
  Pallas kernels: 1.91 us -> 7.66 us
  matrix products: 14 us -> 8.31 us
    ppermute x17 -> x10, starting transfers between devices: 81.3 us -> 40.2 us  [the longest x7 32.5 us: along_z(): return lax.ppermute(array, 'z', [(z, (z + step) % 16) for z in range(16)])]
    all_gather x0 -> x1, blocking collectives: none -> 39.4 us  [shards(): rows = lax.all_gather(own, 'z', axis=0, tiled=True).reshape(8, 2, 32, 640)]
    ppermute x17 -> x10, waiting for transfers between devices: 32 us -> 1.49 us  [the longest x7 1.49 us: along_z(): return lax.ppermute(array, 'z', [(z, (z + step) % 16) for z in range(16)])]
    all_to_all x0 -> x1, blocking collectives: none -> 22.6 us  [exchange(): return lax.all_to_all(blocks, ('yh', 'x'), 0, 0, tiled=True)]
    all_to_all x3 -> x1, starting transfers between devices: 19.2 us -> 7.24 us  [exchange(): return lax.all_to_all(blocks, ('yh', 'x'), 0, 0, tiled=True)]
    all_to_all x3 -> x1, waiting for transfers between devices: 21.9 us -> 14.4 us  [exchange(): return lax.all_to_all(blocks, ('yh', 'x'), 0, 0, tiled=True)]
    pallas_call x2 -> x4, Pallas kernels: 1.91 us -> 7.66 us  [the longest x1 2.58 us: spread(): pl.pallas_call(spread_kernel, out_shape=shapes, in_specs=[SMEM] + [VMEM]...]
    dot_general x7 -> x4, matrix products: 13.7 us -> 8.01 us  [dot(): lax.dot_general(a, b, (dims, ((), ())), preferred_element_type=jnp.float32)]
  transfers between devices with their start and end apart: 24 -> 13, of which waited for: 9 -> 3; matrix products, arithmetic and copies ran while one was open for 6% -> 6% of each run, Pallas kernels for 0% -> 3%
where the time goes in v3:
time: 158 us; the launch traced here: 155 us
  blocking collectives  62 us (39%)
  starting transfers between devices  51.3 us (32%)
  waiting for transfers between devices  18.7 us (12%)
  matrix products  8.31 us (5%)
  Pallas kernels  7.66 us (5%)
  local copies, waits for them, and re-layouts  3.88 us (2%)
  other arithmetic  2.44 us (2%)
    all_gather x1, blocking collectives, shards(): rows = lax.all_gather(own, 'z', axis=0, tiled=True).reshape(8, 2, 32, 640)  39.4 us
    ppermute x7, starting transfers between devices, along_z(): return lax.ppermute(array, 'z', [(z, (z + step) % 16) for z in range(16)])  32.5 us
    all_to_all x1, blocking collectives, exchange(): return lax.all_to_all(blocks, ('yh', 'x'), 0, 0, tiled=True)  22.6 us
    all_to_all x1, waiting for transfers between devices, exchange(): return lax.all_to_all(blocks, ('yh', 'x'), 0, 0, tiled=True)  14.4 us
    dot_general x4, matrix products, dot(): lax.dot_general(a, b, (dims, ((), ())), preferred_element_type=jnp.float32)  8.01 us
    ppermute x3, starting transfers between devices, swap_pair(): return lax.ppermute(array, 'yl', SWAP)  7.71 us
    all_to_all x1, starting transfers between devices, exchange(): return lax.all_to_all(blocks, ('yh', 'x'), 0, 0, tiled=True)  7.24 us
    ppermute x2, starting transfers between devices, swap_cores(): return lax.ppermute(array, 'c', SWAP)  3.83 us
  transfers between devices with their start and end apart: 13, of which 3 were waited for; matrix products, arithmetic and copies ran while one was open for 6% of the time, Pallas kernels for 3%

profile of v3, /device:TPU:6, one launch (start us, length us, event | category | flops | bytes accessed | tf_op | source)
XLA Modules:
  0.0 155.3 jit_solution(9156914060251449706)
XLA Ops:
  0.6 3.6 %collective-permute-start.1 = (bf16[640,1152]{1,0:T(8,128)(2,1)}, bf16[640,1152]{1,0:T(8,128)(2,1)S(1)}, u32[]{:S(2)}, u32[]{:S(2)}) collective-permute-start(bf16[640,1152]{1,0:T(8,128)(2,1)} %w_ref.7), channel_id=1, source_target_pairs={{0,1},{1,0},{2,3},{3,2},{4,5},{5,4},{6,7},{7,6},{8,9},{9,8},{10,11... | collective-permute-start | bytes 4423688 | tf_op jit(solution)/shard_map/ppermute | solution.py:157
  6.3 39.4 %all_gather.3 = bf16[512,640]{1,0:T(8,128)(2,1)S(1)} all-gather(bf16[32,640]{1,0:T(8,128)(2,1)S(1)} %bitcast.45), channel_id=1, replica_groups=mesh['yh'=2,'x'=4,'c'=2,'z'=16,'yl'=2] {'z'}, dimensions={0}, use_global_device_ids=true | all-gather | bytes 696320 | tf_op jit(solution)/shard_map/all_gather | solution.py:164
  47.0 1.9 %collective-permute-start.2 = (bf16[256,2304]{1,0:T(8,128)(2,1)S(1)}, bf16[256,2304]{1,0:T(8,128)(2,1)S(1)}, u32[]{:S(2)}, u32[]{:S(2)}) collective-permute-start(bf16[256,2304]{1,0:T(8,128)(2,1)S(1)} %shard_map.68), channel_id=1, source_target_pairs={{0,32},{32,0},{1,33},{33,1},{2,34},{34,2},{3,35},{35,3},{4,36},{36... | collective-permute-start | bytes 3538952 | tf_op jit(solution)/shard_map/ppermute | solution.py:58
  48.9 2.8 %collective-permute-done.2.far_ref = bf16[256,2304]{1,0:T(8,128)(2,1)S(1)} collective-permute-done((bf16[256,2304]{1,0:T(8,128)(2,1)S(1)}, bf16[256,2304]{1,0:T(8,128)(2,1)S(1)}, u32[]{:S(2)}, u32[]{:S(2)}) %collective-permute-start.2) | collective-permute-done | bytes 1179680 | tf_op jit(solution)/shard_map/ppermute | solution.py:58
  54.1 7.2 %all-to-all-start = ((bf16[8,32,2304]{2,1,0:T(8,128)(2,1)}), bf16[8,32,2304]{2,1,0:T(8,128)(2,1)}, u32[]{:S(2)}, u32[]{:S(2)}) async-start(bf16[8,32,2304]{2,1,0:T(8,128)(2,1)} %copy-done.2), calls=%async_computation | async-start | bytes 2359296 | tf_op jit(solution)/shard_map/all_to_all | solution.py:62
  61.3 2.0 %collective-permute-start = (bf16[32,1152]{1,0:T(8,128)(2,1)S(1)}, bf16[32,1152]{1,0:T(8,128)(2,1)S(1)}, u32[]{:S(2)}, u32[]{:S(2)}) collective-permute-start(bf16[32,1152]{1,0:T(8,128)(2,1)S(1)} %get-tuple-element.17), channel_id=1, source_target_pairs={{0,1},{1,0},{2,3},{3,2},{4,5},{5,4},{6,7},{7,6},{8,9},{9,8},{10,11... | collective-permute-start | bytes 221192 | tf_op jit(solution)/shard_map/ppermute | solution.py:157
  63.4 14.4 %all-to-all-done = bf16[8,32,2304]{2,1,0:T(8,128)(2,1)} async-done(((bf16[8,32,2304]{2,1,0:T(8,128)(2,1)}), bf16[8,32,2304]{2,1,0:T(8,128)(2,1)}, u32[]{:S(2)}, u32[]{:S(2)}) %all-to-all-start) | async-done | bytes 1179680 | tf_op jit(solution)/shard_map/all_to_all | solution.py:62
  79.5 22.6 %all_to_all.10 = bf16[8,32,2304]{2,1,0:T(8,128)(2,1)} all-to-all(bf16[8,32,2304]{2,1,0:T(8,128)(2,1)S(1)} %broadcast_in_dim.2), channel_id=1, replica_groups=mesh['yh'=2,'x'=4,'c'=2,'z'=16,'yl'=2] {'yh','x'}, dimensions={0} | all-to-all | bytes 2359296 | tf_op jit(solution)/shard_map/all_to_all | solution.py:62
  102.1 1.9 %collective-permute-start.3 = (bf16[256,2304]{1,0:T(8,128)(2,1)}, bf16[256,2304]{1,0:T(8,128)(2,1)}, u32[]{:S(2)}, u32[]{:S(2)}) collective-permute-start(bf16[256,2304]{1,0:T(8,128)(2,1)} %bitcast.6.pre_ref), channel_id=1, source_target_pairs={{0,32},{32,0},{1,33},{33,1},{2,34},{34,2},{3,35},{35,3},{4,36},{36... | collective-permute-start | bytes 3538952 | tf_op jit(solution)/shard_map/ppermute | solution.py:58
  105.2 2.5 %shard_map.70.mine_ref = bf16[8,32,640]{2,1,0:T(8,128)(2,1)S(1)} custom-call(s32[1]{0:T(128)} %bitcast.core_ref, bf16[256,2304]{1,0:T(8,128)(2,1)} %bitcast.6.pre_ref, bf16[640,1152]{1,0:T(8,128)(2,1)S(1)} %copy-done, bf16[640,1152]{1,0:T(8,128)(2,1)S(1)} %collective-permute-done.1.v_ref), custom_call_target="tpu_custom_call" | custom-call | flops 754974720 | bytes 6000000 | tf_op jit(solution)/shard_map/pallas_call | solution.py:178
  107.7 1.7 %fusion.5 = f32[640,1152]{1,0:T(8,128)S(1)} fusion(bf16[256,640]{1,0:T(8,128)(2,1)S(1)} %bitcast.43, bf16[256,2304]{1,0:T(8,128)(2,1)} %bitcast.6.pre_ref), kind=kOutput, calls=%fused_computation.9 | convolution fusion | flops 377487360 | bytes 3866624 | tf_op jit(solution)/shard_map/dot_general | solution.py:50
  109.4 1.7 %fusion.1 = bf16[640,1152]{1,0:T(8,128)(2,1)S(1)} fusion(f32[640,1152]{1,0:T(8,128)S(1)} %fusion.5, bf16[256,640]{1,0:T(8,128)(2,1)S(1)} %bitcast.41, bf16[256,2304]{1,0:T(8,128)(2,1)} %collective-permute-done.3.pre_ref), kind=kOutput, calls=%fused_computation.3 | convolution fusion | flops 378961920 | bytes 5341184 | tf_op jit(solution)/shard_map/dot_general | solution.py:50
  111.2 2.0 %collective-permute-start.11 = (bf16[640,1152]{1,0:T(8,128)(2,1)S(1)}, bf16[640,1152]{1,0:T(8,128)(2,1)S(1)}, u32[]{:S(2)}, u32[]{:S(2)}) collective-permute-start(bf16[640,1152]{1,0:T(8,128)(2,1)S(1)} %fusion.1), channel_id=1, source_target_pairs={{0,1},{1,0},{2,3},{3,2},{4,5},{5,4},{6,7},{7,6},{8,9},{9,8},{10,11... | collective-permute-start | bytes 4423688 | tf_op jit(solution)/shard_map/ppermute | solution.py:157
  113.2 2.6 %shard_map.71 = (bf16[4,32,640]{2,1,0:T(8,128)(2,1)S(1)}, bf16[4,32,640]{2,1,0:T(8,128)(2,1)S(1)}, bf16[4,32,640]{2,1,0:T(8,128)(2,1)S(1)}, bf16[2,32,640]{2,1,0:T(8,128)(2,1)S(1)}, bf16[2,32,640]{2,1,0:T(8,128)(2,1)S(1)}) custom-call(s32[16]{0:T(128)S(1)} %fusion.50.place_ref, bf16[8,32,640]{2,1,0:T(8,128)(2,1)S(1)} %shard_map.70.mine_ref, ...), custom_call_target="tpu_custom_call" | custom-call | flops 754974720 | bytes 6000000 | tf_op jit(solution)/shard_map/pallas_call | solution.py:133
  115.8 1.9 %collective-permute-start.4 = (bf16[4,32,640]{2,1,0:T(8,128)(2,1)S(1)}, bf16[4,32,640]{2,1,0:T(8,128)(2,1)S(1)}, u32[]{:S(2)}, u32[]{:S(2)}) collective-permute-start(bf16[4,32,640]{2,1,0:T(8,128)(2,1)S(1)} %get-tuple-element.8), channel_id=1, source_target_pairs={{0,2},{2,4},{4,6},{6,8},{8,10},{10,12},{12,14},{14,16},{16,18},{18... | collective-permute-start | bytes 491528 | tf_op jit(solution)/shard_map/ppermute | solution.py:54
  117.7 5.1 %collective-permute-start.5 = (bf16[4,32,640]{2,1,0:T(8,128)(2,1)S(1)}, bf16[4,32,640]{2,1,0:T(8,128)(2,1)S(1)}, u32[]{:S(2)}, u32[]{:S(2)}) collective-permute-start(bf16[4,32,640]{2,1,0:T(8,128)(2,1)S(1)} %get-tuple-element.9), channel_id=1, source_target_pairs={{0,30},{2,0},{4,2},{6,4},{8,6},{10,8},{12,10},{14,12},{16,14},{18,... | collective-permute-start | bytes 491528 | tf_op jit(solution)/shard_map/ppermute | solution.py:54
  122.9 1.9 %collective-permute-start.6 = (bf16[2,32,640]{2,1,0:T(8,128)(2,1)S(1)}, bf16[2,32,640]{2,1,0:T(8,128)(2,1)S(1)}, u32[]{:S(2)}, u32[]{:S(2)}) collective-permute-start(bf16[2,32,640]{2,1,0:T(8,128)(2,1)S(1)} %get-tuple-element.10), channel_id=1, source_target_pairs={{0,4},{2,6},{4,8},{6,10},{8,12},{10,14},{12,16},{14,18},{16,20},{1... | collective-permute-start | bytes 245768 | tf_op jit(solution)/shard_map/ppermute | solution.py:54
  124.8 6.0 %collective-permute-start.7 = (bf16[2,32,640]{2,1,0:T(8,128)(2,1)S(1)}, bf16[2,32,640]{2,1,0:T(8,128)(2,1)S(1)}, u32[]{:S(2)}, u32[]{:S(2)}) collective-permute-start(bf16[2,32,640]{2,1,0:T(8,128)(2,1)S(1)} %get-tuple-element.11), channel_id=1, source_target_pairs={{0,28},{2,30},{4,0},{6,2},{8,4},{10,6},{12,8},{14,10},{16,12},{18,... | collective-permute-start | bytes 245768 | tf_op jit(solution)/shard_map/ppermute | solution.py:54
  131.0 7.8 %collective-permute-start.10 = (bf16[32,640]{1,0:T(8,128)(2,1)S(1)}, bf16[32,640]{1,0:T(8,128)(2,1)S(1)}, u32[]{:S(2)}, u32[]{:S(2)}) collective-permute-start(bf16[32,640]{1,0:T(8,128)(2,1)S(1)} %fusion.37), channel_id=1, source_target_pairs={{0,16},{2,18},{4,20},{6,22},{8,24},{10,26},{12,28},{14,30},{16,0},... | collective-permute-start | bytes 122888 | tf_op jit(solution)/shard_map/ppermute | solution.py:54
  138.8 2.7 %collective-permute-start.8 = (bf16[32,640]{1,0:T(8,128)(2,1)S(1)}, bf16[32,640]{1,0:T(8,128)(2,1)S(1)}, u32[]{:S(2)}, u32[]{:S(2)}) collective-permute-start(bf16[32,640]{1,0:T(8,128)(2,1)S(1)} %get-tuple-element.14), channel_id=1, source_target_pairs={{0,24},{2,26},{4,28},{6,30},{8,0},{10,2},{12,4},{14,6},{16,8},{18,... | collective-permute-start | bytes 122888 | tf_op jit(solution)/shard_map/ppermute | solution.py:54
  141.5 7.0 %collective-permute-start.9 = (bf16[32,640]{1,0:T(8,128)(2,1)S(1)}, bf16[32,640]{1,0:T(8,128)(2,1)S(1)}, u32[]{:S(2)}, u32[]{:S(2)}) collective-permute-start(bf16[32,640]{1,0:T(8,128)(2,1)S(1)} %get-tuple-element.15), channel_id=1, source_target_pairs={{0,8},{2,10},{4,12},{6,14},{8,16},{10,18},{12,20},{14,22},{16,24},... | collective-permute-start | bytes 122888 | tf_op jit(solution)/shard_map/ppermute | solution.py:54
  148.5 1.7 %fusion.8 = f32[640,1152]{1,0:T(8,128)S(1)} fusion(bf16[256,640]{1,0:T(8,128)(2,1)S(1)} %bitcast.44, bf16[256,2304]{1,0:T(8,128)(2,1)} %bitcast.6.pre_ref), kind=kOutput, calls=%fused_computation.12 | convolution fusion | flops 377487360 | bytes 3866624 | tf_op jit(solution)/shard_map/dot_general | solution.py:50
  150.3 1.5 collective-permute-done.9
  152.4 2.9 %fusion.2 = bf16[640,1152]{1,0:T(8,128)(2,1)} fusion(f32[640,1152]{1,0:T(8,128)S(1)} %fusion.8, bf16[256,640]{1,0:T(8,128)(2,1)S(1)} %bitcast.42, bf16[640,1152]{1,0:T(8,128)(2,1)S(1)} %collective-permute-done.11, bf16[256,2304]{1,0:T(8,128)(2,1)} %collective-permute-done.3.pre_ref), kind=kOutput, calls=%fused_computation.4 | convolution fusion | flops 380436480 | bytes 6815744 | tf_op jit(solution)/shard_map/dot_general | solution.py:50
  (37 shorter events, 9.2 us)
Async XLA Ops:
  0.6 45.1 %copy-start = (bf16[640,1152]{1,0:T(8,128)(2,1)S(1)}, bf16[640,1152]{1,0:T(8,128)(2,1)}, u32[]{:S(2)}) copy-start(bf16[640,1152]{1,0:T(8,128)(2,1)} %w_ref.7) | copy-start | bytes 4423684
  0.6 45.1 %collective-permute-start.1 = (bf16[640,1152]{1,0:T(8,128)(2,1)}, bf16[640,1152]{1,0:T(8,128)(2,1)S(1)}, u32[]{:S(2)}, u32[]{:S(2)}) collective-permute-start(bf16[640,1152]{1,0:T(8,128)(2,1)} %w_ref.7), channel_id=1, source_target_pairs={{0,1},{1,0},{2,3},{3,2},{4,5},{5,4},{6,7},{7,6},{8,9},{9,8},{10,11... | collective-permute-start | bytes 4423688 | tf_op jit(solution)/shard_map/ppermute | solution.py:157
  45.7 6.1 %copy-start.1 = (bf16[512,640]{1,0:T(8,128)(2,1)}, bf16[512,640]{1,0:T(8,128)(2,1)S(1)}, u32[]{:S(2)}) copy-start(bf16[512,640]{1,0:T(8,128)(2,1)S(1)} %all_gather.3) | copy-start | bytes 1966084
  47.0 4.7 %collective-permute-start.2 = (bf16[256,2304]{1,0:T(8,128)(2,1)S(1)}, bf16[256,2304]{1,0:T(8,128)(2,1)S(1)}, u32[]{:S(2)}, u32[]{:S(2)}) collective-permute-start(bf16[256,2304]{1,0:T(8,128)(2,1)S(1)} %shard_map.68), channel_id=1, source_target_pairs={{0,32},{32,0},{1,33},{33,1},{2,34},{34,2},{3,35},{35,3},{4,36},{36... | collective-permute-start | bytes 3538952 | tf_op jit(solution)/shard_map/ppermute | solution.py:58
  53.0 1.0 copy-start.2
  54.1 7.2 %copy-start.3 = (bf16[64,1152]{1,0:T(8,128)(2,1)S(1)}, bf16[64,1152]{1,0:T(8,128)(2,1)}, u32[]{:S(2)}) copy-start(bf16[64,1152]{1,0:T(8,128)(2,1)} %param.7) | copy-start | bytes 442372
  54.1 23.7 %all-to-all-start = ((bf16[8,32,2304]{2,1,0:T(8,128)(2,1)}), bf16[8,32,2304]{2,1,0:T(8,128)(2,1)}, u32[]{:S(2)}, u32[]{:S(2)}) async-start(bf16[8,32,2304]{2,1,0:T(8,128)(2,1)} %copy-done.2), calls=%async_computation | async-start | bytes 2359296 | tf_op jit(solution)/shard_map/all_to_all | solution.py:62
  61.3 17.9 %collective-permute-start = (bf16[32,1152]{1,0:T(8,128)(2,1)S(1)}, bf16[32,1152]{1,0:T(8,128)(2,1)S(1)}, u32[]{:S(2)}, u32[]{:S(2)}) collective-permute-start(bf16[32,1152]{1,0:T(8,128)(2,1)S(1)} %get-tuple-element.17), channel_id=1, source_target_pairs={{0,1},{1,0},{2,3},{3,2},{4,5},{5,4},{6,7},{7,6},{8,9},{9,8},{10,11... | collective-permute-start | bytes 221192 | tf_op jit(solution)/shard_map/ppermute | solution.py:157
  79.5 25.7 %copy-start.4 = (s32[16]{0:T(128)S(1)}, s32[16]{0:T(128)}, u32[]{:S(2)}) copy-start(s32[16]{0:T(128)} %constant.94.clone) | copy-start | bytes 196
  102.1 7.3 %collective-permute-start.3 = (bf16[256,2304]{1,0:T(8,128)(2,1)}, bf16[256,2304]{1,0:T(8,128)(2,1)}, u32[]{:S(2)}, u32[]{:S(2)}) collective-permute-start(bf16[256,2304]{1,0:T(8,128)(2,1)} %bitcast.6.pre_ref), channel_id=1, source_target_pairs={{0,32},{32,0},{1,33},{33,1},{2,34},{34,2},{3,35},{35,3},{4,36},{36... | collective-permute-start | bytes 3538952 | tf_op jit(solution)/shard_map/ppermute | solution.py:58
  111.2 41.2 %collective-permute-start.11 = (bf16[640,1152]{1,0:T(8,128)(2,1)S(1)}, bf16[640,1152]{1,0:T(8,128)(2,1)S(1)}, u32[]{:S(2)}, u32[]{:S(2)}) collective-permute-start(bf16[640,1152]{1,0:T(8,128)(2,1)S(1)} %fusion.1), channel_id=1, source_target_pairs={{0,1},{1,0},{2,3},{3,2},{4,5},{5,4},{6,7},{7,6},{8,9},{9,8},{10,11... | collective-permute-start | bytes 4423688 | tf_op jit(solution)/shard_map/ppermute | solution.py:157
  115.8 15.1 %collective-permute-start.4 = (bf16[4,32,640]{2,1,0:T(8,128)(2,1)S(1)}, bf16[4,32,640]{2,1,0:T(8,128)(2,1)S(1)}, u32[]{:S(2)}, u32[]{:S(2)}) collective-permute-start(bf16[4,32,640]{2,1,0:T(8,128)(2,1)S(1)} %get-tuple-element.8), channel_id=1, source_target_pairs={{0,2},{2,4},{4,6},{6,8},{8,10},{10,12},{12,14},{14,16},{16,18},{18... | collective-permute-start | bytes 491528 | tf_op jit(solution)/shard_map/ppermute | solution.py:54
  117.7 13.1 %collective-permute-start.5 = (bf16[4,32,640]{2,1,0:T(8,128)(2,1)S(1)}, bf16[4,32,640]{2,1,0:T(8,128)(2,1)S(1)}, u32[]{:S(2)}, u32[]{:S(2)}) collective-permute-start(bf16[4,32,640]{2,1,0:T(8,128)(2,1)S(1)} %get-tuple-element.9), channel_id=1, source_target_pairs={{0,30},{2,0},{4,2},{6,4},{8,6},{10,8},{12,10},{14,12},{16,14},{18,... | collective-permute-start | bytes 491528 | tf_op jit(solution)/shard_map/ppermute | solution.py:54
  122.9 15.8 %collective-permute-start.6 = (bf16[2,32,640]{2,1,0:T(8,128)(2,1)S(1)}, bf16[2,32,640]{2,1,0:T(8,128)(2,1)S(1)}, u32[]{:S(2)}, u32[]{:S(2)}) collective-permute-start(bf16[2,32,640]{2,1,0:T(8,128)(2,1)S(1)} %get-tuple-element.10), channel_id=1, source_target_pairs={{0,4},{2,6},{4,8},{6,10},{8,12},{10,14},{12,16},{14,18},{16,20},{1... | collective-permute-start | bytes 245768 | tf_op jit(solution)/shard_map/ppermute | solution.py:54
  124.8 13.9 %collective-permute-start.7 = (bf16[2,32,640]{2,1,0:T(8,128)(2,1)S(1)}, bf16[2,32,640]{2,1,0:T(8,128)(2,1)S(1)}, u32[]{:S(2)}, u32[]{:S(2)}) collective-permute-start(bf16[2,32,640]{2,1,0:T(8,128)(2,1)S(1)} %get-tuple-element.11), channel_id=1, source_target_pairs={{0,28},{2,30},{4,0},{6,2},{8,4},{10,6},{12,8},{14,10},{16,12},{18,... | collective-permute-start | bytes 245768 | tf_op jit(solution)/shard_map/ppermute | solution.py:54
  131.0 19.3 %collective-permute-start.10 = (bf16[32,640]{1,0:T(8,128)(2,1)S(1)}, bf16[32,640]{1,0:T(8,128)(2,1)S(1)}, u32[]{:S(2)}, u32[]{:S(2)}) collective-permute-start(bf16[32,640]{1,0:T(8,128)(2,1)S(1)} %fusion.37), channel_id=1, source_target_pairs={{0,16},{2,18},{4,20},{6,22},{8,24},{10,26},{12,28},{14,30},{16,0},... | collective-permute-start | bytes 122888 | tf_op jit(solution)/shard_map/ppermute | solution.py:54
  138.8 11.5 %collective-permute-start.8 = (bf16[32,640]{1,0:T(8,128)(2,1)S(1)}, bf16[32,640]{1,0:T(8,128)(2,1)S(1)}, u32[]{:S(2)}, u32[]{:S(2)}) collective-permute-start(bf16[32,640]{1,0:T(8,128)(2,1)S(1)} %get-tuple-element.14), channel_id=1, source_target_pairs={{0,24},{2,26},{4,28},{6,30},{8,0},{10,2},{12,4},{14,6},{16,8},{18,... | collective-permute-start | bytes 122888 | tf_op jit(solution)/shard_map/ppermute | solution.py:54
  141.5 10.2 %collective-permute-start.9 = (bf16[32,640]{1,0:T(8,128)(2,1)S(1)}, bf16[32,640]{1,0:T(8,128)(2,1)S(1)}, u32[]{:S(2)}, u32[]{:S(2)}) collective-permute-start(bf16[32,640]{1,0:T(8,128)(2,1)S(1)} %get-tuple-element.15), channel_id=1, source_target_pairs={{0,8},{2,10},{4,12},{6,14},{8,16},{10,18},{12,20},{14,22},{16,24},... | collective-permute-start | bytes 122888 | tf_op jit(solution)/shard_map/ppermute | solution.py:54

commit v4 on v3

v4 whole, which is shorter than its diff:
```python
import math

import jax
import jax.numpy as jnp
from jax import lax
from jax.experimental import pallas as pl
from jax.experimental.pallas import tpu as pltpu
from jax.sharding import Mesh
from jax.sharding import PartitionSpec as P

AXES = ("yh", "x", "c", "za", "zl", "yl")
SIZES = (2, 4, 2, 4, 4, 2)
DP = ("yh", "x", "c")
TENSOR = ("za", "zl", "yl")
SWAP = [(0, 1), (1, 0)]
VMEM = pl.BlockSpec(memory_space=pltpu.VMEM)
SMEM = pl.BlockSpec(memory_space=pltpu.SMEM)
ANY = pl.BlockSpec(memory_space=pl.ANY)
PARAMS = pltpu.CompilerParams(vmem_limit_bytes=16 * 1024 * 1024)


def hadamard_table():
    index = lax.iota(jnp.int32, 128)
    common = jnp.bitwise_and(index[:, None], index[None, :])
    parity = jnp.zeros((128, 128), jnp.int32)
    for shift in range(7):
        parity = parity + jnp.bitwise_and(jnp.right_shift(common, shift), 1)
    signs = 1.0 - 2.0 * (parity % 2).astype(jnp.float32)
    return signs / math.sqrt(128.0)


def decode(coded, scales):
    count = coded.shape[0]
    blocks = coded.astype(jnp.float32).reshape(count, scales.shape[1], 128) * scales[:, :, None]
    turned = jnp.einsum("rbk,kj->rbj", blocks, hadamard_table(), precision=lax.Precision.HIGHEST)
    return turned.reshape(count, coded.shape[1]).astype(jnp.bfloat16)


def gelu_slope(value):
    cdf = 0.5 * (1.0 + jax.scipy.special.erf(value / math.sqrt(2.0)))
    pdf = jnp.exp(-0.5 * value * value) / math.sqrt(2.0 * math.pi)
    return cdf + value * pdf


def slope_grad(pre, grads):
    return (grads.astype(jnp.float32) * gelu_slope(pre)).astype(jnp.bfloat16)


def dot(a, b, dims):
    return lax.dot_general(a, b, (dims, ((), ())), preferred_element_type=jnp.float32)


def along_z(array, step):
    return lax.ppermute(array, ("za", "zl"), [(z, (z + step) % 16) for z in range(16)])


def swap_cores(array):
    return lax.ppermute(array, "c", SWAP)


def exchange(blocks):
    return lax.all_to_all(blocks, ("yh", "x"), 0, 0, tiled=True)


def copies(grad):
    return jnp.broadcast_to(grad[None], (8,) + grad.shape)


def call(kernel, out_shape, count, flops, moved, after=0):
    return pl.pallas_call(
        kernel,
        out_shape=out_shape,
        in_specs=[SMEM] + [VMEM] * count + [ANY] * after,
        out_specs=[VMEM] * len(out_shape),
        compiler_params=PARAMS,
        cost_estimate=pl.CostEstimate(flops=flops, bytes_accessed=moved, transcendentals=0),
    )


def shape(*dims):
    return jax.ShapeDtypeStruct(dims, jnp.bfloat16)


def far_kernel(core_ref, rows_ref, w_ref, v_ref, far_ref):
    rows = rows_ref[:, 1 - core_ref[0]].reshape(256, 640)
    for i, weight in enumerate((w_ref, v_ref)):
        for j in range(0, 1152, 384):
            far_ref[:, 1152 * i + j : 1152 * i + j + 384] = jnp.dot(
                rows, weight[:, j : j + 384], preferred_element_type=jnp.float32
            ).astype(jnp.bfloat16)


def near_kernel(core_ref, rows_ref, w_ref, v_ref, near_ref):
    rows = rows_ref[:, core_ref[0]].reshape(256, 640)
    for i, weight in enumerate((w_ref, v_ref)):
        for j in range(0, 1152, 384):
            near_ref[:, 1152 * i + j : 1152 * i + j + 384] = jnp.dot(
                rows, weight[:, j : j + 384], preferred_element_type=jnp.float32
            ).astype(jnp.bfloat16)


def input_part(pre_ref, w_ref, v_ref):
    nt = (((1,), (1,)), ((), ()))
    part = lax.dot_general(pre_ref[:, :1152], w_ref[...], nt, preferred_element_type=jnp.float32)
    part += lax.dot_general(pre_ref[:, 1152:], v_ref[...], nt, preferred_element_type=jnp.float32)
    return part.astype(jnp.bfloat16).reshape(8, 32, 640)


def part_kernel(core_ref, pre_ref, w_ref, v_ref, part_ref):
    part_ref[...] = input_part(pre_ref, w_ref, v_ref)


def weight_terms(core, rows_ref, mine_ref, other_ref, first):
    tn = (((0,), (0,)), ((), ()))
    left = [rows_ref[:, at].reshape(256, 640) for at in (core, 1 - core)]
    for j in range(0, 1152, 384):
        at = slice(first + j, first + j + 384)
        total = lax.dot_general(left[0], mine_ref[:, at], tn, preferred_element_type=jnp.float32)
        yield slice(j, j + 384), total + lax.dot_general(left[1], other_ref[:, at], tn, preferred_element_type=jnp.float32)


def spread_kernel(place_ref, rows_ref, part_ref, mine_ref, pre_ref, w_ref, v_ref, lent_ref, own_ref, right2_ref, left2_ref, right_ref, left_ref, all_ref):
    core, place = place_ref[0], place_ref[1]
    for at, total in weight_terms(core, rows_ref, mine_ref, pre_ref, 1152):
        lent_ref[:, at] = total.astype(jnp.bfloat16)
    other = input_part(pre_ref, w_ref, v_ref)
    for low in range(2):
        for high in range(4):
            all_ref[2 * low + core, high] = part_ref[2 * high + low]
            all_ref[2 * low + 1 - core, high] = other[2 * high + low]
    own_ref[...] = all_ref[place]
    right_ref[...] = all_ref[lax.rem(place + 1, 4)]
    left_ref[...] = all_ref[lax.rem(place + 3, 4)]
    apart = lax.rem(place + 2, 4)
    right2_ref[...] = all_ref[apart, 0:2]
    left2_ref[...] = all_ref[apart, 2:4]


def spread(place, rows, part, mine, pre, w_in, w_pair):
    return pl.pallas_call(
        spread_kernel,
        out_shape=[shape(640, 1152)] + [shape(count, 32, 640) for count in (4, 2, 2, 4, 4)],
        in_specs=[SMEM] + [VMEM] * 6,
        out_specs=[VMEM] * 6,
        scratch_shapes=[pltpu.VMEM((4, 4, 32, 640), jnp.bfloat16)],
        compiler_params=PARAMS,
        cost_estimate=pl.CostEstimate(flops=4 * 256 * 640 * 2304, bytes_accessed=9000000, transcendentals=0),
    )(place, rows, part, mine, pre, w_in, w_pair)


def kept_kernel(core_ref, rows_ref, mine_ref, other_ref, out_ref):
    for at, total in weight_terms(core_ref[0], rows_ref, mine_ref, other_ref, 0):
        out_ref[:, at] = total.astype(jnp.bfloat16)


def summed_near(own, right2, left2, right, left):
    right2, left2, right, left = along_z(right2, 2), along_z(left2, -2), along_z(right, 1), along_z(left, -1)
    f = lambda v: v.astype(jnp.float32)
    return (f(own) + f(right) + f(left) + f(jnp.concatenate([right2, left2]))).astype(jnp.bfloat16)


def swap_pair(array):
    return lax.ppermute(array, "yl", SWAP)


def shards(x_rotated, block_scales, grad_act, w_in):
    side, core = lax.axis_index("yl"), lax.axis_index("c")
    w_pair = swap_pair(w_in)
    own = decode(x_rotated, block_scales)
    rows = lax.all_gather(own, ("za", "zl"), axis=0, tiled=True).reshape(8, 2, 32, 640)
    at = jnp.reshape(core, (1,)).astype(jnp.int32)
    flops = 2 * 256 * 640 * 2304
    (far,) = call(far_kernel, [shape(256, 2304)], 3, flops, 6000000)(at, rows, w_in, w_pair)
    grads = grad_act.reshape(2, 32, 1152)
    lent = lax.dynamic_index_in_dim(grads, 1 - side, 0, keepdims=False)
    kept = lax.dynamic_index_in_dim(grads, side, 0, keepdims=False)
    far, lent = swap_cores(far), swap_pair(lent)
    grads = jnp.concatenate([kept, lent], axis=1)
    (near,) = call(near_kernel, [shape(256, 2304)], 3, flops, 6000000)(at, rows, w_in, w_pair)
    near = (near.astype(jnp.float32) + far.astype(jnp.float32)).astype(jnp.bfloat16).reshape(8, 32, 2304)
    pre = jnp.sum(exchange(near).astype(jnp.float32), axis=0)
    mine = exchange(copies(slope_grad(pre, grads))).reshape(256, 2304)
    other = swap_cores(mine)
    (part,) = call(part_kernel, [shape(8, 32, 640)], 3, flops, 6000000)(at, mine, w_in, w_pair)
    place = jnp.stack([core, lax.axis_index("zl")]).astype(jnp.int32)
    lent, *pieces = spread(place, rows, part, mine, other, w_in, w_pair)
    lent = swap_pair(lent)
    near = summed_near(*pieces)
    blocks = lax.all_to_all(near, "za", 0, 0, tiled=True)
    (kept,) = call(kept_kernel, [shape(640, 1152)], 3, flops, 4000000)(at, rows, mine, other)
    grad_weight = (kept.astype(jnp.float32) + lent.astype(jnp.float32)).astype(jnp.bfloat16)
    blocks, grad_weight = lax.optimization_barrier((blocks, grad_weight))
    return jnp.sum(blocks.astype(jnp.float32), axis=0).astype(jnp.bfloat16), grad_weight


def solution(mesh):
    fine = Mesh(mesh.devices.reshape(SIZES), AXES)
    in_specs = (P(TENSOR, DP), P(TENSOR, DP), P(DP, TENSOR), P(DP, TENSOR))
    out_specs = (P(TENSOR, DP), P(DP, TENSOR))
    return jax.shard_map(shards, mesh=fine, in_specs=in_specs, out_specs=out_specs, check_vma=False)
```

time: 158 us -> 157 us (level)
  waiting for transfers between devices: 18.7 us -> 31.3 us
  starting transfers between devices: 51.3 us -> 40.9 us
  matrix products: 8.31 us -> 0.3 us
  Pallas kernels: 7.66 us -> 12 us
  other arithmetic: 2.44 us -> 5.91 us
  local copies, waits for them, and re-layouts: 3.88 us -> 1.72 us
    ppermute x7 -> x4, starting transfers between devices: 32.5 us -> 15 us  [along_z(): lax.ppermute(array, ('za', 'zl'), [(z, (z + step) % 16) for z in range(16)])]
    ppermute x3, waiting for transfers between devices: 0.01 us -> 8.56 us  [swap_pair(): return lax.ppermute(array, 'yl', SWAP)]
    dot_general x4 -> x0, matrix products: 8.01 us -> none  [dot(): lax.dot_general(a, b, (dims, ((), ())), preferred_element_type=jnp.float32)]
    all_to_all x0 -> x1, starting transfers between devices: none -> 7.13 us  [shards(): blocks = lax.all_to_all(near, 'za', 0, 0, tiled=True)]
    all_to_all x0 -> x1, waiting for transfers between devices: none -> 6.32 us  [shards(): blocks = lax.all_to_all(near, 'za', 0, 0, tiled=True)]
    pallas_call x2 -> x3, Pallas kernels: 3.87 us -> 8.11 us  [the longest x1 3.98 us: spread(): pl.pallas_call(spread_kernel, out_shape=[shape(640, 1152)] + [shape(count...]
    convert_element_type x2 -> x3, other arithmetic: 0.67 us -> 3.5 us  [the longest x1 1.46 us: shards(): (kept.astype(jnp.float32) + lent.astype(jnp.float32)).astype(jnp.bfloat16)]
  transfers between devices with their start and end apart: 13 -> 11, of which waited for: 3 -> 5; matrix products, arithmetic and copies ran while one was open for 6% -> 4% of each run, Pallas kernels for 3% -> 4%
where the time goes in v4:
time: 157 us; the launch traced here: 155 us
  blocking collectives  62 us (39%)
  starting transfers between devices  40.9 us (26%)
  waiting for transfers between devices  31.3 us (20%)
  Pallas kernels  12 us (8%)
  other arithmetic  5.91 us (4%)
  local copies, waits for them, and re-layouts  1.72 us (1%)
    all_gather x1, blocking collectives, shards(): lax.all_gather(own, ('za', 'zl'), axis=0, tiled=True).reshape(8, 2, 32, 640)  39.4 us
    all_to_all x1, blocking collectives, exchange(): return lax.all_to_all(blocks, ('yh', 'x'), 0, 0, tiled=True)  22.7 us
    ppermute x4, starting transfers between devices, along_z(): lax.ppermute(array, ('za', 'zl'), [(z, (z + step) % 16) for z in range(16)])  15 us
    all_to_all x1, waiting for transfers between devices, exchange(): return lax.all_to_all(blocks, ('yh', 'x'), 0, 0, tiled=True)  14.4 us
    ppermute x3, waiting for transfers between devices, swap_pair(): return lax.ppermute(array, 'yl', SWAP)  8.56 us
    ppermute x3, starting transfers between devices, swap_pair(): return lax.ppermute(array, 'yl', SWAP)  7.7 us
    all_to_all x1, starting transfers between devices, exchange(): return lax.all_to_all(blocks, ('yh', 'x'), 0, 0, tiled=True)  7.24 us
    all_to_all x1, starting transfers between devices, shards(): blocks = lax.all_to_all(near, 'za', 0, 0, tiled=True)  7.13 us
  transfers between devices with their start and end apart: 11, of which 5 were waited for; matrix products, arithmetic and copies ran while one was open for 4% of the time, Pallas kernels for 4%

profile of v4, /device:TPU:6, one launch (start us, length us, event | category | flops | bytes accessed | tf_op | source)
XLA Modules:
  0.0 155.0 jit_solution(10722157549059941524)
XLA Ops:
  0.6 3.6 %collective-permute-start.1 = (bf16[640,1152]{1,0:T(8,128)(2,1)}, bf16[640,1152]{1,0:T(8,128)(2,1)S(1)}, u32[]{:S(2)}, u32[]{:S(2)}) collective-permute-start(bf16[640,1152]{1,0:T(8,128)(2,1)} %w_ref.7), channel_id=1, source_target_pairs={{0,1},{1,0},{2,3},{3,2},{4,5},{5,4},{6,7},{7,6},{8,9},{9,8},{10,11... | collective-permute-start | bytes 4423688 | tf_op jit(solution)/shard_map/ppermute | solution.py:163
  6.3 39.4 %all_gather.3 = bf16[512,640]{1,0:T(8,128)(2,1)S(1)} all-gather(bf16[32,640]{1,0:T(8,128)(2,1)S(1)} %bitcast.23), channel_id=1, replica_groups=mesh['yh'=2,'x'=4,'c'=2,'za'=4,'zl'=4,'yl'=2] {'za','zl'}, dimensions={0}, use_global_device_ids=true | all-gather | bytes 696320 | tf_op jit(solution)/shard_map/all_gather | solution.py:170
  45.7 1.3 shard_map.60
  47.0 1.9 %collective-permute-start.2 = (bf16[256,2304]{1,0:T(8,128)(2,1)S(1)}, bf16[256,2304]{1,0:T(8,128)(2,1)S(1)}, u32[]{:S(2)}, u32[]{:S(2)}) collective-permute-start(bf16[256,2304]{1,0:T(8,128)(2,1)S(1)} %shard_map.60), channel_id=1, source_target_pairs={{0,32},{32,0},{1,33},{33,1},{2,34},{34,2},{3,35},{35,3},{4,36},{36... | collective-permute-start | bytes 3538952 | tf_op jit(solution)/shard_map/ppermute | solution.py:58
  50.2 1.5 collective-permute-done.2
  51.7 1.3 add_convert_fusion.1
  53.0 7.2 %all-to-all-start = ((bf16[8,32,2304]{2,1,0:T(8,128)(2,1)}), bf16[8,32,2304]{2,1,0:T(8,128)(2,1)}, u32[]{:S(2)}, u32[]{:S(2)}) async-start(bf16[8,32,2304]{2,1,0:T(8,128)(2,1)} %bitcast.22), calls=%async_computation | async-start | bytes 2359296 | tf_op jit(solution)/shard_map/all_to_all | solution.py:62
  60.3 2.0 %collective-permute-start = (bf16[32,1152]{1,0:T(8,128)(2,1)S(1)}, bf16[32,1152]{1,0:T(8,128)(2,1)S(1)}, u32[]{:S(2)}, u32[]{:S(2)}) collective-permute-start(bf16[32,1152]{1,0:T(8,128)(2,1)S(1)} %get-tuple-element.19), channel_id=1, source_target_pairs={{0,1},{1,0},{2,3},{3,2},{4,5},{5,4},{6,7},{7,6},{8,9},{9,8},{10,11... | collective-permute-start | bytes 221192 | tf_op jit(solution)/shard_map/ppermute | solution.py:163
  62.4 14.4 %all-to-all-done = bf16[8,32,2304]{2,1,0:T(8,128)(2,1)} async-done(((bf16[8,32,2304]{2,1,0:T(8,128)(2,1)}), bf16[8,32,2304]{2,1,0:T(8,128)(2,1)}, u32[]{:S(2)}, u32[]{:S(2)}) %all-to-all-start) | async-done | bytes 1179680 | tf_op jit(solution)/shard_map/all_to_all | solution.py:62
  76.7 1.5 convert_reduce_fusion
  78.4 22.7 %all_to_all.15 = bf16[8,32,2304]{2,1,0:T(8,128)(2,1)} all-to-all(bf16[8,32,2304]{2,1,0:T(8,128)(2,1)S(1)} %broadcast_in_dim.2), channel_id=1, replica_groups=mesh['yh'=2,'x'=4,'c'=2,'za'=4,'zl'=4,'yl'=2] {'yh','x'}, dimensions={0} | all-to-all | bytes 2359296 | tf_op jit(solution)/shard_map/all_to_all | solution.py:62
  101.1 1.9 %collective-permute-start.3 = (bf16[256,2304]{1,0:T(8,128)(2,1)}, bf16[256,2304]{1,0:T(8,128)(2,1)}, u32[]{:S(2)}, u32[]{:S(2)}) collective-permute-start(bf16[256,2304]{1,0:T(8,128)(2,1)} %bitcast.8.pre_ref.mine_ref), channel_id=1, source_target_pairs={{0,32},{32,0},{1,33},{33,1},{2,34},{34,2},{3,35},{35,3},{4,36},{36... | collective-permute-start | bytes 3538952 | tf_op jit(solution)/shard_map/ppermute | solution.py:58
  103.1 2.6 %shard_map.61.part_ref = bf16[8,32,640]{2,1,0:T(8,128)(2,1)S(1)} custom-call(s32[1]{0:T(128)} %bitcast.core_ref, bf16[256,2304]{1,0:T(8,128)(2,1)} %bitcast.8.pre_ref.mine_ref, bf16[640,1152]{1,0:T(8,128)(2,1)S(1)} %copy-done, bf16[640,1152]{1,0:T(8,128)(2,1)S(1)} %collective-permute-done.1.v_ref), custom_call_target="tpu_custom_call" | custom-call | flops 754974720 | bytes 6000000 | tf_op jit(solution)/shard_map/pallas_call | solution.py:184
  106.1 4.0 %shard_map.62 = (bf16[640,1152]{1,0:T(8,128)(2,1)}, bf16[4,32,640]{2,1,0:T(8,128)(2,1)S(1)}, bf16[2,32,640]{2,1,0:T(8,128)(2,1)S(1)}, bf16[2,32,640]{2,1,0:T(8,1...) custom-call(s32[2]{0:T(128)S(1)} %pad_add_fusion.place_ref, ...), custom_call_target="tpu_custom_call" | custom-call | flops 1509949440 | bytes 9000000 | tf_op jit(solution)/shard_map/pallas_call | solution.py:140
  110.1 2.0 %collective-permute-start.8 = (bf16[640,1152]{1,0:T(8,128)(2,1)}, bf16[640,1152]{1,0:T(8,128)(2,1)S(1)}, u32[]{:S(2)}, u32[]{:S(2)}) collective-permute-start(bf16[640,1152]{1,0:T(8,128)(2,1)} %get-tuple-element.15), channel_id=1, source_target_pairs={{0,1},{1,0},{2,3},{3,2},{4,5},{5,4},{6,7},{7,6},{8,9},{9,8},{10,11... | collective-permute-start | bytes 4423688 | tf_op jit(solution)/shard_map/ppermute | solution.py:163
  112.2 1.9 %collective-permute-start.4 = (bf16[4,32,640]{2,1,0:T(8,128)(2,1)S(1)}, bf16[4,32,640]{2,1,0:T(8,128)(2,1)S(1)}, u32[]{:S(2)}, u32[]{:S(2)}) collective-permute-start(bf16[4,32,640]{2,1,0:T(8,128)(2,1)S(1)} %get-tuple-element.11), channel_id=1, source_target_pairs={{0,2},{2,4},{4,6},{6,8},{8,10},{10,12},{12,14},{14,16},{16,18},{18... | collective-permute-start | bytes 491528 | tf_op jit(solution)/shard_map/ppermute | solution.py:54
  114.1 5.1 %collective-permute-start.5 = (bf16[4,32,640]{2,1,0:T(8,128)(2,1)S(1)}, bf16[4,32,640]{2,1,0:T(8,128)(2,1)S(1)}, u32[]{:S(2)}, u32[]{:S(2)}) collective-permute-start(bf16[4,32,640]{2,1,0:T(8,128)(2,1)S(1)} %get-tuple-element.12), channel_id=1, source_target_pairs={{0,30},{2,0},{4,2},{6,4},{8,6},{10,8},{12,10},{14,12},{16,14},{18,... | collective-permute-start | bytes 491528 | tf_op jit(solution)/shard_map/ppermute | solution.py:54
  119.2 1.9 %collective-permute-start.6 = (bf16[2,32,640]{2,1,0:T(8,128)(2,1)S(1)}, bf16[2,32,640]{2,1,0:T(8,128)(2,1)S(1)}, u32[]{:S(2)}, u32[]{:S(2)}) collective-permute-start(bf16[2,32,640]{2,1,0:T(8,128)(2,1)S(1)} %get-tuple-element.13), channel_id=1, source_target_pairs={{0,4},{2,6},{4,8},{6,10},{8,12},{10,14},{12,16},{14,18},{16,20},{1... | collective-permute-start | bytes 245768 | tf_op jit(solution)/shard_map/ppermute | solution.py:54
  121.2 6.0 %collective-permute-start.7 = (bf16[2,32,640]{2,1,0:T(8,128)(2,1)S(1)}, bf16[2,32,640]{2,1,0:T(8,128)(2,1)S(1)}, u32[]{:S(2)}, u32[]{:S(2)}) collective-permute-start(bf16[2,32,640]{2,1,0:T(8,128)(2,1)S(1)} %get-tuple-element.14), channel_id=1, source_target_pairs={{0,28},{2,30},{4,0},{6,2},{8,4},{10,6},{12,8},{14,10},{16,12},{18,... | collective-permute-start | bytes 245768 | tf_op jit(solution)/shard_map/ppermute | solution.py:54
  127.2 2.8 %shard_map.63 = bf16[640,1152]{1,0:T(8,128)(2,1)S(1)} custom-call(s32[1]{0:T(128)} %bitcast.core_ref, bf16[8,2,32,640]{3,2,1,0:T(8,128)(2,1)S(1)} %bitcast.21, bf16[256,2304]{1,0:T(8,128)(2,1)} %bitcast.8.pre_ref.mine_ref, bf16[256,2304]{1,0:T(8,128)(2,1)} %collective-permute-done.3.pre_ref.other_ref), custom_call_target="tpu_custom_call" | custom-call | flops 754974720 | bytes 4000000 | tf_op jit(solution)/shard_map/pallas_call | solution.py:190
  130.9 7.1 %all-to-all-start.2 = ((bf16[4,32,640]{2,1,0:T(8,128)(2,1)}), bf16[4,32,640]{2,1,0:T(8,128)(2,1)S(1)}, u32[]{:S(2)}, u32[]{:S(2)}) async-start(bf16[4,32,640]{2,1,0:T(8,128)(2,1)} %add_convert_fusion.2), calls=%async_computation.2 | async-start | bytes 327680 | tf_op jit(solution)/shard_map/all_to_all | solution.py:189
  138.0 8.6 %collective-permute-done.8 = bf16[640,1152]{1,0:T(8,128)(2,1)S(1)} collective-permute-done((bf16[640,1152]{1,0:T(8,128)(2,1)}, bf16[640,1152]{1,0:T(8,128)(2,1)S(1)}, u32[]{:S(2)}, u32[]{:S(2)}) %collective-permute-start.8) | collective-permute-done | bytes 1474592 | tf_op jit(solution)/shard_map/ppermute | solution.py:163
  146.5 1.5 add_convert_fusion
  148.0 6.3 %all-to-all-done.2 = bf16[4,32,640]{2,1,0:T(8,128)(2,1)S(1)} async-done(((bf16[4,32,640]{2,1,0:T(8,128)(2,1)}), bf16[4,32,640]{2,1,0:T(8,128)(2,1)S(1)}, u32[]{:S(2)}, u32[]{:S(2)}) %all-to-all-start.2) | async-done | bytes 163872 | tf_op jit(solution)/shard_map/all_to_all | solution.py:189
  (27 shorter events, 5.5 us)
Async XLA Ops:
  0.6 45.1 %copy-start = (bf16[640,1152]{1,0:T(8,128)(2,1)S(1)}, bf16[640,1152]{1,0:T(8,128)(2,1)}, u32[]{:S(2)}) copy-start(bf16[640,1152]{1,0:T(8,128)(2,1)} %w_ref.7) | copy-start | bytes 4423684
  0.6 45.1 %collective-permute-start.1 = (bf16[640,1152]{1,0:T(8,128)(2,1)}, bf16[640,1152]{1,0:T(8,128)(2,1)S(1)}, u32[]{:S(2)}, u32[]{:S(2)}) collective-permute-start(bf16[640,1152]{1,0:T(8,128)(2,1)} %w_ref.7), channel_id=1, source_target_pairs={{0,1},{1,0},{2,3},{3,2},{4,5},{5,4},{6,7},{7,6},{8,9},{9,8},{10,11... | collective-permute-start | bytes 4423688 | tf_op jit(solution)/shard_map/ppermute | solution.py:163
  45.7 3.2 %copy-start.1 = (bf16[512,640]{1,0:T(8,128)(2,1)}, bf16[512,640]{1,0:T(8,128)(2,1)S(1)}, u32[]{:S(2)}) copy-start(bf16[512,640]{1,0:T(8,128)(2,1)S(1)} %all_gather.3) | copy-start | bytes 1966084
  47.0 4.7 %collective-permute-start.2 = (bf16[256,2304]{1,0:T(8,128)(2,1)S(1)}, bf16[256,2304]{1,0:T(8,128)(2,1)S(1)}, u32[]{:S(2)}, u32[]{:S(2)}) collective-permute-start(bf16[256,2304]{1,0:T(8,128)(2,1)S(1)} %shard_map.60), channel_id=1, source_target_pairs={{0,32},{32,0},{1,33},{33,1},{2,34},{34,2},{3,35},{35,3},{4,36},{36... | collective-permute-start | bytes 3538952 | tf_op jit(solution)/shard_map/ppermute | solution.py:58
  53.0 7.2 %copy-start.3 = (bf16[64,1152]{1,0:T(8,128)(2,1)S(1)}, bf16[64,1152]{1,0:T(8,128)(2,1)}, u32[]{:S(2)}) copy-start(bf16[64,1152]{1,0:T(8,128)(2,1)} %param.6) | copy-start | bytes 442372
  53.0 23.7 %all-to-all-start = ((bf16[8,32,2304]{2,1,0:T(8,128)(2,1)}), bf16[8,32,2304]{2,1,0:T(8,128)(2,1)}, u32[]{:S(2)}, u32[]{:S(2)}) async-start(bf16[8,32,2304]{2,1,0:T(8,128)(2,1)} %bitcast.22), calls=%async_computation | async-start | bytes 2359296 | tf_op jit(solution)/shard_map/all_to_all | solution.py:62
  60.3 17.9 %collective-permute-start = (bf16[32,1152]{1,0:T(8,128)(2,1)S(1)}, bf16[32,1152]{1,0:T(8,128)(2,1)S(1)}, u32[]{:S(2)}, u32[]{:S(2)}) collective-permute-start(bf16[32,1152]{1,0:T(8,128)(2,1)S(1)} %get-tuple-element.19), channel_id=1, source_target_pairs={{0,1},{1,0},{2,3},{3,2},{4,5},{5,4},{6,7},{7,6},{8,9},{9,8},{10,11... | collective-permute-start | bytes 221192 | tf_op jit(solution)/shard_map/ppermute | solution.py:163
  101.1 5.1 %collective-permute-start.3 = (bf16[256,2304]{1,0:T(8,128)(2,1)}, bf16[256,2304]{1,0:T(8,128)(2,1)}, u32[]{:S(2)}, u32[]{:S(2)}) collective-permute-start(bf16[256,2304]{1,0:T(8,128)(2,1)} %bitcast.8.pre_ref.mine_ref), channel_id=1, source_target_pairs={{0,32},{32,0},{1,33},{33,1},{2,34},{34,2},{3,35},{35,3},{4,36},{36... | collective-permute-start | bytes 3538952 | tf_op jit(solution)/shard_map/ppermute | solution.py:58
  103.1 3.1 %copy-start.2 = (bf16[512,640]{1,0:T(8,128)(2,1)S(1)}, bf16[512,640]{1,0:T(8,128)(2,1)}, u32[]{:S(2)}) copy-start(bf16[512,640]{1,0:T(8,128)(2,1)} %copy-done.1) | copy-start | bytes 1966084
  110.1 36.4 %collective-permute-start.8 = (bf16[640,1152]{1,0:T(8,128)(2,1)}, bf16[640,1152]{1,0:T(8,128)(2,1)S(1)}, u32[]{:S(2)}, u32[]{:S(2)}) collective-permute-start(bf16[640,1152]{1,0:T(8,128)(2,1)} %get-tuple-element.15), channel_id=1, source_target_pairs={{0,1},{1,0},{2,3},{3,2},{4,5},{5,4},{6,7},{7,6},{8,9},{9,8},{10,11... | collective-permute-start | bytes 4423688 | tf_op jit(solution)/shard_map/ppermute | solution.py:163
  112.2 17.9 %collective-permute-start.4 = (bf16[4,32,640]{2,1,0:T(8,128)(2,1)S(1)}, bf16[4,32,640]{2,1,0:T(8,128)(2,1)S(1)}, u32[]{:S(2)}, u32[]{:S(2)}) collective-permute-start(bf16[4,32,640]{2,1,0:T(8,128)(2,1)S(1)} %get-tuple-element.11), channel_id=1, source_target_pairs={{0,2},{2,4},{4,6},{6,8},{8,10},{10,12},{12,14},{14,16},{16,18},{18... | collective-permute-start | bytes 491528 | tf_op jit(solution)/shard_map/ppermute | solution.py:54
  114.1 16.0 %collective-permute-start.5 = (bf16[4,32,640]{2,1,0:T(8,128)(2,1)S(1)}, bf16[4,32,640]{2,1,0:T(8,128)(2,1)S(1)}, u32[]{:S(2)}, u32[]{:S(2)}) collective-permute-start(bf16[4,32,640]{2,1,0:T(8,128)(2,1)S(1)} %get-tuple-element.12), channel_id=1, source_target_pairs={{0,30},{2,0},{4,2},{6,4},{8,6},{10,8},{12,10},{14,12},{16,14},{18,... | collective-permute-start | bytes 491528 | tf_op jit(solution)/shard_map/ppermute | solution.py:54
  119.2 10.8 %collective-permute-start.6 = (bf16[2,32,640]{2,1,0:T(8,128)(2,1)S(1)}, bf16[2,32,640]{2,1,0:T(8,128)(2,1)S(1)}, u32[]{:S(2)}, u32[]{:S(2)}) collective-permute-start(bf16[2,32,640]{2,1,0:T(8,128)(2,1)S(1)} %get-tuple-element.13), channel_id=1, source_target_pairs={{0,4},{2,6},{4,8},{6,10},{8,12},{10,14},{12,16},{14,18},{16,20},{1... | collective-permute-start | bytes 245768 | tf_op jit(solution)/shard_map/ppermute | solution.py:54
  121.2 8.9 %collective-permute-start.7 = (bf16[2,32,640]{2,1,0:T(8,128)(2,1)S(1)}, bf16[2,32,640]{2,1,0:T(8,128)(2,1)S(1)}, u32[]{:S(2)}, u32[]{:S(2)}) collective-permute-start(bf16[2,32,640]{2,1,0:T(8,128)(2,1)S(1)} %get-tuple-element.14), channel_id=1, source_target_pairs={{0,28},{2,30},{4,0},{6,2},{8,4},{10,6},{12,8},{14,10},{16,12},{18,... | collective-permute-start | bytes 245768 | tf_op jit(solution)/shard_map/ppermute | solution.py:54
  130.9 23.5 %all-to-all-start.2 = ((bf16[4,32,640]{2,1,0:T(8,128)(2,1)}), bf16[4,32,640]{2,1,0:T(8,128)(2,1)S(1)}, u32[]{:S(2)}, u32[]{:S(2)}) async-start(bf16[4,32,640]{2,1,0:T(8,128)(2,1)} %add_convert_fusion.2), calls=%async_computation.2 | async-start | bytes 327680 | tf_op jit(solution)/shard_map/all_to_all | solution.py:189

commit v5 on v4

--- a/solution.py
+++ b/solution.py
@@ -50,8 +50,9 @@
     return lax.dot_general(a, b, (dims, ((), ())), preferred_element_type=jnp.float32)
 
 
-def along_z(array, step):
-    return lax.ppermute(array, ("za", "zl"), [(z, (z + step) % 16) for z in range(16)])
+def z_and_core(array, target):
+    pairs = [(16 * core + z, 16 * core + target(z, core) % 16) for core in range(2) for z in range(16)]
+    return lax.ppermute(array, ("c", "za", "zl"), pairs)
 
 
 def swap_cores(array):
@@ -106,57 +107,41 @@
     return part.astype(jnp.bfloat16).reshape(8, 32, 640)
 
 
-def part_kernel(core_ref, pre_ref, w_ref, v_ref, part_ref):
-    part_ref[...] = input_part(pre_ref, w_ref, v_ref)
+def part_kernel(class_ref, pre_ref, w_ref, v_ref, w2_ref, v2_ref, first_ref, second_ref, kept_ref, lent_ref):
+    for i, weights in enumerate(((w_ref, v_ref), (w2_ref, v2_ref))):
+        part = input_part(pre_ref, *weights).reshape(4, 2, 32, 640)
+        for out_ref, which in ((first_ref, class_ref[0]), (second_ref, class_ref[1])):
+
+            @pl.when(which == 0)
+            def _():
+                out_ref[i] = part[:, 0]
+
+            @pl.when(which == 1)
+            def _():
+                out_ref[i] = part[:, 1]
+
+    kept_ref[...] = pre_ref[:, :1152]
+    lent_ref[...] = pre_ref[:, 1152:]
 
 
-def weight_terms(core, rows_ref, mine_ref, other_ref, first):
+def weight_terms(terms):
     tn = (((0,), (0,)), ((), ()))
-    left = [rows_ref[:, at].reshape(256, 640) for at in (core, 1 - core)]
     for j in range(0, 1152, 384):
-        at = slice(first + j, first + j + 384)
-        total = lax.dot_general(left[0], mine_ref[:, at], tn, preferred_element_type=jnp.float32)
-        yield slice(j, j + 384), total + lax.dot_general(left[1], other_ref[:, at], tn, preferred_element_type=jnp.float32)
+        at = slice(j, j + 384)
+        yield at, sum(lax.dot_general(rows, grad[:, at], tn, preferred_element_type=jnp.float32) for rows, grad in terms)
 
 
-def spread_kernel(place_ref, rows_ref, part_ref, mine_ref, pre_ref, w_ref, v_ref, lent_ref, own_ref, right2_ref, left2_ref, right_ref, left_ref, all_ref):
-    core, place = place_ref[0], place_ref[1]
-    for at, total in weight_terms(core, rows_ref, mine_ref, pre_ref, 1152):
-        lent_ref[:, at] = total.astype(jnp.bfloat16)
-    other = input_part(pre_ref, w_ref, v_ref)
-    for low in range(2):
-        for high in range(4):
-            all_ref[2 * low + core, high] = part_ref[2 * high + low]
-            all_ref[2 * low + 1 - core, high] = other[2 * high + low]
-    own_ref[...] = all_ref[place]
-    right_ref[...] = all_ref[lax.rem(place + 1, 4)]
-    left_ref[...] = all_ref[lax.rem(place + 3, 4)]
-    apart = lax.rem(place + 2, 4)
-    right2_ref[...] = all_ref[apart, 0:2]
-    left2_ref[...] = all_ref[apart, 2:4]
-
-
-def spread(place, rows, part, mine, pre, w_in, w_pair):
-    return pl.pallas_call(
-        spread_kernel,
-        out_shape=[shape(640, 1152)] + [shape(count, 32, 640) for count in (4, 2, 2, 4, 4)],
-        in_specs=[SMEM] + [VMEM] * 6,
-        out_specs=[VMEM] * 6,
-        scratch_shapes=[pltpu.VMEM((4, 4, 32, 640), jnp.bfloat16)],
-        compiler_params=PARAMS,
-        cost_estimate=pl.CostEstimate(flops=4 * 256 * 640 * 2304, bytes_accessed=9000000, transcendentals=0),
-    )(place, rows, part, mine, pre, w_in, w_pair)
-
-
-def kept_kernel(core_ref, rows_ref, mine_ref, other_ref, out_ref):
-    for at, total in weight_terms(core_ref[0], rows_ref, mine_ref, other_ref, 0):
+def kept_kernel(at_ref, rows_ref, mine_ref, other_ref, out_ref):
+    left = [rows_ref[:, at].reshape(256, 640) for at in (at_ref[0], 1 - at_ref[0])]
+    for at, total in weight_terms(list(zip(left, (mine_ref, other_ref)))):
         out_ref[:, at] = total.astype(jnp.bfloat16)
 
 
-def summed_near(own, right2, left2, right, left):
-    right2, left2, right, left = along_z(right2, 2), along_z(left2, -2), along_z(right, 1), along_z(left, -1)
-    f = lambda v: v.astype(jnp.float32)
-    return (f(own) + f(right) + f(left) + f(jnp.concatenate([right2, left2]))).astype(jnp.bfloat16)
+def weight_kernel(at_ref, rows_ref, mine_ref, other_ref, other2_ref, kept_ref, out_ref):
+    last = rows_ref[:, 1 - at_ref[0]].reshape(2, 128, 640)
+    left = [rows_ref[:, at_ref[0]].reshape(256, 640), last[0], last[1]]
+    for at, total in weight_terms(list(zip(left, (mine_ref, other_ref, other2_ref)))):
+        out_ref[:, at] = (total + kept_ref[:, at].astype(jnp.float32)).astype(jnp.bfloat16)
 
 
 def swap_pair(array):
@@ -164,31 +149,43 @@
 
 
 def shards(x_rotated, block_scales, grad_act, w_in):
-    side, core = lax.axis_index("yl"), lax.axis_index("c")
+    side, core, zl = lax.axis_index("yl"), lax.axis_index("c"), lax.axis_index("zl")
+    at = jnp.reshape(jnp.bitwise_and(core + zl, 1), (1,)).astype(jnp.int32)
     w_pair = swap_pair(w_in)
     own = decode(x_rotated, block_scales)
     rows = lax.all_gather(own, ("za", "zl"), axis=0, tiled=True).reshape(8, 2, 32, 640)
-    at = jnp.reshape(core, (1,)).astype(jnp.int32)
     flops = 2 * 256 * 640 * 2304
     (far,) = call(far_kernel, [shape(256, 2304)], 3, flops, 6000000)(at, rows, w_in, w_pair)
-    grads = grad_act.reshape(2, 32, 1152)
+    pairs = [(4 * c + z, 4 * ((c + z) % 2) + z) for c in range(2) for z in range(4)]
+    grads = lax.ppermute(grad_act, ("c", "zl"), pairs).reshape(2, 32, 1152)
     lent = lax.dynamic_index_in_dim(grads, 1 - side, 0, keepdims=False)
     kept = lax.dynamic_index_in_dim(grads, side, 0, keepdims=False)
     far, lent = swap_cores(far), swap_pair(lent)
     grads = jnp.concatenate([kept, lent], axis=1)
     (near,) = call(near_kernel, [shape(256, 2304)], 3, flops, 6000000)(at, rows, w_in, w_pair)
     near = (near.astype(jnp.float32) + far.astype(jnp.float32)).astype(jnp.bfloat16).reshape(8, 32, 2304)
+    w_core, w_pair_core = swap_cores(w_in), swap_cores(w_pair)
     pre = jnp.sum(exchange(near).astype(jnp.float32), axis=0)
     mine = exchange(copies(slope_grad(pre, grads))).reshape(256, 2304)
-    other = swap_cores(mine)
-    (part,) = call(part_kernel, [shape(8, 32, 640)], 3, flops, 6000000)(at, mine, w_in, w_pair)
-    place = jnp.stack([core, lax.axis_index("zl")]).astype(jnp.int32)
-    lent, *pieces = spread(place, rows, part, mine, other, w_in, w_pair)
-    lent = swap_pair(lent)
-    near = summed_near(*pieces)
+
+    classes = jnp.stack([jnp.bitwise_and(zl + 2 - core, 3), jnp.bitwise_and(zl + 3 * core, 3)])
+    classes = jnp.right_shift(classes, 1).astype(jnp.int32)
+    shapes = [shape(2, 4, 32, 640), shape(2, 4, 32, 640), shape(256, 1152), shape(256, 1152)]
+    first, second, mine, lent = call(part_kernel, shapes, 5, 2 * flops, 9000000)(
+        classes, mine, w_in, w_pair, w_core, w_pair_core
+    )
+    first = z_and_core(first, lambda z, c: z + 1 if c else z + (2 if z % 2 == 0 else -2))
+    second = z_and_core(second, lambda z, c: z - c)
+    mine_pair = swap_pair(lent)
+    rows_pair, _ = lax.optimization_barrier((rows, lent))
+    rows_pair = swap_pair(rows_pair)
+    near = first.astype(jnp.float32) + second.astype(jnp.float32)
+    lent, other = lax.optimization_barrier((near[1].astype(jnp.bfloat16), swap_cores(mine)))
+    near = (near[0] + swap_cores(lent).astype(jnp.float32)).astype(jnp.bfloat16)
     blocks = lax.all_to_all(near, "za", 0, 0, tiled=True)
-    (kept,) = call(kept_kernel, [shape(640, 1152)], 3, flops, 4000000)(at, rows, mine, other)
-    grad_weight = (kept.astype(jnp.float32) + lent.astype(jnp.float32)).astype(jnp.bfloat16)
+    other_pair = [swap_cores(mine_pair.reshape(2, 128, 1152)[i // 576]) for i in (0, 576)]
+    (kept,) = call(kept_kernel, [shape(640, 1152)], 3, flops, 5000000)(at, rows, mine, other)
+    (grad_weight,) = call(weight_kernel, [shape(640, 1152)], 5, flops, 5000000)(at, rows_pair, mine_pair, *other_pair, kept)
     blocks, grad_weight = lax.optimization_barrier((blocks, grad_weight))
     return jnp.sum(blocks.astype(jnp.float32), axis=0).astype(jnp.bfloat16), grad_weight
 

time: 157 us -> 155 us (0.987)
  blocking collectives: 62 us -> 39.4 us
  starting transfers between devices: 40.9 us -> 53 us
  waiting for transfers between devices: 31.3 us -> 38.3 us
    all_to_all x1 -> x0, blocking collectives: 22.7 us -> none  [exchange(): return lax.all_to_all(blocks, ('yh', 'x'), 0, 0, tiled=True)]
    ppermute x2 -> x7, starting transfers between devices: 3.83 us -> 18.6 us  [swap_cores(): return lax.ppermute(array, 'c', SWAP)]
    ppermute x4 -> x3, starting transfers between devices: 15 us -> 3.61 us  [the longest x2 2.95 us: z_and_core(): return lax.ppermute(array, ('c', 'za', 'zl'), pairs)]
    all_to_all x1 -> x2, waiting for transfers between devices: 14.4 us -> 25.5 us  [exchange(): return lax.all_to_all(blocks, ('yh', 'x'), 0, 0, tiled=True)]
    all_to_all x1 -> x2, starting transfers between devices: 7.24 us -> 14 us  [exchange(): return lax.all_to_all(blocks, ('yh', 'x'), 0, 0, tiled=True)]
    all_to_all x1, waiting for transfers between devices: 6.32 us -> 0.01 us  [shards(): blocks = lax.all_to_all(near, 'za', 0, 0, tiled=True)]
    ppermute x3 -> x4, starting transfers between devices: 7.7 us -> 10.3 us  [swap_pair(): return lax.ppermute(array, 'yl', SWAP)]
    ppermute x3 -> x4, waiting for transfers between devices: 8.56 us -> 9.71 us  [swap_pair(): return lax.ppermute(array, 'yl', SWAP)]
  transfers between devices with their start and end apart: 11 -> 17, of which waited for: 5 -> 6; matrix products, arithmetic and copies ran while one was open for 4% -> 4% of each run, Pallas kernels for 4% -> 3%
where the time goes in v5:
time: 155 us; the launch traced here: 152 us
  starting transfers between devices  53 us (34%)
  blocking collectives  39.4 us (25%)
  waiting for transfers between devices  38.3 us (25%)
  Pallas kernels  12 us (8%)
  other arithmetic  5.41 us (3%)
  local copies, waits for them, and re-layouts  2.81 us (2%)
    all_gather x1, blocking collectives, shards(): lax.all_gather(own, ('za', 'zl'), axis=0, tiled=True).reshape(8, 2, 32, 640)  39.4 us
    all_to_all x2, waiting for transfers between devices, exchange(): return lax.all_to_all(blocks, ('yh', 'x'), 0, 0, tiled=True)  25.5 us
    ppermute x7, starting transfers between devices, swap_cores(): return lax.ppermute(array, 'c', SWAP)  18.6 us
    all_to_all x2, starting transfers between devices, exchange(): return lax.all_to_all(blocks, ('yh', 'x'), 0, 0, tiled=True)  14 us
    ppermute x4, starting transfers between devices, swap_pair(): return lax.ppermute(array, 'yl', SWAP)  10.3 us
    ppermute x4, waiting for transfers between devices, swap_pair(): return lax.ppermute(array, 'yl', SWAP)  9.71 us
    all_to_all x1, starting transfers between devices, shards(): blocks = lax.all_to_all(near, 'za', 0, 0, tiled=True)  6.42 us
    pallas_call x1, Pallas kernels, shards(): call(part_kernel, shapes, 5, 2 * flops, 9000000)  5.54 us
  transfers between devices with their start and end apart: 17, of which 6 were waited for; matrix products, arithmetic and copies ran while one was open for 4% of the time, Pallas kernels for 3%

profile of v5, /device:TPU:6, one launch (start us, length us, event | category | flops | bytes accessed | tf_op | source)
XLA Modules:
  0.0 152.1 jit_solution(1306199450644278468)
XLA Ops:
  0.6 3.6 %collective-permute-start.2 = (bf16[640,1152]{1,0:T(8,128)(2,1)}, bf16[640,1152]{1,0:T(8,128)(2,1)S(1)}, u32[]{:S(2)}, u32[]{:S(2)}) collective-permute-start(bf16[640,1152]{1,0:T(8,128)(2,1)} %w_ref.5), channel_id=1, source_target_pairs={{0,1},{1,0},{2,3},{3,2},{4,5},{5,4},{6,7},{7,6},{8,9},{9,8},{10,11... | collective-permute-start | bytes 4423688 | tf_op jit(solution)/shard_map/ppermute | solution.py:148
  6.3 39.4 %all_gather.3 = bf16[512,640]{1,0:T(8,128)(2,1)S(1)} all-gather(bf16[32,640]{1,0:T(8,128)(2,1)S(1)} %bitcast.32), channel_id=1, replica_groups=mesh['yh'=2,'x'=4,'c'=2,'za'=4,'zl'=4,'yl'=2] {'za','zl'}, dimensions={0}, use_global_device_ids=true | all-gather | bytes 696320 | tf_op jit(solution)/shard_map/all_gather | solution.py:156
  47.0 1.9 %collective-permute-start.3 = (bf16[256,2304]{1,0:T(8,128)(2,1)S(1)}, bf16[256,2304]{1,0:T(8,128)(2,1)S(1)}, u32[]{:S(2)}, u32[]{:S(2)}) collective-permute-start(bf16[256,2304]{1,0:T(8,128)(2,1)S(1)} %shard_map.60), channel_id=1, source_target_pairs={{0,32},{32,0},{1,33},{33,1},{2,34},{34,2},{3,35},{35,3},{4,36},{36... | collective-permute-start | bytes 3538952 | tf_op jit(solution)/shard_map/ppermute | solution.py:59
  53.0 7.2 %all-to-all-start = ((bf16[8,32,2304]{2,1,0:T(8,128)(2,1)}), bf16[8,32,2304]{2,1,0:T(8,128)(2,1)}, u32[]{:S(2)}, u32[]{:S(2)}) async-start(bf16[8,32,2304]{2,1,0:T(8,128)(2,1)} %bitcast.31), calls=%async_computation | async-start | bytes 2359296 | tf_op jit(solution)/shard_map/all_to_all | solution.py:63
  61.0 1.9 %collective-permute-start.4 = (bf16[640,1152]{1,0:T(8,128)(2,1)S(1)}, bf16[640,1152]{1,0:T(8,128)(2,1)}, u32[]{:S(2)}, u32[]{:S(2)}) collective-permute-start(bf16[640,1152]{1,0:T(8,128)(2,1)S(1)} %copy-done), channel_id=1, source_target_pairs={{0,32},{32,0},{1,33},{33,1},{2,34},{34,2},{3,35},{35,3},{4,36},{36... | collective-permute-start | bytes 4423688 | tf_op jit(solution)/shard_map/ppermute | solution.py:59
  62.9 2.1 %collective-permute-start.1 = (bf16[32,1152]{1,0:T(8,128)(2,1)S(1)}, bf16[32,1152]{1,0:T(8,128)(2,1)S(1)}, u32[]{:S(2)}, u32[]{:S(2)}) collective-permute-start(bf16[32,1152]{1,0:T(8,128)(2,1)S(1)} %get-tuple-element.23), channel_id=1, source_target_pairs={{0,1},{1,0},{2,3},{3,2},{4,5},{5,4},{6,7},{7,6},{8,9},{9,8},{10,11... | collective-permute-start | bytes 221192 | tf_op jit(solution)/shard_map/ppermute | solution.py:148
  65.0 2.3 %collective-permute-start.5 = (bf16[640,1152]{1,0:T(8,128)(2,1)S(1)}, bf16[640,1152]{1,0:T(8,128)(2,1)}, u32[]{:S(2)}, u32[]{:S(2)}) collective-permute-start(bf16[640,1152]{1,0:T(8,128)(2,1)S(1)} %collective-permute-done.2.v_ref), channel_id=1, source_target_pairs={{0,32},{32,0},{1,33},{33,1},{2,34},{34,2},{3,35},{35,3},{4,36},{36... | collective-permute-start | bytes 4423688 | tf_op jit(solution)/shard_map/ppermute | solution.py:59
  67.3 9.5 %all-to-all-done = bf16[8,32,2304]{2,1,0:T(8,128)(2,1)} async-done(((bf16[8,32,2304]{2,1,0:T(8,128)(2,1)}), bf16[8,32,2304]{2,1,0:T(8,128)(2,1)}, u32[]{:S(2)}, u32[]{:S(2)}) %all-to-all-start) | async-done | bytes 1179680 | tf_op jit(solution)/shard_map/all_to_all | solution.py:63
  79.4 6.8 %all-to-all-start.1 = ((bf16[8,32,2304]{2,1,0:T(8,128)(2,1)}), bf16[8,32,2304]{2,1,0:T(8,128)(2,1)}, u32[]{:S(2)}, u32[]{:S(2)}) async-start(bf16[8,32,2304]{2,1,0:T(8,128)(2,1)} %broadcast_in_dim.2), calls=%async_computation.1 | async-start | bytes 2359296 | tf_op jit(solution)/shard_map/all_to_all | solution.py:63
  86.3 16.1 %all-to-all-done.1 = bf16[8,32,2304]{2,1,0:T(8,128)(2,1)} async-done(((bf16[8,32,2304]{2,1,0:T(8,128)(2,1)}), bf16[8,32,2304]{2,1,0:T(8,128)(2,1)}, u32[]{:S(2)}, u32[]{:S(2)}) %all-to-all-start.1) | async-done | bytes 1179680 | tf_op jit(solution)/shard_map/all_to_all | solution.py:63
  102.4 5.5 %shard_map.61 = (bf16[2,4,32,640]{3,2,1,0:T(8,128)(2,1)S(1)}, bf16[2,4,32,640]{3,2,1,0:T(8,128)(2,1)S(1)}, bf16[256,1152]{1,0:T(8,128)(2,1)S(1)}, bf16[256,1152]{1,0:T(8,128)(2,1)}) custom-call(s32[2]{0:T(128)S(1)} %add_shift-right-arithmetic_fusion.class_ref, bf16[256,2304]{1,0:T(8,128)(2,1)} %bitcast.9.pre_ref, bf16[640,1152]{1,0:T(8,128)(2,1)S(1)} %copy-done, ...), custom_call_target="tpu_custom_call" | custom-call | flops 1509949440 | bytes 9000000 | tf_op jit(solution)/shard_map/pallas_call | solution.py:174
  107.9 2.3 %collective-permute-start.6 = (bf16[2,4,32,640]{3,2,1,0:T(8,128)(2,1)S(1)}, bf16[2,4,32,640]{3,2,1,0:T(8,128)(2,1)S(1)}, u32[]{:S(2)}, u32[]{:S(2)}) collective-permute-start(bf16[2,4,32,640]{3,2,1,0:T(8,128)(2,1)S(1)} %get-tuple-element.11), channel_id=1, source_target_pairs={{0,4},{2,30},{4,8},{6,2},{8,12},{10,6},{12,16},{14,10},{16,20},{18... | collective-permute-start | bytes 983048 | tf_op jit(solution)/shard_map/ppermute | solution.py:55
  110.9 5.6 %collective-permute-start.8 = (bf16[256,1152]{1,0:T(8,128)(2,1)S(1)}, bf16[256,1152]{1,0:T(8,128)(2,1)S(1)}, u32[]{:S(2)}, u32[]{:S(2)}) collective-permute-start(bf16[256,1152]{1,0:T(8,128)(2,1)S(1)} %get-tuple-element.13.mine_ref), channel_id=1, source_target_pairs={{0,32},{32,0},{1,33},{33,1},{2,34},{34,2},{3,35},{35,3},{4,36},{36... | collective-permute-start | bytes 1769480 | tf_op jit(solution)/shard_map/ppermute | solution.py:59
  116.5 2.1 %collective-permute-start.11 = (bf16[256,1152]{1,0:T(8,128)(2,1)}, bf16[256,1152]{1,0:T(8,128)(2,1)S(1)}, u32[]{:S(2)}, u32[]{:S(2)}) collective-permute-start(bf16[256,1152]{1,0:T(8,128)(2,1)} %get-tuple-element.15), channel_id=1, source_target_pairs={{0,1},{1,0},{2,3},{3,2},{4,5},{5,4},{6,7},{7,6},{8,9},{9,8},{10,11... | collective-permute-start | bytes 1769480 | tf_op jit(solution)/shard_map/ppermute | solution.py:148
  118.5 1.5 %collective-permute-done.6 = bf16[2,4,32,640]{3,2,1,0:T(8,128)(2,1)S(1)} collective-permute-done((bf16[2,4,32,640]{3,2,1,0:T(8,128)(2,1)S(1)}, bf16[2,4,32,640]{3,2,1,0:T(8,128)(2,1)S(1)}, u32[]{:S(2)}, u32[]{:S(2)}) %collective-permute-start.6) | collective-permute-done | bytes 327712 | tf_op jit(solution)/shard_map/ppermute | solution.py:55
  120.2 2.6 %collective-permute-start.9 = (bf16[4,32,640]{2,1,0:T(8,128)(2,1)S(1)}, bf16[4,32,640]{2,1,0:T(8,128)(2,1)S(1)}, u32[]{:S(2)}, u32[]{:S(2)}) collective-permute-start(bf16[4,32,640]{2,1,0:T(8,128)(2,1)S(1)} %fusion.9), channel_id=1, source_target_pairs={{0,32},{32,0},{1,33},{33,1},{2,34},{34,2},{3,35},{35,3},{4,36},{36... | collective-permute-start | bytes 491528 | tf_op jit(solution)/shard_map/ppermute | solution.py:59
  122.8 2.6 %collective-permute-start.10 = (bf16[8,2,32,640]{3,2,1,0:T(8,128)(2,1)S(1)}, bf16[8,2,32,640]{3,2,1,0:T(8,128)(2,1)S(1)}, u32[]{:S(2)}, u32[]{:S(2)}) collective-permute-start(bf16[8,2,32,640]{3,2,1,0:T(8,128)(2,1)S(1)} %bitcast.29), channel_id=1, source_target_pairs={{0,1},{1,0},{2,3},{3,2},{4,5},{5,4},{6,7},{7,6},{8,9},{9,8},{10,11... | collective-permute-start | bytes 1966088 | tf_op jit(solution)/shard_map/ppermute | solution.py:148
  126.1 6.4 %all-to-all-start.2 = ((bf16[4,32,640]{2,1,0:T(8,128)(2,1)}), bf16[4,32,640]{2,1,0:T(8,128)(2,1)}, u32[]{:S(2)}, u32[]{:S(2)}) async-start(bf16[4,32,640]{2,1,0:T(8,128)(2,1)} %fusion.2), calls=%async_computation.2 | async-start | bytes 327680 | tf_op jit(solution)/shard_map/all_to_all | solution.py:185
  132.5 2.2 %collective-permute-done.11.mine_ref = bf16[256,1152]{1,0:T(8,128)(2,1)S(1)} collective-permute-done((bf16[256,1152]{1,0:T(8,128)(2,1)}, bf16[256,1152]{1,0:T(8,128)(2,1)S(1)}, u32[]{:S(2)}, u32[]{:S(2)}) %collective-permute-start.11) | collective-permute-done | bytes 589856 | tf_op jit(solution)/shard_map/ppermute | solution.py:148
  134.8 1.9 %collective-permute-start.13 = (bf16[128,1152]{1,0:T(8,128)(2,1)S(1)}, bf16[128,1152]{1,0:T(8,128)(2,1)S(1)}, u32[]{:S(2)}, u32[]{:S(2)}) collective-permute-start(bf16[128,1152]{1,0:T(8,128)(2,1)S(1)} %get-tuple-element.20), channel_id=1, source_target_pairs={{0,32},{32,0},{1,33},{33,1},{2,34},{34,2},{3,35},{35,3},{4,36},{36... | collective-permute-start | bytes 884744 | tf_op jit(solution)/shard_map/ppermute | solution.py:59
  136.8 2.4 %collective-permute-start.12 = (bf16[128,1152]{1,0:T(8,128)(2,1)S(1)}, bf16[128,1152]{1,0:T(8,128)(2,1)S(1)}, u32[]{:S(2)}, u32[]{:S(2)}) collective-permute-start(bf16[128,1152]{1,0:T(8,128)(2,1)S(1)} %get-tuple-element.21), channel_id=1, source_target_pairs={{0,32},{32,0},{1,33},{33,1},{2,34},{34,2},{3,35},{35,3},{4,36},{36... | collective-permute-start | bytes 884744 | tf_op jit(solution)/shard_map/ppermute | solution.py:59
  140.4 7.5 %collective-permute-done.10.rows_ref = bf16[8,2,32,640]{3,2,1,0:T(8,128)(2,1)S(1)} collective-permute-done((bf16[8,2,32,640]{3,2,1,0:T(8,128)(2,1)S(1)}, bf16[8,2,32,640]{3,2,1,0:T(8,128)(2,1)S(1)}, u32[]{:S(2)}, u32[]{:S(2)}) %collective-permute-start.10) | collective-permute-done | bytes 655392 | tf_op jit(solution)/shard_map/ppermute | solution.py:148
  147.9 2.6 %shard_map.63 = bf16[640,1152]{1,0:T(8,128)(2,1)} custom-call(s32[1]{0:T(128)} %bitcast.5.core_ref.at_ref, bf16[8,2,32,640]{3,2,1,0:T(8,128)(2,1)S(1)} %collective-permute-done.10.rows_ref, bf16[256,1152]{1,0:T(8,128)(2,1)S(1)} %collective-permute-done.11.mine_ref, bf16[128,1152]{1,0:T(8,128)(2,1)S(1)} %collective-permute-done.12.other_ref, ...), custom_call_target="tpu_custom_call" | custom-call | flops 754974720 | bytes 5000000 | tf_op jit(solution)/shard_map/pallas_call | solution.py:188
  150.5 1.6 %reduce_sum.22 = bf16[32,640]{1,0:T(8,128)(2,1)} reduce(bf16[4,32,640]{2,1,0:T(8,128)(2,1)} %all-to-all-done.2, bf16[]{:T(256)} %constant.69.clone.1), dimensions={0}, to_apply=%region_1.2 | reduce | flops 61440 | bytes 204802 | tf_op jit(solution)/shard_map/reduce_sum | solution.py:190
  (40 shorter events, 13.6 us)
Async XLA Ops:
  0.6 45.1 %copy-start = (bf16[640,1152]{1,0:T(8,128)(2,1)S(1)}, bf16[640,1152]{1,0:T(8,128)(2,1)}, u32[]{:S(2)}) copy-start(bf16[640,1152]{1,0:T(8,128)(2,1)} %w_ref.5) | copy-start | bytes 4423684
  0.6 45.1 %collective-permute-start.2 = (bf16[640,1152]{1,0:T(8,128)(2,1)}, bf16[640,1152]{1,0:T(8,128)(2,1)S(1)}, u32[]{:S(2)}, u32[]{:S(2)}) collective-permute-start(bf16[640,1152]{1,0:T(8,128)(2,1)} %w_ref.5), channel_id=1, source_target_pairs={{0,1},{1,0},{2,3},{3,2},{4,5},{5,4},{6,7},{7,6},{8,9},{9,8},{10,11... | collective-permute-start | bytes 4423688 | tf_op jit(solution)/shard_map/ppermute | solution.py:148
  45.7 3.2 %copy-start.1 = (bf16[512,640]{1,0:T(8,128)(2,1)}, bf16[512,640]{1,0:T(8,128)(2,1)S(1)}, u32[]{:S(2)}) copy-start(bf16[512,640]{1,0:T(8,128)(2,1)S(1)} %all_gather.3) | copy-start | bytes 1966084
  47.0 4.7 %collective-permute-start.3 = (bf16[256,2304]{1,0:T(8,128)(2,1)S(1)}, bf16[256,2304]{1,0:T(8,128)(2,1)S(1)}, u32[]{:S(2)}, u32[]{:S(2)}) collective-permute-start(bf16[256,2304]{1,0:T(8,128)(2,1)S(1)} %shard_map.60), channel_id=1, source_target_pairs={{0,32},{32,0},{1,33},{33,1},{2,34},{34,2},{3,35},{35,3},{4,36},{36... | collective-permute-start | bytes 3538952 | tf_op jit(solution)/shard_map/ppermute | solution.py:59
  53.0 7.3 %copy-start.3 = (bf16[64,1152]{1,0:T(8,128)(2,1)S(1)}, bf16[64,1152]{1,0:T(8,128)(2,1)}, u32[]{:S(2)}) copy-start(bf16[64,1152]{1,0:T(8,128)(2,1)} %param.6) | copy-start | bytes 442372
  53.0 23.7 %all-to-all-start = ((bf16[8,32,2304]{2,1,0:T(8,128)(2,1)}), bf16[8,32,2304]{2,1,0:T(8,128)(2,1)}, u32[]{:S(2)}, u32[]{:S(2)}) async-start(bf16[8,32,2304]{2,1,0:T(8,128)(2,1)} %bitcast.31), calls=%async_computation | async-start | bytes 2359296 | tf_op jit(solution)/shard_map/all_to_all | solution.py:63
  60.3 2.6 %collective-permute-start = (bf16[64,1152]{1,0:T(8,128)(2,1)S(1)}, bf16[64,1152]{1,0:T(8,128)(2,1)S(1)}, u32[]{:S(2)}, u32[]{:S(2)}) collective-permute-start(bf16[64,1152]{1,0:T(8,128)(2,1)S(1)} %copy-done.3), channel_id=1, source_target_pairs={{0,0},{2,34},{4,4},{6,38},{32,32},{34,2},{36,36},{38,6},{1,1},{3,3... | collective-permute-start | bytes 442376 | tf_op jit(solution)/shard_map/ppermute | solution.py:160
  61.0 25.4 %collective-permute-start.4 = (bf16[640,1152]{1,0:T(8,128)(2,1)S(1)}, bf16[640,1152]{1,0:T(8,128)(2,1)}, u32[]{:S(2)}, u32[]{:S(2)}) collective-permute-start(bf16[640,1152]{1,0:T(8,128)(2,1)S(1)} %copy-done), channel_id=1, source_target_pairs={{0,32},{32,0},{1,33},{33,1},{2,34},{34,2},{3,35},{35,3},{4,36},{36... | collective-permute-start | bytes 4423688 | tf_op jit(solution)/shard_map/ppermute | solution.py:59
  62.9 15.3 %collective-permute-start.1 = (bf16[32,1152]{1,0:T(8,128)(2,1)S(1)}, bf16[32,1152]{1,0:T(8,128)(2,1)S(1)}, u32[]{:S(2)}, u32[]{:S(2)}) collective-permute-start(bf16[32,1152]{1,0:T(8,128)(2,1)S(1)} %get-tuple-element.23), channel_id=1, source_target_pairs={{0,1},{1,0},{2,3},{3,2},{4,5},{5,4},{6,7},{7,6},{8,9},{9,8},{10,11... | collective-permute-start | bytes 221192 | tf_op jit(solution)/shard_map/ppermute | solution.py:148
  65.0 21.3 %collective-permute-start.5 = (bf16[640,1152]{1,0:T(8,128)(2,1)S(1)}, bf16[640,1152]{1,0:T(8,128)(2,1)}, u32[]{:S(2)}, u32[]{:S(2)}) collective-permute-start(bf16[640,1152]{1,0:T(8,128)(2,1)S(1)} %collective-permute-done.2.v_ref), channel_id=1, source_target_pairs={{0,32},{32,0},{1,33},{33,1},{2,34},{34,2},{3,35},{35,3},{4,36},{36... | collective-permute-start | bytes 4423688 | tf_op jit(solution)/shard_map/ppermute | solution.py:59
  79.4 22.9 %all-to-all-start.1 = ((bf16[8,32,2304]{2,1,0:T(8,128)(2,1)}), bf16[8,32,2304]{2,1,0:T(8,128)(2,1)}, u32[]{:S(2)}, u32[]{:S(2)}) async-start(bf16[8,32,2304]{2,1,0:T(8,128)(2,1)} %broadcast_in_dim.2), calls=%async_computation.1 | async-start | bytes 2359296 | tf_op jit(solution)/shard_map/all_to_all | solution.py:63
  107.9 14.9 %copy-start.2 = (bf16[512,640]{1,0:T(8,128)(2,1)S(1)}, bf16[512,640]{1,0:T(8,128)(2,1)}, u32[]{:S(2)}) copy-start(bf16[512,640]{1,0:T(8,128)(2,1)} %copy-done.1) | copy-start | bytes 1966084
  107.9 12.2 %collective-permute-start.6 = (bf16[2,4,32,640]{3,2,1,0:T(8,128)(2,1)S(1)}, bf16[2,4,32,640]{3,2,1,0:T(8,128)(2,1)S(1)}, u32[]{:S(2)}, u32[]{:S(2)}) collective-permute-start(bf16[2,4,32,640]{3,2,1,0:T(8,128)(2,1)S(1)} %get-tuple-element.11), channel_id=1, source_target_pairs={{0,4},{2,30},{4,8},{6,2},{8,12},{10,6},{12,16},{14,10},{16,20},{18... | collective-permute-start | bytes 983048 | tf_op jit(solution)/shard_map/ppermute | solution.py:55
  110.2 9.9 %collective-permute-start.7 = (bf16[2,4,32,640]{3,2,1,0:T(8,128)(2,1)S(1)}, bf16[2,4,32,640]{3,2,1,0:T(8,128)(2,1)S(1)}, u32[]{:S(2)}, u32[]{:S(2)}) collective-permute-start(bf16[2,4,32,640]{3,2,1,0:T(8,128)(2,1)S(1)} %get-tuple-element.12), channel_id=1, source_target_pairs={{0,0},{2,2},{4,4},{6,6},{8,8},{10,10},{12,12},{14,14},{16,16},{18,... | collective-permute-start | bytes 983048 | tf_op jit(solution)/shard_map/ppermute | solution.py:55
  110.9 9.3 %collective-permute-start.8 = (bf16[256,1152]{1,0:T(8,128)(2,1)S(1)}, bf16[256,1152]{1,0:T(8,128)(2,1)S(1)}, u32[]{:S(2)}, u32[]{:S(2)}) collective-permute-start(bf16[256,1152]{1,0:T(8,128)(2,1)S(1)} %get-tuple-element.13.mine_ref), channel_id=1, source_target_pairs={{0,32},{32,0},{1,33},{33,1},{2,34},{34,2},{3,35},{35,3},{4,36},{36... | collective-permute-start | bytes 1769480 | tf_op jit(solution)/shard_map/ppermute | solution.py:59
  116.5 18.3 %collective-permute-start.11 = (bf16[256,1152]{1,0:T(8,128)(2,1)}, bf16[256,1152]{1,0:T(8,128)(2,1)S(1)}, u32[]{:S(2)}, u32[]{:S(2)}) collective-permute-start(bf16[256,1152]{1,0:T(8,128)(2,1)} %get-tuple-element.15), channel_id=1, source_target_pairs={{0,1},{1,0},{2,3},{3,2},{4,5},{5,4},{6,7},{7,6},{8,9},{9,8},{10,11... | collective-permute-start | bytes 1769480 | tf_op jit(solution)/shard_map/ppermute | solution.py:148
  120.2 5.2 %collective-permute-start.9 = (bf16[4,32,640]{2,1,0:T(8,128)(2,1)S(1)}, bf16[4,32,640]{2,1,0:T(8,128)(2,1)S(1)}, u32[]{:S(2)}, u32[]{:S(2)}) collective-permute-start(bf16[4,32,640]{2,1,0:T(8,128)(2,1)S(1)} %fusion.9), channel_id=1, source_target_pairs={{0,32},{32,0},{1,33},{33,1},{2,34},{34,2},{3,35},{35,3},{4,36},{36... | collective-permute-start | bytes 491528 | tf_op jit(solution)/shard_map/ppermute | solution.py:59
  122.8 25.0 %collective-permute-start.10 = (bf16[8,2,32,640]{3,2,1,0:T(8,128)(2,1)S(1)}, bf16[8,2,32,640]{3,2,1,0:T(8,128)(2,1)S(1)}, u32[]{:S(2)}, u32[]{:S(2)}) collective-permute-start(bf16[8,2,32,640]{3,2,1,0:T(8,128)(2,1)S(1)} %bitcast.29), channel_id=1, source_target_pairs={{0,1},{1,0},{2,3},{3,2},{4,5},{5,4},{6,7},{7,6},{8,9},{9,8},{10,11... | collective-permute-start | bytes 1966088 | tf_op jit(solution)/shard_map/ppermute | solution.py:148
  126.1 24.4 %all-to-all-start.2 = ((bf16[4,32,640]{2,1,0:T(8,128)(2,1)}), bf16[4,32,640]{2,1,0:T(8,128)(2,1)}, u32[]{:S(2)}, u32[]{:S(2)}) async-start(bf16[4,32,640]{2,1,0:T(8,128)(2,1)} %fusion.2), calls=%async_computation.2 | async-start | bytes 327680 | tf_op jit(solution)/shard_map/all_to_all | solution.py:185
  134.8 13.0 %collective-permute-start.13 = (bf16[128,1152]{1,0:T(8,128)(2,1)S(1)}, bf16[128,1152]{1,0:T(8,128)(2,1)S(1)}, u32[]{:S(2)}, u32[]{:S(2)}) collective-permute-start(bf16[128,1152]{1,0:T(8,128)(2,1)S(1)} %get-tuple-element.20), channel_id=1, source_target_pairs={{0,32},{32,0},{1,33},{33,1},{2,34},{34,2},{3,35},{35,3},{4,36},{36... | collective-permute-start | bytes 884744 | tf_op jit(solution)/shard_map/ppermute | solution.py:59
  136.8 11.1 %collective-permute-start.12 = (bf16[128,1152]{1,0:T(8,128)(2,1)S(1)}, bf16[128,1152]{1,0:T(8,128)(2,1)S(1)}, u32[]{:S(2)}, u32[]{:S(2)}) collective-permute-start(bf16[128,1152]{1,0:T(8,128)(2,1)S(1)} %get-tuple-element.21), channel_id=1, source_target_pairs={{0,32},{32,0},{1,33},{33,1},{2,34},{34,2},{3,35},{35,3},{4,36},{36... | collective-permute-start | bytes 884744 | tf_op jit(solution)/shard_map/ppermute | solution.py:59

commit v6 on v5

--- a/solution.py
+++ b/solution.py
@@ -107,21 +107,39 @@
     return part.astype(jnp.bfloat16).reshape(8, 32, 640)
 
 
-def part_kernel(class_ref, pre_ref, w_ref, v_ref, w2_ref, v2_ref, first_ref, second_ref, kept_ref, lent_ref):
-    for i, weights in enumerate(((w_ref, v_ref), (w2_ref, v2_ref))):
-        part = input_part(pre_ref, *weights).reshape(4, 2, 32, 640)
-        for out_ref, which in ((first_ref, class_ref[0]), (second_ref, class_ref[1])):
-
-            @pl.when(which == 0)
-            def _():
-                out_ref[i] = part[:, 0]
-
-            @pl.when(which == 1)
-            def _():
-                out_ref[i] = part[:, 1]
-
+def part_kernel(class_ref, w_ref, v_ref, pre_hbm, w2_hbm, v2_hbm, first_ref, second_ref, kept_ref, lent_ref, pre_ref, w2_ref, v2_ref, part_ref, sems):
+    fetches = []
+    for i, (far, here) in enumerate(((pre_hbm, pre_ref), (w2_hbm, w2_ref), (v2_hbm, v2_ref))):
+        rows = here.shape[0] // 4
+        for j in range(4):
+            at = pl.ds(rows * j, rows)
+            fetches.append(pltpu.make_async_copy(far.at[at], here.at[at], sems.at[4 * i + j]))
+            fetches[-1].start()
+    for fetch in fetches[:4]:
+        fetch.wait()
     kept_ref[...] = pre_ref[:, :1152]
     lent_ref[...] = pre_ref[:, 1152:]
+    for i in range(2):
+        if i == 1:
+            for fetch in fetches[4:]:
+                fetch.wait()
+        part_ref[...] = input_part(pre_ref, *((w_ref, v_ref), (w2_ref, v2_ref))[i]).reshape(4, 2, 32, 640)
+        first_ref[i] = part_ref[:, class_ref[0]]
+        second_ref[i] = part_ref[:, class_ref[1]]
+
+
+def parts_of(classes, mine, w_in, w_pair, w_core, w_pair_core):
+    return pl.pallas_call(
+        part_kernel,
+        out_shape=[shape(2, 4, 32, 640), shape(2, 4, 32, 640), shape(256, 1152), shape(256, 1152)],
+        in_specs=[SMEM] + [VMEM] * 2 + [ANY] * 3,
+        out_specs=[VMEM] * 4,
+        scratch_shapes=[pltpu.VMEM((256, 2304), jnp.bfloat16)]
+        + [pltpu.VMEM((640, 1152), jnp.bfloat16)] * 2
+        + [pltpu.VMEM((4, 2, 32, 640), jnp.bfloat16), pltpu.SemaphoreType.DMA((12,))],
+        compiler_params=PARAMS,
+        cost_estimate=pl.CostEstimate(flops=4 * 256 * 640 * 2304, bytes_accessed=9000000, transcendentals=0),
+    )(classes, w_in, w_pair, mine, w_core, w_pair_core)
 
 
 def weight_terms(terms):
@@ -170,10 +188,7 @@
 
     classes = jnp.stack([jnp.bitwise_and(zl + 2 - core, 3), jnp.bitwise_and(zl + 3 * core, 3)])
     classes = jnp.right_shift(classes, 1).astype(jnp.int32)
-    shapes = [shape(2, 4, 32, 640), shape(2, 4, 32, 640), shape(256, 1152), shape(256, 1152)]
-    first, second, mine, lent = call(part_kernel, shapes, 5, 2 * flops, 9000000)(
-        classes, mine, w_in, w_pair, w_core, w_pair_core
-    )
+    first, second, mine, lent = parts_of(classes, mine, w_in, w_pair, w_core, w_pair_core)
     first = z_and_core(first, lambda z, c: z + 1 if c else z + (2 if z % 2 == 0 else -2))
     second = z_and_core(second, lambda z, c: z - c)
     mine_pair = swap_pair(lent)

time: 155 us -> 154 us (level)
  no operation moved by 1% of the time
where the time goes in v6:
time: 154 us; the launch traced here: 151 us
  starting transfers between devices  53 us (34%)
  blocking collectives  39.4 us (26%)
  waiting for transfers between devices  38.3 us (25%)
  Pallas kernels  10.9 us (7%)
  other arithmetic  5.41 us (4%)
  local copies, waits for them, and re-layouts  2.81 us (2%)
    all_gather x1, blocking collectives, shards(): lax.all_gather(own, ('za', 'zl'), axis=0, tiled=True).reshape(8, 2, 32, 640)  39.4 us
    all_to_all x2, waiting for transfers between devices, exchange(): return lax.all_to_all(blocks, ('yh', 'x'), 0, 0, tiled=True)  25.5 us
    ppermute x7, starting transfers between devices, swap_cores(): return lax.ppermute(array, 'c', SWAP)  18.6 us
    all_to_all x2, starting transfers between devices, exchange(): return lax.all_to_all(blocks, ('yh', 'x'), 0, 0, tiled=True)  14 us
    ppermute x4, starting transfers between devices, swap_pair(): return lax.ppermute(array, 'yl', SWAP)  10.3 us
    ppermute x4, waiting for transfers between devices, swap_pair(): return lax.ppermute(array, 'yl', SWAP)  9.71 us
    all_to_all x1, starting transfers between devices, shards(): blocks = lax.all_to_all(near, 'za', 0, 0, tiled=True)  6.42 us
    pallas_call x1, Pallas kernels, parts_of(): pl.pallas_call(part_kernel, out_shape=[shape(2, 4, 32, 640), shape(2, 4,...  4.47 us
  transfers between devices with their start and end apart: 17, of which 6 were waited for; matrix products, arithmetic and copies ran while one was open for 4% of the time, Pallas kernels for 3%

profile of v6, /device:TPU:6, one launch (start us, length us, event | category | flops | bytes accessed | tf_op | source)
XLA Modules:
  0.0 151.0 jit_solution(376763186250343763)
XLA Ops:
  0.6 3.6 %collective-permute-start = (bf16[640,1152]{1,0:T(8,128)(2,1)}, bf16[640,1152]{1,0:T(8,128)(2,1)S(1)}, u32[]{:S(2)}, u32[]{:S(2)}) collective-permute-start(bf16[640,1152]{1,0:T(8,128)(2,1)} %w_ref.5), channel_id=1, source_target_pairs={{0,1},{1,0},{2,3},{3,2},{4,5},{5,4},{6,7},{7,6},{8,9},{9,8},{10,11... | collective-permute-start | bytes 4423688 | tf_op jit(solution)/shard_map/ppermute | solution.py:166
  6.3 39.4 %all_gather.3 = bf16[512,640]{1,0:T(8,128)(2,1)S(1)} all-gather(bf16[32,640]{1,0:T(8,128)(2,1)S(1)} %bitcast.32), channel_id=1, replica_groups=mesh['yh'=2,'x'=4,'c'=2,'za'=4,'zl'=4,'yl'=2] {'za','zl'}, dimensions={0}, use_global_device_ids=true | all-gather | bytes 696320 | tf_op jit(solution)/shard_map/all_gather | solution.py:174
  47.0 1.9 %collective-permute-start.3 = (bf16[256,2304]{1,0:T(8,128)(2,1)S(1)}, bf16[256,2304]{1,0:T(8,128)(2,1)S(1)}, u32[]{:S(2)}, u32[]{:S(2)}) collective-permute-start(bf16[256,2304]{1,0:T(8,128)(2,1)S(1)} %shard_map.60), channel_id=1, source_target_pairs={{0,32},{32,0},{1,33},{33,1},{2,34},{34,2},{3,35},{35,3},{4,36},{36... | collective-permute-start | bytes 3538952 | tf_op jit(solution)/shard_map/ppermute | solution.py:59
  53.0 7.2 %all-to-all-start = ((bf16[8,32,2304]{2,1,0:T(8,128)(2,1)}), bf16[8,32,2304]{2,1,0:T(8,128)(2,1)}, u32[]{:S(2)}, u32[]{:S(2)}) async-start(bf16[8,32,2304]{2,1,0:T(8,128)(2,1)} %bitcast.31), calls=%async_computation | async-start | bytes 2359296 | tf_op jit(solution)/shard_map/all_to_all | solution.py:63
  61.0 1.9 %collective-permute-start.4 = (bf16[640,1152]{1,0:T(8,128)(2,1)S(1)}, bf16[640,1152]{1,0:T(8,128)(2,1)}, u32[]{:S(2)}, u32[]{:S(2)}) collective-permute-start(bf16[640,1152]{1,0:T(8,128)(2,1)S(1)} %copy-done), channel_id=1, source_target_pairs={{0,32},{32,0},{1,33},{33,1},{2,34},{34,2},{3,35},{35,3},{4,36},{36... | collective-permute-start | bytes 4423688 | tf_op jit(solution)/shard_map/ppermute | solution.py:59
  62.9 2.1 %collective-permute-start.2 = (bf16[32,1152]{1,0:T(8,128)(2,1)S(1)}, bf16[32,1152]{1,0:T(8,128)(2,1)S(1)}, u32[]{:S(2)}, u32[]{:S(2)}) collective-permute-start(bf16[32,1152]{1,0:T(8,128)(2,1)S(1)} %get-tuple-element.23), channel_id=1, source_target_pairs={{0,1},{1,0},{2,3},{3,2},{4,5},{5,4},{6,7},{7,6},{8,9},{9,8},{10,11... | collective-permute-start | bytes 221192 | tf_op jit(solution)/shard_map/ppermute | solution.py:166
  65.0 2.3 %collective-permute-start.5 = (bf16[640,1152]{1,0:T(8,128)(2,1)S(1)}, bf16[640,1152]{1,0:T(8,128)(2,1)}, u32[]{:S(2)}, u32[]{:S(2)}) collective-permute-start(bf16[640,1152]{1,0:T(8,128)(2,1)S(1)} %collective-permute-done.v_ref), channel_id=1, source_target_pairs={{0,32},{32,0},{1,33},{33,1},{2,34},{34,2},{3,35},{35,3},{4,36},{36... | collective-permute-start | bytes 4423688 | tf_op jit(solution)/shard_map/ppermute | solution.py:59
  67.3 9.5 %all-to-all-done = bf16[8,32,2304]{2,1,0:T(8,128)(2,1)} async-done(((bf16[8,32,2304]{2,1,0:T(8,128)(2,1)}), bf16[8,32,2304]{2,1,0:T(8,128)(2,1)}, u32[]{:S(2)}, u32[]{:S(2)}) %all-to-all-start) | async-done | bytes 1179680 | tf_op jit(solution)/shard_map/all_to_all | solution.py:63
  79.4 6.8 %all-to-all-start.1 = ((bf16[8,32,2304]{2,1,0:T(8,128)(2,1)}), bf16[8,32,2304]{2,1,0:T(8,128)(2,1)}, u32[]{:S(2)}, u32[]{:S(2)}) async-start(bf16[8,32,2304]{2,1,0:T(8,128)(2,1)} %broadcast_in_dim.2), calls=%async_computation.1 | async-start | bytes 2359296 | tf_op jit(solution)/shard_map/all_to_all | solution.py:63
  86.3 16.1 %all-to-all-done.1 = bf16[8,32,2304]{2,1,0:T(8,128)(2,1)} async-done(((bf16[8,32,2304]{2,1,0:T(8,128)(2,1)}), bf16[8,32,2304]{2,1,0:T(8,128)(2,1)}, u32[]{:S(2)}, u32[]{:S(2)}) %all-to-all-start.1) | async-done | bytes 1179680 | tf_op jit(solution)/shard_map/all_to_all | solution.py:63
  102.4 4.5 %shard_map.61 = (bf16[2,4,32,640]{3,2,1,0:T(8,128)(2,1)S(1)}, bf16[2,4,32,640]{3,2,1,0:T(8,128)(2,1)S(1)}, bf16[256,1152]{1,0:T(8,128)(2,1)S(1)}, bf16[256,1152]{1,0:T(8,128)(2,1)}) custom-call(s32[2]{0:T(128)S(1)} %add_shift-right-arithmetic_fusion.class_ref, bf16[640,1152]{1,0:T(8,128)(2,1)S(1)} %copy-done, ...), custom_call_target="tpu_custom_call" | custom-call | flops 1509949440 | bytes 9000000 | tf_op jit(solution)/shard_map/pallas_call | solution.py:132
  106.9 2.3 %collective-permute-start.6 = (bf16[2,4,32,640]{3,2,1,0:T(8,128)(2,1)S(1)}, bf16[2,4,32,640]{3,2,1,0:T(8,128)(2,1)S(1)}, u32[]{:S(2)}, u32[]{:S(2)}) collective-permute-start(bf16[2,4,32,640]{3,2,1,0:T(8,128)(2,1)S(1)} %get-tuple-element.11), channel_id=1, source_target_pairs={{0,4},{2,30},{4,8},{6,2},{8,12},{10,6},{12,16},{14,10},{16,20},{18... | collective-permute-start | bytes 983048 | tf_op jit(solution)/shard_map/ppermute | solution.py:55
  109.9 5.6 %collective-permute-start.8 = (bf16[256,1152]{1,0:T(8,128)(2,1)S(1)}, bf16[256,1152]{1,0:T(8,128)(2,1)S(1)}, u32[]{:S(2)}, u32[]{:S(2)}) collective-permute-start(bf16[256,1152]{1,0:T(8,128)(2,1)S(1)} %get-tuple-element.13.mine_ref), channel_id=1, source_target_pairs={{0,32},{32,0},{1,33},{33,1},{2,34},{34,2},{3,35},{35,3},{4,36},{36... | collective-permute-start | bytes 1769480 | tf_op jit(solution)/shard_map/ppermute | solution.py:59
  115.4 2.1 %collective-permute-start.11 = (bf16[256,1152]{1,0:T(8,128)(2,1)}, bf16[256,1152]{1,0:T(8,128)(2,1)S(1)}, u32[]{:S(2)}, u32[]{:S(2)}) collective-permute-start(bf16[256,1152]{1,0:T(8,128)(2,1)} %get-tuple-element.15), channel_id=1, source_target_pairs={{0,1},{1,0},{2,3},{3,2},{4,5},{5,4},{6,7},{7,6},{8,9},{9,8},{10,11... | collective-permute-start | bytes 1769480 | tf_op jit(solution)/shard_map/ppermute | solution.py:166
  117.5 1.5 %collective-permute-done.6 = bf16[2,4,32,640]{3,2,1,0:T(8,128)(2,1)S(1)} collective-permute-done((bf16[2,4,32,640]{3,2,1,0:T(8,128)(2,1)S(1)}, bf16[2,4,32,640]{3,2,1,0:T(8,128)(2,1)S(1)}, u32[]{:S(2)}, u32[]{:S(2)}) %collective-permute-start.6) | collective-permute-done | bytes 327712 | tf_op jit(solution)/shard_map/ppermute | solution.py:55
  119.2 2.6 %collective-permute-start.9 = (bf16[4,32,640]{2,1,0:T(8,128)(2,1)S(1)}, bf16[4,32,640]{2,1,0:T(8,128)(2,1)S(1)}, u32[]{:S(2)}, u32[]{:S(2)}) collective-permute-start(bf16[4,32,640]{2,1,0:T(8,128)(2,1)S(1)} %fusion.9), channel_id=1, source_target_pairs={{0,32},{32,0},{1,33},{33,1},{2,34},{34,2},{3,35},{35,3},{4,36},{36... | collective-permute-start | bytes 491528 | tf_op jit(solution)/shard_map/ppermute | solution.py:59
  121.8 2.5 %collective-permute-start.10 = (bf16[8,2,32,640]{3,2,1,0:T(8,128)(2,1)S(1)}, bf16[8,2,32,640]{3,2,1,0:T(8,128)(2,1)S(1)}, u32[]{:S(2)}, u32[]{:S(2)}) collective-permute-start(bf16[8,2,32,640]{3,2,1,0:T(8,128)(2,1)S(1)} %bitcast.29), channel_id=1, source_target_pairs={{0,1},{1,0},{2,3},{3,2},{4,5},{5,4},{6,7},{7,6},{8,9},{9,8},{10,11... | collective-permute-start | bytes 1966088 | tf_op jit(solution)/shard_map/ppermute | solution.py:166
  125.1 6.4 %all-to-all-start.2 = ((bf16[4,32,640]{2,1,0:T(8,128)(2,1)}), bf16[4,32,640]{2,1,0:T(8,128)(2,1)}, u32[]{:S(2)}, u32[]{:S(2)}) async-start(bf16[4,32,640]{2,1,0:T(8,128)(2,1)} %fusion.2), calls=%async_computation.2 | async-start | bytes 327680 | tf_op jit(solution)/shard_map/all_to_all | solution.py:200
  131.5 2.2 %collective-permute-done.11.mine_ref = bf16[256,1152]{1,0:T(8,128)(2,1)S(1)} collective-permute-done((bf16[256,1152]{1,0:T(8,128)(2,1)}, bf16[256,1152]{1,0:T(8,128)(2,1)S(1)}, u32[]{:S(2)}, u32[]{:S(2)}) %collective-permute-start.11) | collective-permute-done | bytes 589856 | tf_op jit(solution)/shard_map/ppermute | solution.py:166
  133.8 1.9 %collective-permute-start.13 = (bf16[128,1152]{1,0:T(8,128)(2,1)S(1)}, bf16[128,1152]{1,0:T(8,128)(2,1)S(1)}, u32[]{:S(2)}, u32[]{:S(2)}) collective-permute-start(bf16[128,1152]{1,0:T(8,128)(2,1)S(1)} %get-tuple-element.20), channel_id=1, source_target_pairs={{0,32},{32,0},{1,33},{33,1},{2,34},{34,2},{3,35},{35,3},{4,36},{36... | collective-permute-start | bytes 884744 | tf_op jit(solution)/shard_map/ppermute | solution.py:59
  135.7 2.4 %collective-permute-start.12 = (bf16[128,1152]{1,0:T(8,128)(2,1)S(1)}, bf16[128,1152]{1,0:T(8,128)(2,1)S(1)}, u32[]{:S(2)}, u32[]{:S(2)}) collective-permute-start(bf16[128,1152]{1,0:T(8,128)(2,1)S(1)} %get-tuple-element.21), channel_id=1, source_target_pairs={{0,32},{32,0},{1,33},{33,1},{2,34},{34,2},{3,35},{35,3},{4,36},{36... | collective-permute-start | bytes 884744 | tf_op jit(solution)/shard_map/ppermute | solution.py:59
  139.4 7.5 %collective-permute-done.10.rows_ref = bf16[8,2,32,640]{3,2,1,0:T(8,128)(2,1)S(1)} collective-permute-done((bf16[8,2,32,640]{3,2,1,0:T(8,128)(2,1)S(1)}, bf16[8,2,32,640]{3,2,1,0:T(8,128)(2,1)S(1)}, u32[]{:S(2)}, u32[]{:S(2)}) %collective-permute-start.10) | collective-permute-done | bytes 655392 | tf_op jit(solution)/shard_map/ppermute | solution.py:166
  146.8 2.6 %shard_map.63 = bf16[640,1152]{1,0:T(8,128)(2,1)} custom-call(s32[1]{0:T(128)} %bitcast.5.core_ref.at_ref, bf16[8,2,32,640]{3,2,1,0:T(8,128)(2,1)S(1)} %collective-permute-done.10.rows_ref, bf16[256,1152]{1,0:T(8,128)(2,1)S(1)} %collective-permute-done.11.mine_ref, bf16[128,1152]{1,0:T(8,128)(2,1)S(1)} %collective-permute-done.12.other_ref, ...), custom_call_target="tpu_custom_call" | custom-call | flops 754974720 | bytes 5000000 | tf_op jit(solution)/shard_map/pallas_call | solution.py:203
  149.4 1.6 %reduce_sum.22 = bf16[32,640]{1,0:T(8,128)(2,1)} reduce(bf16[4,32,640]{2,1,0:T(8,128)(2,1)} %all-to-all-done.2, bf16[]{:T(256)} %constant.69.clone.1), dimensions={0}, to_apply=%region_1.2 | reduce | flops 61440 | bytes 204802 | tf_op jit(solution)/shard_map/reduce_sum | solution.py:205
  (40 shorter events, 13.6 us)
Async XLA Ops:
  0.6 45.1 %copy-start = (bf16[640,1152]{1,0:T(8,128)(2,1)S(1)}, bf16[640,1152]{1,0:T(8,128)(2,1)}, u32[]{:S(2)}) copy-start(bf16[640,1152]{1,0:T(8,128)(2,1)} %w_ref.5) | copy-start | bytes 4423684
  0.6 45.1 %collective-permute-start = (bf16[640,1152]{1,0:T(8,128)(2,1)}, bf16[640,1152]{1,0:T(8,128)(2,1)S(1)}, u32[]{:S(2)}, u32[]{:S(2)}) collective-permute-start(bf16[640,1152]{1,0:T(8,128)(2,1)} %w_ref.5), channel_id=1, source_target_pairs={{0,1},{1,0},{2,3},{3,2},{4,5},{5,4},{6,7},{7,6},{8,9},{9,8},{10,11... | collective-permute-start | bytes 4423688 | tf_op jit(solution)/shard_map/ppermute | solution.py:166
  45.7 3.2 %copy-start.1 = (bf16[512,640]{1,0:T(8,128)(2,1)}, bf16[512,640]{1,0:T(8,128)(2,1)S(1)}, u32[]{:S(2)}) copy-start(bf16[512,640]{1,0:T(8,128)(2,1)S(1)} %all_gather.3) | copy-start | bytes 1966084
  47.0 4.7 %collective-permute-start.3 = (bf16[256,2304]{1,0:T(8,128)(2,1)S(1)}, bf16[256,2304]{1,0:T(8,128)(2,1)S(1)}, u32[]{:S(2)}, u32[]{:S(2)}) collective-permute-start(bf16[256,2304]{1,0:T(8,128)(2,1)S(1)} %shard_map.60), channel_id=1, source_target_pairs={{0,32},{32,0},{1,33},{33,1},{2,34},{34,2},{3,35},{35,3},{4,36},{36... | collective-permute-start | bytes 3538952 | tf_op jit(solution)/shard_map/ppermute | solution.py:59
  53.0 7.3 %copy-start.3 = (bf16[64,1152]{1,0:T(8,128)(2,1)S(1)}, bf16[64,1152]{1,0:T(8,128)(2,1)}, u32[]{:S(2)}) copy-start(bf16[64,1152]{1,0:T(8,128)(2,1)} %param.6) | copy-start | bytes 442372
  53.0 23.7 %all-to-all-start = ((bf16[8,32,2304]{2,1,0:T(8,128)(2,1)}), bf16[8,32,2304]{2,1,0:T(8,128)(2,1)}, u32[]{:S(2)}, u32[]{:S(2)}) async-start(bf16[8,32,2304]{2,1,0:T(8,128)(2,1)} %bitcast.31), calls=%async_computation | async-start | bytes 2359296 | tf_op jit(solution)/shard_map/all_to_all | solution.py:63
  60.3 2.6 %collective-permute-start.1 = (bf16[64,1152]{1,0:T(8,128)(2,1)S(1)}, bf16[64,1152]{1,0:T(8,128)(2,1)S(1)}, u32[]{:S(2)}, u32[]{:S(2)}) collective-permute-start(bf16[64,1152]{1,0:T(8,128)(2,1)S(1)} %copy-done.3), channel_id=1, source_target_pairs={{0,0},{2,34},{4,4},{6,38},{32,32},{34,2},{36,36},{38,6},{1,1},{3,3... | collective-permute-start | bytes 442376 | tf_op jit(solution)/shard_map/ppermute | solution.py:178
  61.0 25.4 %collective-permute-start.4 = (bf16[640,1152]{1,0:T(8,128)(2,1)S(1)}, bf16[640,1152]{1,0:T(8,128)(2,1)}, u32[]{:S(2)}, u32[]{:S(2)}) collective-permute-start(bf16[640,1152]{1,0:T(8,128)(2,1)S(1)} %copy-done), channel_id=1, source_target_pairs={{0,32},{32,0},{1,33},{33,1},{2,34},{34,2},{3,35},{35,3},{4,36},{36... | collective-permute-start | bytes 4423688 | tf_op jit(solution)/shard_map/ppermute | solution.py:59
  62.9 15.3 %collective-permute-start.2 = (bf16[32,1152]{1,0:T(8,128)(2,1)S(1)}, bf16[32,1152]{1,0:T(8,128)(2,1)S(1)}, u32[]{:S(2)}, u32[]{:S(2)}) collective-permute-start(bf16[32,1152]{1,0:T(8,128)(2,1)S(1)} %get-tuple-element.23), channel_id=1, source_target_pairs={{0,1},{1,0},{2,3},{3,2},{4,5},{5,4},{6,7},{7,6},{8,9},{9,8},{10,11... | collective-permute-start | bytes 221192 | tf_op jit(solution)/shard_map/ppermute | solution.py:166
  65.0 21.3 %collective-permute-start.5 = (bf16[640,1152]{1,0:T(8,128)(2,1)S(1)}, bf16[640,1152]{1,0:T(8,128)(2,1)}, u32[]{:S(2)}, u32[]{:S(2)}) collective-permute-start(bf16[640,1152]{1,0:T(8,128)(2,1)S(1)} %collective-permute-done.v_ref), channel_id=1, source_target_pairs={{0,32},{32,0},{1,33},{33,1},{2,34},{34,2},{3,35},{35,3},{4,36},{36... | collective-permute-start | bytes 4423688 | tf_op jit(solution)/shard_map/ppermute | solution.py:59
  79.4 22.9 %all-to-all-start.1 = ((bf16[8,32,2304]{2,1,0:T(8,128)(2,1)}), bf16[8,32,2304]{2,1,0:T(8,128)(2,1)}, u32[]{:S(2)}, u32[]{:S(2)}) async-start(bf16[8,32,2304]{2,1,0:T(8,128)(2,1)} %broadcast_in_dim.2), calls=%async_computation.1 | async-start | bytes 2359296 | tf_op jit(solution)/shard_map/all_to_all | solution.py:63
  106.9 14.9 %copy-start.2 = (bf16[512,640]{1,0:T(8,128)(2,1)S(1)}, bf16[512,640]{1,0:T(8,128)(2,1)}, u32[]{:S(2)}) copy-start(bf16[512,640]{1,0:T(8,128)(2,1)} %copy-done.1) | copy-start | bytes 1966084
  106.9 12.2 %collective-permute-start.6 = (bf16[2,4,32,640]{3,2,1,0:T(8,128)(2,1)S(1)}, bf16[2,4,32,640]{3,2,1,0:T(8,128)(2,1)S(1)}, u32[]{:S(2)}, u32[]{:S(2)}) collective-permute-start(bf16[2,4,32,640]{3,2,1,0:T(8,128)(2,1)S(1)} %get-tuple-element.11), channel_id=1, source_target_pairs={{0,4},{2,30},{4,8},{6,2},{8,12},{10,6},{12,16},{14,10},{16,20},{18... | collective-permute-start | bytes 983048 | tf_op jit(solution)/shard_map/ppermute | solution.py:55
  109.2 9.9 %collective-permute-start.7 = (bf16[2,4,32,640]{3,2,1,0:T(8,128)(2,1)S(1)}, bf16[2,4,32,640]{3,2,1,0:T(8,128)(2,1)S(1)}, u32[]{:S(2)}, u32[]{:S(2)}) collective-permute-start(bf16[2,4,32,640]{3,2,1,0:T(8,128)(2,1)S(1)} %get-tuple-element.12), channel_id=1, source_target_pairs={{0,0},{2,2},{4,4},{6,6},{8,8},{10,10},{12,12},{14,14},{16,16},{18,... | collective-permute-start | bytes 983048 | tf_op jit(solution)/shard_map/ppermute | solution.py:55
  109.9 9.3 %collective-permute-start.8 = (bf16[256,1152]{1,0:T(8,128)(2,1)S(1)}, bf16[256,1152]{1,0:T(8,128)(2,1)S(1)}, u32[]{:S(2)}, u32[]{:S(2)}) collective-permute-start(bf16[256,1152]{1,0:T(8,128)(2,1)S(1)} %get-tuple-element.13.mine_ref), channel_id=1, source_target_pairs={{0,32},{32,0},{1,33},{33,1},{2,34},{34,2},{3,35},{35,3},{4,36},{36... | collective-permute-start | bytes 1769480 | tf_op jit(solution)/shard_map/ppermute | solution.py:59
  115.4 18.3 %collective-permute-start.11 = (bf16[256,1152]{1,0:T(8,128)(2,1)}, bf16[256,1152]{1,0:T(8,128)(2,1)S(1)}, u32[]{:S(2)}, u32[]{:S(2)}) collective-permute-start(bf16[256,1152]{1,0:T(8,128)(2,1)} %get-tuple-element.15), channel_id=1, source_target_pairs={{0,1},{1,0},{2,3},{3,2},{4,5},{5,4},{6,7},{7,6},{8,9},{9,8},{10,11... | collective-permute-start | bytes 1769480 | tf_op jit(solution)/shard_map/ppermute | solution.py:166
  119.2 5.2 %collective-permute-start.9 = (bf16[4,32,640]{2,1,0:T(8,128)(2,1)S(1)}, bf16[4,32,640]{2,1,0:T(8,128)(2,1)S(1)}, u32[]{:S(2)}, u32[]{:S(2)}) collective-permute-start(bf16[4,32,640]{2,1,0:T(8,128)(2,1)S(1)} %fusion.9), channel_id=1, source_target_pairs={{0,32},{32,0},{1,33},{33,1},{2,34},{34,2},{3,35},{35,3},{4,36},{36... | collective-permute-start | bytes 491528 | tf_op jit(solution)/shard_map/ppermute | solution.py:59
  121.8 25.0 %collective-permute-start.10 = (bf16[8,2,32,640]{3,2,1,0:T(8,128)(2,1)S(1)}, bf16[8,2,32,640]{3,2,1,0:T(8,128)(2,1)S(1)}, u32[]{:S(2)}, u32[]{:S(2)}) collective-permute-start(bf16[8,2,32,640]{3,2,1,0:T(8,128)(2,1)S(1)} %bitcast.29), channel_id=1, source_target_pairs={{0,1},{1,0},{2,3},{3,2},{4,5},{5,4},{6,7},{7,6},{8,9},{9,8},{10,11... | collective-permute-start | bytes 1966088 | tf_op jit(solution)/shard_map/ppermute | solution.py:166
  125.1 24.4 %all-to-all-start.2 = ((bf16[4,32,640]{2,1,0:T(8,128)(2,1)}), bf16[4,32,640]{2,1,0:T(8,128)(2,1)}, u32[]{:S(2)}, u32[]{:S(2)}) async-start(bf16[4,32,640]{2,1,0:T(8,128)(2,1)} %fusion.2), calls=%async_computation.2 | async-start | bytes 327680 | tf_op jit(solution)/shard_map/all_to_all | solution.py:200
  133.8 13.0 %collective-permute-start.13 = (bf16[128,1152]{1,0:T(8,128)(2,1)S(1)}, bf16[128,1152]{1,0:T(8,128)(2,1)S(1)}, u32[]{:S(2)}, u32[]{:S(2)}) collective-permute-start(bf16[128,1152]{1,0:T(8,128)(2,1)S(1)} %get-tuple-element.20), channel_id=1, source_target_pairs={{0,32},{32,0},{1,33},{33,1},{2,34},{34,2},{3,35},{35,3},{4,36},{36... | collective-permute-start | bytes 884744 | tf_op jit(solution)/shard_map/ppermute | solution.py:59
  135.7 11.1 %collective-permute-start.12 = (bf16[128,1152]{1,0:T(8,128)(2,1)S(1)}, bf16[128,1152]{1,0:T(8,128)(2,1)S(1)}, u32[]{:S(2)}, u32[]{:S(2)}) collective-permute-start(bf16[128,1152]{1,0:T(8,128)(2,1)S(1)} %get-tuple-element.21), channel_id=1, source_target_pairs={{0,32},{32,0},{1,33},{33,1},{2,34},{34,2},{3,35},{35,3},{4,36},{36... | collective-permute-start | bytes 884744 | tf_op jit(solution)/shard_map/ppermute | solution.py:59
